TPU v7x, 128 devices: a whole 4x4x4 slice. The times are simulated.
128 devices in a mesh: dp: 32 (over x, y, core), mp: 4 (over z).
Axes of the slice: x: 4, y: 4, z: 4, core: 2. Of those that a mesh axis runs over, the one named last changes fastest.
Arguments:
- attention_output: bfloat16 [16384, 4096], P('dp', 'mp'), may hold values from -6 to 6
- residual: bfloat16 [16384, 4096], P('dp', 'mp')
- output_projection_weight: bfloat16 [4096, 4096], P(None, 'mp'), may hold values from -0.09375 to 0.09375
- adapter_down_matrix: bfloat16 [4096, 16], replicated, may hold values from -0.09375 to 0.09375
- adapter_up_matrix: bfloat16 [16, 4096], P(None, 'mp'), may hold values from -1.5 to 1.5
- final_norm_gain: bfloat16 [4096], P('mp'), may hold values from 0.5 to 1.5
- query_hidden_states: bfloat16 [1024, 4096], P('dp', 'mp')
- pair_passage_index: int32 [1024, 17], P('dp'), may hold values from 0 to 4095, as said below
- lengths: int32 [4096], P('dp'), may hold values from 1 to 4
Outputs:
- per_query_loss: float32 [1024], P('dp')
- query_gradient: bfloat16 [1024, 4096], P('dp', 'mp')
- residual_gradient: bfloat16 [16384, 4096], P('dp', 'mp')
- attention_gradient: bfloat16 [16384, 4096], P('dp', 'mp')
- down_matrix_gradient: float32 [4096, 16], P('mp')
- up_matrix_gradient: float32 [16, 4096], P(None, 'mp')
Inputs may be any that keep to these rules, and one draw needn't show every extreme that they name: `pair_passage_index`: passage p is held at dp index p // 128. Among the 544 entries of one device's rows (aligned blocks of 32 rows), at most 25 name passages of any one owner; in every block exactly 25 name passages of one owner, the same owner for all blocks.
All inputs are finite; a program needn't handle non-finite values.
Results may differ from a plain program's by a relative error of at most 0.03.
Values may be sent and summed in bfloat16 or wider, within the bound.
No kernel may reach another device: no remote copies, remote signals or barrier semaphores. Data moves between devices by JAX's collectives and lax.ppermute only.
A program may use at most 128 MiB of HBM per device.

v0:
```python
import jax
import jax.numpy as jnp
from jax import lax
from jax.sharding import PartitionSpec as P

SOFTMAX_TEMPER = 0.02
LOSS_SCALE = 1024.0


def token_totals(values):
    return lax.psum(values.astype(jnp.bfloat16), "mp").astype(jnp.float32)


def body(
    attention_output,
    residual,
    output_projection_weight,
    adapter_down_matrix,
    adapter_up_matrix,
    final_norm_gain,
    query_hidden_states,
    pair_passage_index,
    lengths,
):
    single_float = jnp.float32
    tokens, width_portion = attention_output.shape
    passages = lengths.shape[0]
    seq_len = tokens // passages
    queries, hard_count = pair_passage_index.shape
    full_width = width_portion * lax.axis_size("mp")
    n_owners = lax.axis_size("dp")
    fragment = lax.all_gather(attention_output, "mp", axis=1, tiled=True)
    projected = jnp.dot(fragment, output_projection_weight, preferred_element_type=single_float)
    adapter_total_sum = jnp.dot(fragment, adapter_down_matrix, preferred_element_type=single_float)
    adapter_middle = adapter_total_sum.astype(jnp.bfloat16)
    residual_stream = (
        residual.astype(single_float)
        + projected
        + 2.0 * jnp.dot(adapter_middle, adapter_up_matrix, preferred_element_type=single_float)
    )
    square_sum = token_totals(jnp.sum(residual_stream * residual_stream, axis=1))
    inverse_rms = lax.rsqrt(square_sum / full_width + 1e-05)[:, None]
    gain_f32 = final_norm_gain.astype(single_float)
    normed = residual_stream * inverse_rms * gain_f32
    valid = (jnp.arange(seq_len)[None, :] < lengths[:, None]).astype(single_float)
    length_f32 = lengths.astype(single_float)[:, None]
    pooled = (
        jnp.sum(normed.reshape(passages, seq_len, width_portion) * valid[:, :, None], axis=1)
        / length_f32
    )
    pooled_b = pooled.astype(jnp.bfloat16)
    pooled_f32 = pooled_b.astype(single_float)
    query_f32 = query_hidden_states.astype(single_float)
    flat_ids = pair_passage_index.reshape(-1)
    every_row = lax.all_gather(pooled_b, "dp", axis=0, tiled=True)
    fetched = every_row[flat_ids]
    hard_rows = fetched.reshape(queries, hard_count, width_portion)
    negative_product = jnp.einsum(
        "qkd,qd->qk", hard_rows, query_hidden_states, preferred_element_type=single_float
    )
    hard_square = jnp.einsum(
        "qkd,qkd->qk", hard_rows, hard_rows, preferred_element_type=single_float
    )
    batch_product = lax.dot_general(
        query_hidden_states, pooled_b, (((1,), (1,)), ((), ())), preferred_element_type=single_float
    )
    pass_square = jnp.sum(pooled_f32 * pooled_f32, axis=1)
    query_square = jnp.sum(query_f32 * query_f32, axis=1)
    negative_product, batch_product, hard_square, pass_square, query_square = lax.psum(
        (negative_product, batch_product, hard_square, pass_square, query_square), "mp"
    )
    query_inverse = lax.rsqrt(query_square + 1e-06)
    negative_inverse = lax.rsqrt(hard_square + 1e-06)
    passage_inverse = lax.rsqrt(pass_square + 1e-06)
    negative_logits = negative_product * query_inverse[:, None] * negative_inverse / SOFTMAX_TEMPER
    batch_logits = (
        batch_product * query_inverse[:, None] * passage_inverse[None, :] / SOFTMAX_TEMPER
    )
    log_total = jnp.log(
        jnp.sum(jnp.exp(negative_logits), axis=1) + jnp.sum(jnp.exp(batch_logits), axis=1)
    )
    per_query_loss = log_total - negative_logits[:, 0]
    positive = (jnp.arange(hard_count) == 0).astype(single_float)
    negative_coefficient = LOSS_SCALE * (
        jnp.exp(negative_logits - log_total[:, None]) - positive[None, :]
    )
    batch_coefficient = LOSS_SCALE * jnp.exp(batch_logits - log_total[:, None])
    negative_softmax_weight = (
        negative_coefficient * query_inverse[:, None] * negative_inverse / SOFTMAX_TEMPER
    ).astype(jnp.bfloat16)
    batch_softmax_weight = (
        batch_coefficient * query_inverse[:, None] * passage_inverse[None, :] / SOFTMAX_TEMPER
    ).astype(jnp.bfloat16)
    query_scalar = jnp.sum(negative_coefficient * negative_logits, axis=1) + jnp.sum(
        batch_coefficient * batch_logits, axis=1
    )
    toward_query = jnp.einsum(
        "qk,qkd->qd", negative_softmax_weight, hard_rows, preferred_element_type=single_float
    )
    toward_query = toward_query + jnp.dot(
        batch_softmax_weight, pooled_b, preferred_element_type=single_float
    )
    query_gradient = (
        toward_query - (query_scalar * query_inverse * query_inverse)[:, None] * query_f32
    ).astype(jnp.bfloat16)
    hard_terms = (
        negative_softmax_weight.astype(single_float)[:, :, None] * query_f32[:, None, :]
    ).reshape(queries * hard_count, width_portion)
    hard_scalars = (negative_coefficient * negative_logits).reshape(-1)
    table_terms = jax.ops.segment_sum(hard_terms, flat_ids, num_segments=passages * n_owners)
    table_scalars = jax.ops.segment_sum(hard_scalars, flat_ids, num_segments=passages * n_owners)
    home_terms, home_scalars = (
        lax.psum_scatter(
            table_terms.astype(jnp.bfloat16), "dp", scatter_dimension=0, tiled=True
        ).astype(jnp.float32),
        lax.psum_scatter(
            table_scalars.astype(jnp.bfloat16), "dp", scatter_dimension=0, tiled=True
        ).astype(jnp.float32),
    )
    batch_to_pass = lax.dot_general(
        batch_softmax_weight,
        query_hidden_states,
        (((0,), (0,)), ((), ())),
        preferred_element_type=single_float,
    )
    pass_scalar = home_scalars + jnp.sum(batch_coefficient * batch_logits, axis=0)
    grad_pooled = (
        home_terms
        + batch_to_pass
        - (pass_scalar * passage_inverse * passage_inverse)[:, None] * pooled_f32
    )
    grad_normed = ((grad_pooled / length_f32)[:, None, :] * valid[:, :, None]).reshape(
        tokens, width_portion
    )
    gain_grad = gain_f32 * grad_normed
    inner_sum = token_totals(jnp.sum(residual_stream * gain_grad, axis=1))[:, None]
    grad_stream = (
        inverse_rms * gain_grad - residual_stream * inverse_rms**3 * inner_sum / full_width
    )
    residual_gradient = grad_stream.astype(jnp.bfloat16)
    adapter_partial_sum = lax.dot_general(
        residual_gradient,
        adapter_up_matrix,
        (((1,), (1,)), ((), ())),
        preferred_element_type=single_float,
    )
    adapter_backward = (2.0 * token_totals(adapter_partial_sum)).astype(jnp.bfloat16)
    partial_terms = lax.dot_general(
        residual_gradient,
        output_projection_weight,
        (((1,), (1,)), ((), ())),
        preferred_element_type=single_float,
    )
    summed_terms = lax.psum_scatter(
        partial_terms.astype(jnp.bfloat16), "mp", scatter_dimension=1, tiled=True
    ).astype(jnp.float32)
    down_matrix_block = lax.dynamic_slice_in_dim(
        adapter_down_matrix, lax.axis_index("mp") * width_portion, width_portion, 0
    )
    local_term = lax.dot_general(
        adapter_backward,
        down_matrix_block,
        (((1,), (1,)), ((), ())),
        preferred_element_type=single_float,
    )
    attention_gradient = (summed_terms + local_term).astype(jnp.bfloat16)
    down_partial_sum = lax.dot_general(
        attention_output,
        adapter_backward,
        (((0,), (0,)), ((), ())),
        preferred_element_type=single_float,
    )
    up_partial_sum = lax.dot_general(
        adapter_middle,
        residual_gradient,
        (((0,), (0,)), ((), ())),
        preferred_element_type=single_float,
    )
    down_matrix_gradient, up_total_sum = (
        lax.psum(down_partial_sum.astype(jnp.bfloat16), "dp").astype(jnp.float32),
        lax.psum(up_partial_sum.astype(jnp.bfloat16), "dp").astype(jnp.float32),
    )
    up_matrix_gradient = 2.0 * up_total_sum
    return (
        per_query_loss,
        query_gradient,
        residual_gradient,
        attention_gradient,
        down_matrix_gradient,
        up_matrix_gradient,
    )


def solution(mesh):
    in_specs = (
        P("dp", "mp"),
        P("dp", "mp"),
        P(None, "mp"),
        P(),
        P(None, "mp"),
        P("mp"),
        P("dp", "mp"),
        P("dp", None),
        P("dp"),
    )
    out_specs = (P("dp"), P("dp", "mp"), P("dp", "mp"), P("dp", "mp"), P("mp", None), P(None, "mp"))
    return jax.shard_map(body, mesh=mesh, in_specs=in_specs, out_specs=out_specs, check_vma=False)
```

profile of v0, /device:TPU:0, one launch (start us, length us, event | category | flops | bytes accessed | tf_op | source)
XLA Modules:
  0.0 481.0 jit_solution(8652517450530126003)
XLA Ops:
  7.2 0.7 all-gather.3.cloned.1.call-update
  8.0 0.7 convert_element_type.117
  8.6 0.7 convert_element_type.115
  9.3 0.7 fusion.13
  10.1 50.6 %all-gather.3.cloned.1.call-done = bf16[512,4096]{1,0:T(8,128)(2,1)} async-done(((bf16[512,1024]{1,0:T(8,128)(2,1)}), bf16[512,4096]{1,0:T(8,128)(2,1)}) %all-gather.3.cloned.1.call-update) | async-done | bytes 4194320 | tf_op jit(solution)/shard_map/all_gather | solution.py:32
  60.6 3.5 convolution_convert_fusion.4
  64.2 7.0 %fusion.28 = f32[512,1024]{1,0:T(8,128)S(1)} fusion(bf16[512,4096]{1,0:T(8,128)(2,1)S(1)} %copy-done.5, bf16[4096,1024]{1,0:T(8,128)(2,1)} %param.11), kind=kOutput, calls=%fused_computation.79 | convolution fusion | flops 4294967296 | bytes 14680064 | tf_op jit(solution)/shard_map/dot_general | solution.py:33
  71.2 0.6 multiply_reduce_fusion.2
  71.8 8.5 %psum.70 = bf16[512]{0:T(512)(128)(2,1)S(1)} all-reduce(bf16[512]{0:T(512)(128)(2,1)S(1)} %get-tuple-element.28), channel_id=1, replica_groups=mesh['dp'=32,'mp'=4] {'mp'}, use_global_device_ids=true, to_apply=%region_1.0 | all-reduce | flops 512 | bytes 2048 | tf_op jit(solution)/shard_map/psum | solution.py:11
  80.3 0.5 multiply_multiply_fusion.6
  80.9 1.6 multiply_multiply_fusion.1
  82.5 2.8 reshape.113
  85.3 3.0 multiply_reduce_fusion.1
  88.3 0.8 fusion.10
  89.3 0.1 copy.19
  89.3 0.1 reshape.114
  89.5 0.1 reshape.129
  89.6 2.1 mul.264
  91.7 3.1 mul.265
  94.9 0.1 multiply_reduce_fusion.3
  95.0 0.2 convolution_bitcast_fusion
  95.2 46.3 %all-gather.5.cloned.1.call-done = bf16[4096,1024]{1,0:T(8,128)(2,1)} async-done(((bf16[128,1024]{1,0:T(8,128)(2,1)}), bf16[4096,1024]{1,0:T(8,128)(2,1)}) %all-gather.5.cloned.1.call-update) | async-done | bytes 8388624 | tf_op jit(solution)/shard_map/all_gather | solution.py:55
  141.4 8.3 %gather_fusion = bf16[544,1024]{1,0:T(8,128)(2,1)S(1)} fusion(bf16[4096,1024]{1,0:T(8,128)(2,1)} %all-gather.5.cloned.1.call-done, s32[1024]{0:T(1024)S(1)} %pad_clamp_fusion), kind=kCustom, calls=%fused_computation | custom fusion | bytes 2230400 | tf_op jit(solution)/shard_map/gather | solution.py:56
  149.8 1.4 reshape.115
  151.2 1.8 fusion.2
  153.1 2.0 fusion.11
  155.0 17.7 %all-reduce.1 = (f32[32,17]{1,0:T(8,128)S(1)}, f32[32,17]{1,0:T(8,128)S(1)}, f32[32]{0:T(128)S(1)}, f32[128]{0:T(128)S(1)}, f32[32,128]{1,0:T(8,128)S(1)}) all-reduce(f32[32,17]{1,0:T(8,128)S(1)} %bitcast.32, f32[32,17]{1,0:T(8,128)S(1)} %fusion.2, f32[32]{0:T(128)S(1)} %multiply_reduce_fusion.3, ...), channel_id=1, replica_groups=mesh['dp'=32,'mp'=4] {'mp'}, use_global_device_ids=true, to_apply=%region_3.0 | all-reduce | flops 5344 | bytes 42752 | tf_op jit(solution)/shard_map/psum | solution.py:69
  172.8 0.2 exponential_reduce_fusion.1
  173.0 0.1 slice_reduce_fusion
  173.1 0.2 exponential_reduce_fusion
  173.3 0.5 fusion.27
  173.8 0.8 fusion.26
  174.6 0.1 reshape.117
  174.7 17.6 %scatter_custom_fusion = f32[4096,1024]{1,0:T(8,128)} fusion(s32[544]{0:T(1024)S(1)} %reshape.129, f32[]{:T(128)} %constant.12.clone.1, f32[544,1024]{1,0:T(8,128)} %mul.265, f32[544]{0:T(1024)S(1)} %reshape.117), kind=kCustom, calls=%fused_computation.3 | custom fusion | flops 1114112 | bytes 19009540 | tf_op jit(solution)/shard_map/scatter-add | solution.py:110
  192.4 9.1 %convert_element_type.125 = bf16[4096,1024]{1,0:T(8,128)(2,1)} convert(f32[4096,1024]{1,0:T(8,128)} %scatter_custom_fusion) | non-fusion elementwise | flops 4194304 | bytes 25165824 | tf_op jit(solution)/shard_map/convert_element_type | solution.py:114
  201.6 0.7 copy-done.12
  202.3 0.1 reshape.118
  202.5 0.6 dynamic-slice
  203.7 0.1 reshape.139
  203.8 4.8 scatter_custom_fusion.1
  208.6 64.6 %all-reduce = bf16[4096]{0:T(1024)(128)(2,1)S(1)} all-reduce(bf16[4096]{0:T(1024)(128)(2,1)S(1)} %convert_element_type.127), channel_id=3, replica_groups=mesh['dp'=32,'mp'=4] {'dp'}, use_global_device_ids=true, to_apply=%region_17.0.clone | all-reduce | flops 4096 | bytes 16384
  273.2 0.7 fusion.17
  274.0 0.1 multiply_multiply_fusion.7
  274.0 18.3 %reduce-scatter.3.cloned.1.call-done = bf16[128,1024]{1,0:T(8,128)(2,1)} async-done(((bf16[4096,1024]{1,0:T(8,128)(2,1)}), bf16[128,1024]{1,0:T(8,128)(2,1)}) %reduce-scatter.3.cloned.1.call-update) | async-done | bytes 262160 | tf_op jit(solution)/shard_map/reduce_scatter | solution.py:113
  292.4 1.3 fusion.5
  293.7 1.9 mul.271
  295.6 3.0 mul.272
  298.6 2.0 multiply_reduce_fusion
  300.6 10.9 %psum.76 = bf16[512]{0:T(512)(128)(2,1)S(1)} all-reduce(bf16[512]{0:T(512)(128)(2,1)S(1)} %multiply_reduce_fusion), channel_id=1, replica_groups=mesh['dp'=32,'mp'=4] {'mp'}, use_global_device_ids=true, to_apply=%region_20.0 | all-reduce | flops 512 | bytes 2048 | tf_op jit(solution)/shard_map/psum | solution.py:11
  311.5 2.2 subtract_convert_fusion
  313.8 0.9 convolution_convert_fusion.1
  314.6 0.4 convolution_convert_fusion.3
  315.0 14.3 %psum.77 = bf16[512,16]{0,1:T(8,128)(2,1)S(1)} all-reduce(bf16[512,16]{0,1:T(8,128)(2,1)S(1)} %convolution_convert_fusion.3), channel_id=1, replica_groups=mesh['dp'=32,'mp'=4] {'mp'}, use_global_device_ids=true, to_apply=%region_22.0 | all-reduce | flops 8192 | bytes 32768 | tf_op jit(solution)/shard_map/psum | solution.py:11
  329.3 0.9 fusion.9
  330.3 9.4 %convolution_convert_fusion = bf16[512,4096]{1,0:T(8,128)(2,1)} fusion(bf16[512,1024]{1,0:T(8,128)(2,1)S(1)} %subtract_convert_fusion, bf16[4096,1024]{1,0:T(8,128)(2,1)} %param.11), kind=kOutput, calls=%fused_computation.5 | convolution fusion | flops 4297064448 | bytes 13631488 | tf_op jit(solution)/shard_map/dot_general | solution.py:148
  339.8 0.5 copy-done.31
  340.4 0.7 copy-done.1
  341.1 0.4 fusion.15
  341.6 0.9 fusion.7
  342.5 81.0 %all-reduce.5.cloned.1.call-done = (bf16[1024,16]{0,1:T(8,128)(2,1)}, bf16[16,1024]{1,0:T(8,128)(2,1)}) async-done(((bf16[1024,16]{0,1:T(8,128)(2,1)}, bf16[16,1024]{1,0:T(8,128)(2,1)}), (bf16[1024,16]{0,1:T(8,128)(2,1)}, bf16[16,1024]{1,0:T(8,128)(2,1)})) %all-reduce.5.cloned.1.call-update) | async-done | bytes 65552 | tf_op jit(solution)/shard_map/psum | solution.py:180
  423.5 1.4 convert_element_type.142
  424.9 1.4 convert_multiply_fusion.3
  426.3 45.6 %reduce-scatter.5.cloned.1.call-done = bf16[512,1024]{1,0:T(8,128)(2,1)} async-done(((bf16[512,4096]{1,0:T(8,128)(2,1)}), bf16[512,1024]{1,0:T(8,128)(2,1)}) %reduce-scatter.5.cloned.1.call-update) | async-done | bytes 1048592 | tf_op jit(solution)/shard_map/reduce_scatter | solution.py:154
  471.9 2.6 add_convert_fusion
  (94 shorter events, 0.6 us)
Async XLA Ops:
  7.2 53.5 %copy-start = (bf16[4096,16]{0,1:T(8,128)(2,1)S(1)}, bf16[4096,16]{0,1:T(8,128)(2,1)}, u32[]{:S(2)}) copy-start(bf16[4096,16]{0,1:T(8,128)(2,1)} %param.12) | copy-start | bytes 393220
  7.2 53.4 %all-gather.3.cloned.1.call-start = ((), (), s32[]{:S(2)}) async-start(), calls=%async_computation.2 | async-start | bytes 5242880 | tf_op jit(solution)/shard_map/all_gather | solution.py:32
  7.9 133.5 %all-gather.5.cloned.1.call-start = ((), (), s32[]{:S(2)}) async-start(), calls=%async_computation.3 | async-start | bytes 8650752 | tf_op jit(solution)/shard_map/all_gather | solution.py:55
  8.6 79.7 %copy-start.35 = (f32[128]{0:T(128)}, f32[128]{0:T(128)S(1)}, u32[]{:S(2)}) copy-start(f32[128]{0:T(128)S(1)} %convert_element_type.117) | copy-start | bytes 1540
  9.3 71.6 %copy-start.19 = (f32[1024]{0:T(1024)}, f32[1024]{0:T(1024)S(1)}, u32[]{:S(2)}) copy-start(f32[1024]{0:T(1024)S(1)} %convert_element_type.115) | copy-start | bytes 12292
  10.1 75.3 %copy-start.11 = (f32[128,4]{1,0:T(8,128)}, f32[128,4]{1,0:T(8,128)S(1)}, u32[]{:S(2)}) copy-start(f32[128,4]{1,0:T(8,128)S(1)} %fusion.13) | copy-start | bytes 6148
  60.6 3.5 copy-start.5
  64.2 7.0 %copy-start.10 = (bf16[512,1024]{1,0:T(8,128)(2,1)S(1)}, bf16[512,1024]{1,0:T(8,128)(2,1)}, u32[]{:S(2)}) copy-start(bf16[512,1024]{1,0:T(8,128)(2,1)} %param.10) | copy-start | bytes 3145732
  64.2 7.0 %copy-start.15 = (bf16[16,1024]{1,0:T(8,128)(2,1)S(1)}, bf16[16,1024]{1,0:T(8,128)(2,1)}, u32[]{:S(2)}) copy-start(bf16[16,1024]{1,0:T(8,128)(2,1)} %param.13) | copy-start | bytes 98308
  80.9 1.6 copy-start.22
  85.3 3.9 copy-start.23
  85.3 4.2 copy-start.7
  89.2 203.1 %reduce-scatter.3.cloned.1.call-start = ((), (), s32[]{:S(2)}) async-start(), calls=%async_computation.4 | async-start | bytes 8650752 | tf_op jit(solution)/shard_map/reduce_scatter | solution.py:113
  89.6 85.2 %copy-start.30 = (s32[544]{0:T(1024)}, s32[544]{0:T(1024)S(1)}, u32[]{:S(2)}) copy-start(s32[544]{0:T(1024)S(1)} %reshape.129) | copy-start | bytes 6532
  91.7 3.3 copy-start.3
  172.7 0.6 copy-start.37
  172.7 119.6 %copy-start.13 = (f32[32,128]{1,0:T(8,128)}, f32[32,128]{1,0:T(8,128)S(1)}, u32[]{:S(2)}) copy-start(f32[32,128]{1,0:T(8,128)S(1)} %get-tuple-element.12) | copy-start | bytes 49156
  172.8 119.6 %copy-start.28 = (f32[128]{0:T(128)}, f32[128]{0:T(128)S(1)}, u32[]{:S(2)}) copy-start(f32[128]{0:T(128)S(1)} %add_rsqrt_fusion.2) | copy-start | bytes 1540
  172.8 119.5 %copy-start.24 = (f32[32]{0:T(128)}, f32[32]{0:T(128)S(1)}, u32[]{:S(2)}) copy-start(f32[32]{0:T(128)S(1)} %get-tuple-element.27) | copy-start | bytes 388
  172.8 119.5 %copy-start.32 = (f32[32]{0:T(128)}, f32[32]{0:T(128)S(1)}, u32[]{:S(2)}) copy-start(f32[32]{0:T(128)S(1)} %get-tuple-element.26) | copy-start | bytes 388
  173.8 118.5 %copy-start.26 = (f32[32]{0:T(128)}, f32[32]{0:T(128)S(1)}, u32[]{:S(2)}) copy-start(f32[32]{0:T(128)S(1)} %get-tuple-element.18) | copy-start | bytes 388
  174.6 17.8 %copy-start.17 = (bf16[32,17]{1,0:T(8,128)(2,1)}, bf16[32,17]{1,0:T(8,128)(2,1)S(1)}, u32[]{:S(2)}) copy-start(bf16[32,17]{1,0:T(8,128)(2,1)S(1)} %get-tuple-element.23) | copy-start | bytes 3268
  201.5 0.8 copy-start.12
  201.5 1.0 copy-start.39
  201.5 90.9 %copy-start.4 = (bf16[128,1024]{1,0:T(8,128)(2,1)S(1)}, bf16[128,1024]{1,0:T(8,128)(2,1)}, u32[]{:S(2)}) copy-start(bf16[128,1024]{1,0:T(8,128)(2,1)} %get-tuple-element.22) | copy-start | bytes 786436
  201.5 90.9 %copy-start.8 = (bf16[32,1024]{1,0:T(8,128)(2,1)S(1)}, bf16[32,1024]{1,0:T(8,128)(2,1)}, u32[]{:S(2)}) copy-start(bf16[32,1024]{1,0:T(8,128)(2,1)} %param.15) | copy-start | bytes 196612
  201.5 90.9 %copy-start.36 = (f32[128]{0:T(128)S(1)}, f32[128]{0:T(128)}, u32[]{:S(2)}) copy-start(f32[128]{0:T(128)} %copy-done.35) | copy-start | bytes 1540
  201.5 222.0 %all-reduce.5.cloned.1.call-start = ((), (), s32[]{:S(2)}) async-start(), calls=%async_computation.6 | async-start | bytes 131072 | tf_op jit(solution)/shard_map/psum | solution.py:180
  202.4 96.1 %copy-start.21 = (f32[512]{0:T(512)}, f32[512]{0:T(512)S(1)}, u32[]{:S(2)}) copy-start(f32[512]{0:T(512)S(1)} %reshape.118) | copy-start | bytes 6148
  295.6 3.0 copy-start.20
  311.5 3.1 copy-start.16
  313.8 26.0 %copy-start.2 = (bf16[512,1024]{1,0:T(8,128)(2,1)}, bf16[512,1024]{1,0:T(8,128)(2,1)S(1)}, u32[]{:S(2)}) copy-start(bf16[512,1024]{1,0:T(8,128)(2,1)S(1)} %subtract_convert_fusion) | copy-start | bytes 3145732
  313.8 15.5 %copy-start.6 = (bf16[512,1024]{1,0:T(8,128)(2,1)S(1)}, bf16[512,1024]{1,0:T(8,128)(2,1)}, u32[]{:S(2)}) copy-start(bf16[512,1024]{1,0:T(8,128)(2,1)} %param.9) | copy-start | bytes 3145732
  330.2 141.6 %reduce-scatter.5.cloned.1.call-start = ((), (), s32[]{:S(2)}) async-start(), calls=%async_computation.5 | async-start | bytes 5242880 | tf_op jit(solution)/shard_map/reduce_scatter | solution.py:154
  339.7 0.6 copy-start.31
  339.7 0.7 copy-start.34
  339.7 0.7 copy-start.38
  339.7 1.4 copy-start.1
  339.7 1.4 copy-start.18
  339.7 1.8 copy-start.9
  339.7 1.8 copy-start.14
  339.8 1.8 copy-start.25
  339.8 1.8 copy-start.27
  339.8 1.8 copy-start.29
  339.8 1.8 copy-start.33
Sparse Core Ops, SparseCore 0:
  9.7 50.9 all-gather.2
  89.3 52.0 all-gather.4
  201.7 90.6 reduce-scatter.2
  330.3 93.1 all-reduce.4
  425.7 46.0 reduce-scatter.4
where the time goes:
time: 483 us; the launch traced here: 481 us
  waiting for transfers between devices  242 us (50%)
  blocking collectives  116 us (24%)
  other arithmetic  51.1 us (11%)
  matrix products  30 us (6%)
  local copies, waits for them, and re-layouts  26.3 us (5%)
  between operations  14.9 us (3%)
    psum x1, waiting for transfers between devices, body(): lax.psum(down_partial_sum.astype(jnp.bfloat16), 'dp').astype(jnp.float32)  81 us
    unnamed x1, blocking collectives  64.6 us
    all_gather x1, waiting for transfers between devices, body(): fragment = lax.all_gather(attention_output, 'mp', axis=1, tiled=True)  50.6 us
    all_gather x1, waiting for transfers between devices, body(): every_row = lax.all_gather(pooled_b, 'dp', axis=0, tiled=True)  46.3 us
    reduce_scatter x1, waiting for transfers between devices, body(): lax.psum_scatter(partial_terms.astype(jnp.bfloat16), 'mp', scatter_dimens...  45.6 us
    psum x3, blocking collectives, token_totals(): return lax.psum(values.astype(jnp.bfloat16), 'mp').astype(jnp.float32)  33.7 us
    reduce_scatter x1, waiting for transfers between devices, body(): lax.psum_scatter(table_terms.astype(jnp.bfloat16), 'dp', scatter_dimensio...  18.3 us
    psum x1, blocking collectives, body(): lax.psum((negative_product, batch_product, hard_square, pass_square, quer...  17.7 us
  transfers between devices with their start and end apart: 5, of which 5 were waited for; matrix products, arithmetic and copies ran while one was open for 6% of the time, Pallas kernels for 0%

commit v1 on v0

v1 whole, which is shorter than its diff:
```python
import jax
import jax.numpy as jnp
from jax import lax
from jax.experimental import pallas as pl
from jax.experimental.pallas import tpu as pltpu
from jax.sharding import PartitionSpec as P

F32 = jnp.float32
BF16 = jnp.bfloat16
INV_TEMPER = 1.0 / 0.02
LOSS_SCALE = 1024.0
SLOTS = 32
PAIRS = [(a, b) for a in range(4) for b in range(a, 4)]


def dot(a, b, dims):
    return lax.dot_general(a, b, ((dims[0], dims[1]), ((), ())), preferred_element_type=F32)


def split3(x):
    a = x.astype(BF16).astype(F32)
    b = (x - a).astype(BF16).astype(F32)
    return [a, b, x - a - b]


def iota(shape, dim):
    return lax.broadcasted_iota(jnp.int32, shape, dim)


def stack_rows(rows, height):
    where = iota((height, rows[0].shape[1]), 0)
    total = jnp.zeros((height, rows[0].shape[1]), F32)
    for place, row in enumerate(rows):
        total = jnp.where(where == place, row, total)
    return total


def decode(code):
    used = code > 0
    value = code - 1
    return used, value >> 8, (value >> 1) & 127, value & 1


def partial_kernel(stream, qslot, qown, code, squares, gain, pack):
    used, _, passage, _ = decode(code[...])
    onehot = (iota((128, 1024), 0) == passage) & used
    g = gain[...]
    columns = []
    scaled = []
    for s in range(4):
        x = stream[s * 128 : s * 128 + 128, :]
        u = x * g
        scaled.append(u)
        columns.append(jnp.sum(x * x, axis=1, keepdims=True))
        ub = u.astype(BF16)
        scores = dot(ub, qslot[...], ((1,), (1,)))
        pack[16 + s : 17 + s, :] = jnp.sum(jnp.where(onehot, scores, 0.0), axis=0, keepdims=True)
        batch = dot(qown[...], ub, ((1,), (1,)))
        pack[0:16, s * 128 : s * 128 + 128] = batch[0:16]
        pack[0:16, 512 + s * 128 : 640 + s * 128] = batch[16:32]
    for a, b in PAIRS:
        columns.append(jnp.sum(scaled[a] * scaled[b], axis=1, keepdims=True))
    lane = iota((128, 128), 1)
    table = jnp.zeros((128, 128), F32)
    for place, column in enumerate(columns):
        table = jnp.where(lane == place, column, table)
    table = table.T
    pack[20:21, :] = squares[0:1, :]
    pack[21:23, :] = jnp.zeros((2, 1024), F32)
    for place in range(len(columns)):
        row, off = 21 + place // 8, (place % 8) * 128
        pack[row : row + 1, off : off + 128] = table[place : place + 1, :]
    pack[23:24, :] = squares[1:2, :]


def score_kernel(p0, p1, p2, p3, code, lens, home, slot, batch, stats, sums):
    def total(rows, lanes):
        return (p0[rows, lanes] + p2[rows, lanes]) + (p1[rows, lanes] + p3[rows, lanes])

    def stat(place):
        row, off = 21 + place // 8, (place % 8) * 128
        return total(slice(row, row + 1), slice(off, off + 128))

    every = slice(0, 1024)
    used, query, passage, first = decode(code[...])
    length = lens[...]
    inv = [lax.rsqrt(stat(s) / 4096.0 + 1e-05) for s in range(4)]
    a = [jnp.where(s < length, inv[s] / length, 0.0) for s in range(4)]
    gram = {pair: stat(4 + i) for i, pair in enumerate(PAIRS)}
    toward = [
        sum(a[t] * gram[(min(s, t), max(s, t))] for t in range(4)) for s in range(4)
    ]
    square = sum(a[s] * toward[s] for s in range(4))
    pinv = lax.rsqrt(square + 1e-06)
    rows = []
    for row in a + [pinv]:
        rows += split3(row)
    onehot = jnp.where((iota((128, 1024), 0) == passage) & used, 1.0, 0.0).astype(BF16)
    picked = dot(stack_rows(rows, 16).astype(BF16), onehot, ((1,), (0,)))
    pick = [
        picked[3 * i : 3 * i + 1] + picked[3 * i + 1 : 3 * i + 2] + picked[3 * i + 2 : 3 * i + 3]
        for i in range(5)
    ]
    dots = [total(slice(16 + s, 17 + s), every) for s in range(4)]
    product = pick[0] * dots[0] + pick[1] * dots[1] + pick[2] * dots[2] + pick[3] * dots[3]
    qinv = lax.rsqrt(total(slice(20, 21), every) + 1e-06)
    pre = qinv * pick[4] * INV_TEMPER
    score = product * pre
    grown = jnp.where(used, jnp.exp(score), 0.0)
    slot[0:1, :] = score
    slot[1:2, :] = pre
    for s in range(4):
        slot[2 + s : 3 + s, :] = dots[s]
    slot[6:8, :] = jnp.zeros((2, 1024), F32)

    own = total(slice(23, 24), slice(0, 128))
    lane = iota((32, 128), 1)
    qcol = lax.rsqrt(
        jnp.sum(jnp.where(lane == iota((32, 128), 0), own, 0.0), axis=1, keepdims=True) + 1e-06
    )
    pieces = []
    for s in range(4):
        top = total(slice(0, 16), slice(s * 128, s * 128 + 128))
        low = total(slice(0, 16), slice(512 + s * 128, 640 + s * 128))
        pieces.append(jnp.concatenate([top, low], axis=0))
        batch[:, 256 + s * 128 : 384 + s * 128] = pieces[s]
    bpre = qcol * pinv * INV_TEMPER
    bscore = sum(a[s] * pieces[s] for s in range(4)) * bpre
    bgrown = jnp.exp(bscore)
    batch[:, 0:128] = bscore
    batch[:, 128:256] = bpre

    stats[...] = stack_rows(a + inv + toward + [pinv], 16)

    mine = iota((32, 1024), 0) == query
    block = ((iota((1024, 128), 0) >> 5) == iota((1024, 128), 1)).astype(F32).astype(BF16)

    def by_query(row):
        out = jnp.zeros((32, 128), F32)
        for part in split3(row):
            out += dot(jnp.where(mine, part, 0.0).astype(BF16), block, ((1,), (0,)))
        return out

    at_home = lane == home[...]
    exp_sum = by_query(grown) + jnp.where(at_home, jnp.sum(bgrown, axis=1, keepdims=True), 0.0)
    weighted = by_query(grown * score) + jnp.where(
        at_home, jnp.sum(bgrown * bscore, axis=1, keepdims=True), 0.0
    )
    positive = by_query(jnp.where(used & (first == 1), score, 0.0))
    sums[:, 0:128] = exp_sum
    sums[:, 128:256] = weighted
    sums[:, 256:384] = positive
    sums[:, 384:512] = jnp.broadcast_to(qcol, (32, 128))


def gradient_kernel(
    recv, stream, qslot, qown, gain, code, slot, batch, stats, home,
    grad, weights, pooled_out, bweights, logs, scratch,
):
    used, query, passage, first = decode(code[...])
    log_row = jnp.log(jnp.sum(recv[:, 0:1024], axis=0, keepdims=True))
    spread = iota((32, 1024), 0) == (iota((32, 1024), 1) >> 5)
    place = ((iota((1024, 128), 0) & 31) == iota((1024, 128), 1)).astype(F32).astype(BF16)
    table = jnp.zeros((32, 128), F32)
    for part in split3(log_row):
        table += dot(jnp.where(spread, part, 0.0).astype(BF16), place, ((1,), (0,)))
    block = (iota((128, 1024), 0) == (iota((128, 1024), 1) >> 5)).astype(F32).astype(BF16)
    wide = jnp.zeros((32, 1024), F32)
    for part in split3(table):
        wide += dot(part.astype(BF16), block, ((1,), (0,)))
    log_slot = jnp.sum(jnp.where(iota((32, 1024), 0) == query, wide, 0.0), axis=0, keepdims=True)
    log_col = jnp.sum(jnp.where(iota((32, 128), 1) == home[...], table, 0.0), axis=1, keepdims=True)
    logs[...] = jnp.broadcast_to(log_col, (32, 128))

    score = slot[0:1, :]
    coef = jnp.where(used, LOSS_SCALE * (jnp.exp(score - log_slot) - first.astype(F32)), 0.0)
    weight = (coef * slot[1:2, :]).astype(BF16).astype(F32)
    bscore = batch[:, 0:128]
    bcoef = LOSS_SCALE * jnp.exp(bscore - log_col)
    bweight = (bcoef * batch[:, 128:256]).astype(BF16).astype(F32)
    bweights[...] = bweight.astype(BF16)
    onehot = (iota((128, 1024), 0) == passage) & used
    spread_weight = jnp.where(onehot, weight, 0.0)
    wb = spread_weight.astype(BF16)
    weights[...] = wb
    scalar = jnp.sum(jnp.where(onehot, coef * score, 0.0), axis=1, keepdims=True)

    rows = [jnp.sum(bcoef * bscore, axis=0, keepdims=True)]
    for s in range(4):
        rows.append(
            jnp.sum(bweight * batch[:, 256 + s * 128 : 384 + s * 128], axis=0, keepdims=True)
        )
    rows += [stats[i : i + 1, :] for i in range(13)]
    cols = stack_rows(rows, 128).T

    def col(i):
        return cols[:, i : i + 1]

    pinv = col(17)
    scale = (scalar + col(0)) * pinv * pinv
    g = gain[...]
    xs = [stream[s * 128 : s * 128 + 128, :] for s in range(4)]
    pooled = sum(col(5 + s) * (xs[s] * g) for s in range(4)).astype(BF16)
    pooled_out[...] = pooled
    gp = dot(wb, qslot[...], ((1,), (0,)))
    bt = jnp.concatenate([bweight, jnp.zeros((96, 128), F32)], axis=0).T.astype(BF16)
    qpad = jnp.concatenate([qown[...], jnp.zeros((96, 1024), BF16)], axis=0)
    gp = gp + dot(bt, qpad, ((1,), (0,))) - scale * pooled.astype(F32)
    gg = gp * g
    for s in range(4):
        a, inv = col(5 + s), col(9 + s)
        inner = (
            jnp.sum(spread_weight * slot[2 + s : 3 + s, :], axis=1, keepdims=True)
            + col(1 + s)
            - scale * col(13 + s)
        )
        beta = inv * inv * a * inner / 4096.0
        scratch[s * 128 : s * 128 + 128, :] = (a * gg - beta * xs[s]).astype(BF16)
    token = iota((512, 512), 0)
    order = ((token & 3) * 128 + (token >> 2) == iota((512, 512), 1)).astype(F32).astype(BF16)
    grad[...] = dot(order, scratch[...], ((1,), (0,))).astype(BF16)


def call(kernel, outs, *args, scratch=()):
    return pl.pallas_call(
        kernel,
        out_shape=[jax.ShapeDtypeStruct(s, t) for s, t in outs],
        in_specs=[pl.BlockSpec(memory_space=pltpu.VMEM)] * len(args),
        out_specs=[pl.BlockSpec(memory_space=pltpu.VMEM)] * len(outs),
        scratch_shapes=list(scratch),
        compiler_params=pltpu.CompilerParams(vmem_limit_bytes=40 * 2**20),
    )(*args)


def ring(x, step):
    return lax.ppermute(x, "mp", [(i, (i + step) % 4) for i in range(4)])


def ring_sum(x):
    return (x + ring(x, 2)) + (ring(x, 1) + ring(x, 3))


def grid_index(x, y, core):
    return (x * 4 + y) * 2 + core


def grid_shift(v, axis, step):
    pairs = []
    for x in range(4):
        for y in range(4):
            for core in range(2):
                if axis == "core":
                    to = (x, y, 1 - core)
                elif axis == "x":
                    to = ((x + step) % 4, y, core)
                else:
                    to = (x, (y + step) % 4, core)
                pairs.append((grid_index(x, y, core), grid_index(*to)))
    return lax.ppermute(v, "dp", pairs)


def grid_sum(x):
    x = x.astype(BF16)
    x = (x.astype(F32) + grid_shift(x, "core", 1).astype(F32)).astype(BF16)
    for axis in ("x", "y"):
        parts = [x] + [grid_shift(x, axis, step) for step in (1, 2, 3)]
        parts = [p.astype(F32) for p in parts]
        x = (parts[0] + parts[2]) + (parts[1] + parts[3])
        x = x.astype(BF16) if axis == "x" else x
    return x


def body(
    attention_output,
    residual,
    output_projection_weight,
    adapter_down_matrix,
    adapter_up_matrix,
    final_norm_gain,
    query_hidden_states,
    pair_passage_index,
    lengths,
):
    me = lax.axis_index("mp")
    home = jnp.full((1, 128), lax.axis_index("dp"), jnp.int32)
    half = 256

    def rows_of(matrix, offset):
        return lax.dynamic_slice_in_dim(matrix, ((me + offset) % 4) * 1024, 1024, 0)

    top, low = attention_output[:half], attention_output[half:]
    left_top, right_low = ring(top, 1), ring(low, 3)
    left_low, right_top = ring(low, 1), ring(top, 3)
    far_top, far_low = ring(left_top, 1), ring(right_low, 3)

    flat = pair_passage_index.reshape(-1)
    entries = flat.shape[0]
    place = jnp.arange(entries)
    owned = (flat[None, :] >> 7) == jnp.arange(32)[:, None]
    before = (place[:, None] < place[None, :]).astype(BF16)
    rank = dot(owned.astype(BF16), before, ((1,), (0,))).astype(jnp.int32)
    value = 1 + 2 * (128 * (place // 17) + (flat & 127)) + (place % 17 == 0)
    rank = jnp.where(owned, rank, -1)
    code_out = jnp.sum(
        jnp.where(rank[:, None, :] == jnp.arange(SLOTS)[None, :, None], value[None, None, :], 0),
        axis=2,
    )
    used_out, query_out, _, _ = decode(code_out)
    hot = (used_out[:, :, None] & (query_out[:, :, None] == jnp.arange(32))).reshape(1024, 32)
    hot_b = hot.astype(BF16)
    qslot_out = dot(hot_b, query_hidden_states, ((1,), (0,))).astype(BF16)
    query_f32 = query_hidden_states.astype(F32)
    own_square = jnp.sum(query_f32 * query_f32, axis=1)
    slot_square = jnp.sum(jnp.where(hot, own_square[None, :], 0.0), axis=1).reshape(32, SLOTS)
    table = lax.all_to_all(
        jnp.concatenate([code_out.astype(F32), slot_square], axis=1), "dp", 0, 0, tiled=True
    )
    code = table[:, :SLOTS].reshape(1, 1024).astype(jnp.int32)
    squares = jnp.concatenate(
        [table[:, SLOTS:].reshape(1, 1024), jnp.pad(own_square, (0, 992)).reshape(1, 1024)], axis=0
    )
    qslot = lax.all_to_all(qslot_out, "dp", 0, 0, tiled=True)

    middle = ring_sum(dot(rows_of(adapter_down_matrix, 0), attention_output, ((0,), (1,))))
    middle = middle.astype(BF16)
    weight = output_projection_weight
    row = iota((512, 512), 0)
    order = ((row & 127) * 4 + (row >> 7) == iota((512, 512), 1)).astype(BF16)

    def ordered(x):
        return dot(order, x, ((1,), (0,))).astype(BF16)

    stream = ordered(residual).astype(F32)
    stream = stream + dot(ordered(attention_output), rows_of(weight, 0), ((1,), (0,)))
    middle_ordered = dot(order, middle, ((1,), (1,))).astype(BF16)
    stream = stream + 2.0 * dot(middle_ordered, adapter_up_matrix, ((1,), (0,)))
    left = ordered(jnp.concatenate([left_top, left_low], 0))
    stream = stream + dot(left, rows_of(weight, 3), ((1,), (0,)))
    right = ordered(jnp.concatenate([right_top, right_low], 0))
    stream = stream + dot(right, rows_of(weight, 1), ((1,), (0,)))
    far_block = ordered(jnp.concatenate([far_top, far_low], 0))
    stream = stream + dot(far_block, rows_of(weight, 2), ((1,), (0,)))

    gain = final_norm_gain.astype(F32).reshape(1, 1024)
    (pack,) = call(
        partial_kernel,
        [((24, 1024), F32)],
        stream, qslot, query_hidden_states, code, squares, gain,
    )
    packs = [pack, ring(pack, 1), ring(pack, 2), ring(pack, 3)]
    lens = lengths.astype(F32).reshape(1, 128)
    slot, batch, stats, sums = call(
        score_kernel,
        [((8, 1024), F32), ((32, 768), F32), ((16, 128), F32), ((32, 512), F32)],
        *packs, code, lens, home,
    )
    exp_sums = jnp.broadcast_to(sums[:, 0:32].reshape(1, 1024), (32, 1024))
    recv = lax.all_to_all(
        jnp.concatenate([exp_sums, sums[:, 128:160].T, sums[:, 256:288].T], axis=1),
        "dp", 0, 0, tiled=True,
    )
    grad, weights, pooled, bweights, logs = call(
        gradient_kernel,
        [((512, 1024), BF16), ((128, 1024), BF16), ((128, 1024), BF16), ((32, 128), BF16), ((32, 128), F32)],
        recv, stream, qslot, query_hidden_states, gain, code, slot, batch, stats, home,
        scratch=[pltpu.VMEM((512, 1024), BF16)],
    )

    def back(offset, lo, hi):
        return dot(grad[lo:hi], rows_of(weight, offset), ((1,), (1,)))

    far = back(2, 0, 512).astype(BF16)
    via_right, via_left = ring(far[:half], 1), ring(far[half:], 3)
    to_right_low = ring(back(1, half, 512).astype(BF16), 1)
    to_left_top = ring(back(3, 0, half).astype(BF16), 3)
    to_right_top = ring((back(1, 0, half) + via_right.astype(F32)).astype(BF16), 1)
    to_left_low = ring((back(3, half, 512) + via_left.astype(F32)).astype(BF16), 3)

    rows = dot(weights, pooled, ((0,), (0,))).astype(BF16)
    arrived = lax.all_to_all(rows, "dp", 0, 0, tiled=True)
    others = jnp.sum(recv[:, 1024:1088], axis=0)
    log_total, positive = logs[:, 0], others[32:64]
    per_query_loss = log_total - positive
    query_scalar = LOSS_SCALE * (others[0:32] * jnp.exp(-log_total) - positive)
    qinv = sums[:, 384]
    query_gradient = (
        dot(hot_b, arrived, ((0,), (0,)))
        + dot(bweights, pooled, ((1,), (0,)))
        - (query_scalar * qinv * qinv)[:, None] * query_f32
    ).astype(BF16)

    lora_back = (2.0 * ring_sum(dot(adapter_up_matrix, grad, ((1,), (1,))))).astype(BF16)
    down_part = dot(lora_back, attention_output, ((1,), (0,)))
    up_part = dot(middle, grad, ((1,), (0,)))
    adapter = grid_sum(jnp.concatenate([down_part, up_part], axis=0))
    local = dot(lora_back, rows_of(adapter_down_matrix, 0), ((0,), (1,)))
    own = back(0, 0, 512) + local
    from_left = jnp.concatenate([to_right_top, to_right_low], 0).astype(F32)
    from_right = jnp.concatenate([to_left_top, to_left_low], 0).astype(F32)
    attention_gradient = (own + from_left + from_right).astype(BF16)
    return (
        per_query_loss,
        query_gradient,
        grad,
        attention_gradient,
        adapter[0:16].T,
        2.0 * adapter[16:32],
    )


def solution(mesh):
    in_specs = (
        P("dp", "mp"),
        P("dp", "mp"),
        P(None, "mp"),
        P(),
        P(None, "mp"),
        P("mp"),
        P("dp", "mp"),
        P("dp", None),
        P("dp"),
    )
    out_specs = (P("dp"), P("dp", "mp"), P("dp", "mp"), P("dp", "mp"), P("mp", None), P(None, "mp"))
    return jax.shard_map(body, mesh=mesh, in_specs=in_specs, out_specs=out_specs, check_vma=False)
```

time: 483 us -> 213 us (0.44)
  waiting for transfers between devices: 242 us -> 53 us
  blocking collectives: 116 us -> 0 us
  starting transfers between devices: 0.2 us -> 68.9 us
  other arithmetic: 51.1 us -> 4.37 us
  matrix products: 30 us -> 59.6 us
  between operations: 14.9 us -> 1.02 us
  local copies, waits for them, and re-layouts: 26.3 us -> 15 us
  Pallas kernels: 0 us -> 9.41 us
    all_gather x2 -> x0, waiting for transfers between devices: 96.8 us -> none  [the longest x1 50.6 us: body(): fragment = lax.all_gather(attention_output, 'mp', axis=1, tiled=True)]
    psum x1 -> x0, waiting for transfers between devices: 81 us -> none  [body(): lax.psum(down_partial_sum.astype(jnp.bfloat16), 'dp').astype(jnp.float32)]
    unnamed x1 -> x0, blocking collectives: 64.6 us -> none
    reduce_scatter x2 -> x0, waiting for transfers between devices: 63.9 us -> none  [the longest x1 45.6 us: body(): lax.psum_scatter(partial_terms.astype(jnp.bfloat16), 'mp', scatter_dimens...]
    psum x4 -> x0, blocking collectives: 51.4 us -> none  [the longest x3 33.7 us: token_totals(): return lax.psum(values.astype(jnp.bfloat16), 'mp').astype(jnp.float32)]
    ppermute x0 -> x28, waiting for transfers between devices: none -> 46.5 us  [the longest x21 26 us: ring(): return lax.ppermute(x, 'mp', [(i, (i + step) % 4) for i in range(4)])]
    ppermute x0 -> x28, starting transfers between devices: none -> 41.8 us  [the longest x21 28.6 us: ring(): return lax.ppermute(x, 'mp', [(i, (i + step) % 4) for i in range(4)])]
    dot_general x13 -> x22, matrix products: 30 us -> 59.6 us  [dot(): lax.dot_general(a, b, ((dims[0], dims[1]), ((), ())), preferred_element_t...]
  transfers between devices with their start and end apart: 5 -> 32, of which waited for: 5 -> 11; matrix products, arithmetic and copies ran while one was open for 6% -> 29% of each run, Pallas kernels for 0% -> 0%
where the time goes in v1:
time: 213 us; the launch traced here: 211 us
  starting transfers between devices  68.9 us (32%)
  matrix products  59.6 us (28%)
  waiting for transfers between devices  53 us (25%)
  local copies, waits for them, and re-layouts  15 us (7%)
  Pallas kernels  9.41 us (4%)
  other arithmetic  4.37 us (2%)
    dot_general x22, matrix products, dot(): lax.dot_general(a, b, ((dims[0], dims[1]), ((), ())), preferred_element_t...  59.6 us
    ppermute x21, starting transfers between devices, ring(): return lax.ppermute(x, 'mp', [(i, (i + step) % 4) for i in range(4)])  28.6 us
    ppermute x21, waiting for transfers between devices, ring(): return lax.ppermute(x, 'mp', [(i, (i + step) % 4) for i in range(4)])  26 us
    ppermute x7, waiting for transfers between devices, grid_shift(): return lax.ppermute(v, 'dp', pairs)  20.5 us
    ppermute x7, starting transfers between devices, grid_shift(): return lax.ppermute(v, 'dp', pairs)  13.2 us
    pallas_call x3, Pallas kernels, call(): pl.pallas_call(kernel, out_shape=[jax.ShapeDtypeStruct(s, t) for s, t in...  9.41 us
    all_to_all x1, starting transfers between devices, body(): lax.all_to_all(jnp.concatenate([exp_sums, sums[:, 128:160].T, sums[:, 256...  7.47 us
    all_to_all x1, starting transfers between devices, body(): qslot = lax.all_to_all(qslot_out, 'dp', 0, 0, tiled=True)  7.4 us
  transfers between devices with their start and end apart: 32, of which 11 were waited for; matrix products, arithmetic and copies ran while one was open for 29% of the time, Pallas kernels for 0%

profile of v1, /device:TPU:0, one launch (start us, length us, event | category | flops | bytes accessed | tf_op | source)
XLA Modules:
  0.0 211.2 jit_solution(3487638929509341558)
XLA Ops:
  0.7 2.4 %fusion.122 = (bf16[256,1024]{1,0:T(8,128)(2,1)}, bf16[256,1024]{1,0:T(8,128)(2,1)}) fusion(bf16[512,1024]{1,0:T(8,128)(2,1)} %param.9), kind=kLoop, calls=%fused_computation.147 | loop fusion | bytes 2097152 | tf_op jit(solution)/shard_map/slice | solution.py:291
  3.1 4.1 %collective-permute-start.5 = (bf16[256,1024]{1,0:T(8,128)(2,1)}, bf16[256,1024]{1,0:T(8,128)(2,1)}, u32[]{:S(2)}, u32[]{:S(2)}) collective-permute-start(bf16[256,1024]{1,0:T(8,128)(2,1)} %get-tuple-element.26), channel_id=1, source_target_pairs={{0,3},{1,0},{2,1},{3,2},{4,7},{5,4},{6,5},{7,6},{8,11},{9,8},{10,9... | collective-permute-start | bytes 1572872 | tf_op jit(solution)/shard_map/ppermute | solution.py:236
  7.2 1.1 fusion.84
  8.3 1.9 collective-permute-start
  10.2 2.2 %collective-permute-start.1 = (f32[16,512]{1,0:T(8,128)S(1)}, f32[16,512]{1,0:T(8,128)S(1)}, u32[]{:S(2)}, u32[]{:S(2)}) collective-permute-start(f32[16,512]{1,0:T(8,128)S(1)} %fusion.84), channel_id=1, source_target_pairs={{0,1},{1,2},{2,3},{3,0},{4,5},{5,6},{6,7},{7,4},{8,9},{9,10},{10,1... | collective-permute-start | bytes 98312 | tf_op jit(solution)/shard_map/ppermute | solution.py:236
  12.4 1.0 collective-permute-start.6
  15.9 7.3 %all-to-all-start.1 = ((f32[32,1,64]{2,1,0:T(1,128)}), f32[32,1,64]{2,1,0:T(1,128)S(1)}, u32[]{:S(2)}, u32[]{:S(2)}) async-start(f32[32,1,64]{2,1,0:T(1,128)} %bitcast.3), calls=%async_computation.1 | async-start | bytes 32768 | tf_op jit(solution)/shard_map/all_to_all | solution.py:315
  23.2 2.1 convolution_convert_fusion
  25.3 4.8 %fusion.6 = f32[512,1024]{1,0:T(8,128)} fusion(bf16[4096,1024]{1,0:T(8,128)(2,1)} %param.11, s32[]{:T(128)S(6)} %select_n.87, bf16[512,1024]{1,0:T(8,128)(2,1)S(1)} %copy-done.9, s32[512]{0:T(512)S(1)} %fusion.100), kind=kOutput, calls=%fused_computation.12 | convolution fusion | flops 1611399168 | bytes 5244932 | tf_op jit(solution)/shard_map/dot_general | solution.py:17
  30.1 1.7 convolution_convert_fusion.6
  31.9 7.4 %all-to-all-start = ((bf16[32,32,1024]{2,1,0:T(8,128)(2,1)}), bf16[32,32,1024]{2,1,0:T(8,128)(2,1)S(1)}, u32[]{:S(2)}, u32[]{:S(2)}) async-start(bf16[32,32,1024]{2,1,0:T(8,128)(2,1)} %bitcast.51), calls=%async_computation | async-start | bytes 4194304 | tf_op jit(solution)/shard_map/all_to_all | solution.py:322
  39.8 1.9 collective-permute-start.4
  41.7 1.7 collective-permute-done.2
  43.5 1.1 collective-permute-start.7
  44.5 2.2 %collective-permute-start.8 = (bf16[256,1024]{1,0:T(8,128)(2,1)}, bf16[256,1024]{1,0:T(8,128)(2,1)}, u32[]{:S(2)}, u32[]{:S(2)}) collective-permute-start(bf16[256,1024]{1,0:T(8,128)(2,1)} %collective-permute-done.6), channel_id=1, source_target_pairs={{0,3},{1,0},{2,1},{3,2},{4,7},{5,4},{6,5},{7,6},{8,11},{9,8},{10,9... | collective-permute-start | bytes 1572872 | tf_op jit(solution)/shard_map/ppermute | solution.py:236
  46.8 5.1 %fusion.12 = f32[512,1024]{1,0:T(8,128)} fusion(bf16[4096,1024]{1,0:T(8,128)(2,1)} %param.11, s32[]{:T(128)S(6)} %select_n.91, bf16[256,1024]{1,0:T(8,128)(2,1)} %collective-permute-done.6, bf16[256,1024]{1,0:T(8,128)(2,1)} %collective-permute-done.5, s32[512]{0:T(512)S(1)} %fusion.100), kind=kOutput, calls=%fused_computation.18 | convolution fusion | flops 1613496320 | bytes 5244932 | tf_op jit(solution)/shard_map/dot_general | solution.py:17
  51.9 4.3 %collective-permute-done.4 = bf16[256,1024]{1,0:T(8,128)(2,1)} collective-permute-done((bf16[256,1024]{1,0:T(8,128)(2,1)}, bf16[256,1024]{1,0:T(8,128)(2,1)}, u32[]{:S(2)}, u32[]{:S(2)}) %collective-permute-start.4) | collective-permute-done | bytes 524320 | tf_op jit(solution)/shard_map/ppermute | solution.py:236
  56.2 5.2 %fusion.18 = f32[512,1024]{1,0:T(8,128)} fusion(bf16[4096,1024]{1,0:T(8,128)(2,1)} %param.11, s32[]{:T(128)S(6)} %select_n.89, bf16[256,1024]{1,0:T(8,128)(2,1)} %collective-permute-done.4, bf16[256,1024]{1,0:T(8,128)(2,1)} %collective-permute-done.3, s32[512]{0:T(512)S(1)} %fusion.100), kind=kOutput, calls=%fused_computation.24 | convolution fusion | flops 1613496320 | bytes 5244932 | tf_op jit(solution)/shard_map/dot_general | solution.py:17
  61.3 5.2 %collective-permute-done.7 = bf16[256,1024]{1,0:T(8,128)(2,1)} collective-permute-done((bf16[256,1024]{1,0:T(8,128)(2,1)}, bf16[256,1024]{1,0:T(8,128)(2,1)}, u32[]{:S(2)}, u32[]{:S(2)}) %collective-permute-start.7) | collective-permute-done | bytes 524320 | tf_op jit(solution)/shard_map/ppermute | solution.py:236
  66.5 5.1 %fusion.2 = f32[512,1024]{1,0:T(8,128)} fusion(bf16[4096,1024]{1,0:T(8,128)(2,1)} %param.11, s32[]{:T(128)S(6)} %select_n.93, bf16[256,1024]{1,0:T(8,128)(2,1)} %collective-permute-done.8, bf16[256,1024]{1,0:T(8,128)(2,1)} %collective-permute-done.7, s32[512]{0:T(512)S(1)} %fusion.100), kind=kOutput, calls=%fused_computation.8 | convolution fusion | flops 1613496320 | bytes 5244932 | tf_op jit(solution)/shard_map/dot_general | solution.py:17
  71.6 6.0 %add_add_fusion.stream = f32[512,1024]{1,0:T(8,128)} fusion(f32[512,1024]{1,0:T(8,128)} %fusion.2, f32[512,1024]{1,0:T(8,128)} %fusion.12, f32[512,1024]{1,0:T(8,128)} %fusion.18, f32[512,1024]{1,0:T(8,128)} %fusion.6, bf16[512,1024]{1,0:T(8,128)(2,1)} %convolution_convert_fusion.6, bf16[16,1024]{1,0:T(8,128)(2,1)S(1)} %copy-done.16, ...), kind=kOutput, calls=%fused_computation.3 | convolution fusion | flops 29106176 | bytes 11585536 | tf_op jit(solution)/shard_map/dot_general | solution.py:17
  77.7 1.6 copy-done.1
  79.3 3.5 %shard_map.136.p0 = f32[24,1024]{1,0:T(8,128)S(1)} custom-call(f32[512,1024]{1,0:T(8,128)S(1)} %copy-done.1, bf16[1024,1024]{1,0:T(8,128)(2,1)S(1)} %bitcast.44, bf16[32,1024]{1,0:T(8,128)(2,1)S(1)} %copy-done.3, s32[1,1024]{1,0:T(1,128)S(1)} %convert_element_type.148.code, f32[2,1024]{1,0:T(2,128)S(1)} %pad_maximum_fusion.2.squares, f32[1,1024]{1,0:T(1,128)S(1)} %bitcast.48), custom_call_target="tpu_custom_call" | custom-call | tf_op jit(solution)/shard_map/pallas_call | solution.py:225
  82.7 1.7 collective-permute-start.10
  84.4 1.6 collective-permute-start.11
  86.9 2.9 %collective-permute-done.10.p2 = f32[24,1024]{1,0:T(8,128)S(1)} collective-permute-done((f32[24,1024]{1,0:T(8,128)S(1)}, f32[24,1024]{1,0:T(8,128)S(1)}, u32[]{:S(2)}, u32[]{:S(2)}) %collective-permute-start.10) | collective-permute-done | bytes 98336 | tf_op jit(solution)/shard_map/ppermute | solution.py:236
  89.8 2.1 collective-permute-done.9.p1
  92.6 2.2 %shard_map.137 = (f32[8,1024]{1,0:T(8,128)S(1)}, f32[32,768]{1,0:T(8,128)S(1)}, f32[16,128]{1,0:T(8,128)S(1)}, f32[32,512]{1,0:T(8,128)}) custom-call(f32[24,1024]{1,0:T(8,128)S(1)} %shard_map.136.p0, f32[24,1024]{1,0:T(8,128)} %collective-permute-done.9.p1, f32[24,1024]{1,0:T(8,128)S(1)} %collective-permute-done.10.p2, ...), custom_call_target="tpu_custom_call" | custom-call | tf_op jit(solution)/shard_map/pallas_call | solution.py:225
  97.1 0.8 concatenate.33
  98.6 7.5 %all-to-all-start.2 = ((f32[32,1,1088]{2,1,0:T(1,128)}), f32[32,1,1088]{2,1,0:T(1,128)S(1)}, u32[]{:S(2)}, u32[]{:S(2)}) async-start(f32[32,1,1088]{2,1,0:T(1,128)} %all_to_all.34), calls=%async_computation.2 | async-start | bytes 294912 | tf_op jit(solution)/shard_map/all_to_all | solution.py:358
  106.1 1.3 slice_reduce_fusion.1
  107.5 6.4 %all-to-all-done.2 = f32[32,1,1088]{2,1,0:T(1,128)S(1)} async-done(((f32[32,1,1088]{2,1,0:T(1,128)}), f32[32,1,1088]{2,1,0:T(1,128)S(1)}, u32[]{:S(2)}, u32[]{:S(2)}) %all-to-all-start.2) | async-done | bytes 139296 | tf_op jit(solution)/shard_map/all_to_all | solution.py:358
  113.9 1.6 copy-done.2
  115.5 0.9 copy-done.5
  117.1 3.7 %shard_map.138 = (bf16[512,1024]{1,0:T(8,128)(2,1)}, bf16[128,1024]{1,0:T(8,128)(2,1)S(1)}, bf16[128,1024]{1,0:T(8,128)(2,1)S(1)}, bf16[32,128]{1,0:T(8,128)(2,1)S(1)}, f32[32,128]{1,0:T(8,128)S(1)}) custom-call(f32[32,1088]{1,0:T(8,128)S(1)} %bitcast.46, f32[512,1024]{1,0:T(8,128)S(1)} %copy-done.2, bf16[1024,1024]{1,0:T(8,128)(2,1)S(1)} %bitcast.45, ...), custom_call_target="tpu_custom_call" | custom-call | tf_op jit(solution)/shard_map/pallas_call | solution.py:225
  120.8 2.3 %convolution_bitcast_fusion.1 = f32[16,512]{1,0:T(8,128)} fusion(bf16[512,1024]{1,0:T(8,128)(2,1)} %get-tuple-element.11, bf16[16,1024]{1,0:T(8,128)(2,1)S(1)} %copy-done.17), kind=kOutput, calls=%fused_computation.44 | convolution fusion | flops 16777216 | bytes 1114112 | tf_op jit(solution)/shard_map/dot_general | solution.py:17
  123.9 2.5 %collective-permute-start.14 = (f32[16,512]{1,0:T(8,128)}, f32[16,512]{1,0:T(8,128)}, u32[]{:S(2)}, u32[]{:S(2)}) collective-permute-start(f32[16,512]{1,0:T(8,128)} %convolution_bitcast_fusion.1), channel_id=1, source_target_pairs={{0,3},{1,0},{2,1},{3,2},{4,7},{5,4},{6,5},{7,6},{8,11},{9,8},{10,9... | collective-permute-start | bytes 98312 | tf_op jit(solution)/shard_map/ppermute | solution.py:236
  126.3 1.5 convolution_convert_fusion.7
  127.8 2.9 %fusion.20 = bf16[512,1024]{1,0:T(8,128)(2,1)S(1)} fusion(bf16[512,1024]{1,0:T(8,128)(2,1)S(1)} %copy-done.11, bf16[4096,1024]{1,0:T(8,128)(2,1)} %param.11, s32[]{:T(128)S(6)} %select_n.93), kind=kOutput, calls=%fused_computation.26 | convolution fusion | flops 1074266112 | bytes 4194308 | tf_op jit(solution)/shard_map/dot_general | solution.py:17
  130.7 3.1 %fusion.27 = bf16[256,1024]{1,0:T(8,128)(2,1)} fusion(bf16[4096,1024]{1,0:T(8,128)(2,1)} %param.11, s32[]{:T(128)S(6)} %select_n.91, bf16[512,1024]{1,0:T(8,128)(2,1)S(1)} %copy-done.11), kind=kOutput, calls=%fused_computation.35 | convolution fusion | flops 537133056 | bytes 3145732 | tf_op jit(solution)/shard_map/dot_general | solution.py:17
  133.8 3.1 %fusion.24 = bf16[256,1024]{1,0:T(8,128)(2,1)} fusion(bf16[4096,1024]{1,0:T(8,128)(2,1)} %param.11, s32[]{:T(128)S(6)} %select_n.89, bf16[512,1024]{1,0:T(8,128)(2,1)S(1)} %copy-done.11), kind=kOutput, calls=%fused_computation.34 | convolution fusion | flops 537133056 | bytes 3145732 | tf_op jit(solution)/shard_map/dot_general | solution.py:17
  137.0 1.1 fusion.121
  138.1 0.9 collective-permute-start.19
  138.9 1.2 collective-permute-start.15
  140.1 2.1 convolution_convert_fusion.1
  142.2 4.9 %all-to-all-start.3 = ((bf16[32,32,1024]{2,1,0:T(8,128)(2,1)}), bf16[32,32,1024]{2,1,0:T(8,128)(2,1)}, u32[]{:S(2)}, u32[]{:S(2)}) async-start(bf16[32,32,1024]{2,1,0:T(8,128)(2,1)} %bitcast.50), calls=%async_computation.3 | async-start | bytes 4194304 | tf_op jit(solution)/shard_map/all_to_all | solution.py:380
  147.1 0.8 multiply_convert_fusion
  148.5 1.1 collective-permute-done.21
  149.6 3.3 %collective-permute-start.22 = (bf16[32,1024]{1,0:T(8,128)(2,1)S(1)}, bf16[32,1024]{1,0:T(8,128)(2,1)S(1)}, u32[]{:S(2)}, u32[]{:S(2)}) collective-permute-start(bf16[32,1024]{1,0:T(8,128)(2,1)S(1)} %add_convert_fusion.4), channel_id=1, source_target_pairs={{0,64},{4,68},{8,72},{12,76},{16,80},{20,84},{24,88},{28,92},{32,9... | collective-permute-start | bytes 196616 | tf_op jit(solution)/shard_map/ppermute | solution.py:259
  153.5 2.6 %collective-permute-start.24 = (bf16[32,1024]{1,0:T(8,128)(2,1)S(1)}, bf16[32,1024]{1,0:T(8,128)(2,1)S(1)}, u32[]{:S(2)}, u32[]{:S(2)}) collective-permute-start(bf16[32,1024]{1,0:T(8,128)(2,1)S(1)} %add_convert_fusion.4), channel_id=1, source_target_pairs={{0,96},{4,100},{8,104},{12,108},{16,112},{20,116},{24,120},{28,124... | collective-permute-start | bytes 196616 | tf_op jit(solution)/shard_map/ppermute | solution.py:259
  156.7 19.1 %collective-permute-done.22 = bf16[32,1024]{1,0:T(8,128)(2,1)S(1)} collective-permute-done((bf16[32,1024]{1,0:T(8,128)(2,1)S(1)}, bf16[32,1024]{1,0:T(8,128)(2,1)S(1)}, u32[]{:S(2)}, u32[]{:S(2)}) %collective-permute-start.22) | collective-permute-done | bytes 65568 | tf_op jit(solution)/shard_map/ppermute | solution.py:259
  176.4 2.7 %collective-permute-start.18 = (bf16[256,1024]{1,0:T(8,128)(2,1)}, bf16[256,1024]{1,0:T(8,128)(2,1)S(1)}, u32[]{:S(2)}, u32[]{:S(2)}) collective-permute-start(bf16[256,1024]{1,0:T(8,128)(2,1)} %fusion.24), channel_id=1, source_target_pairs={{0,3},{1,0},{2,1},{3,2},{4,7},{5,4},{6,5},{7,6},{8,11},{9,8},{10,9... | collective-permute-start | bytes 1572872 | tf_op jit(solution)/shard_map/ppermute | solution.py:236
  179.1 3.0 %collective-permute-start.25 = (bf16[32,1024]{1,0:T(8,128)(2,1)S(1)}, bf16[32,1024]{1,0:T(8,128)(2,1)S(1)}, u32[]{:S(2)}, u32[]{:S(2)}) collective-permute-start(bf16[32,1024]{1,0:T(8,128)(2,1)S(1)} %add_convert_fusion.3), channel_id=1, source_target_pairs={{0,16},{4,20},{8,24},{12,28},{16,0},{20,4},{24,8},{28,12},{32,48},... | collective-permute-start | bytes 196616 | tf_op jit(solution)/shard_map/ppermute | solution.py:259
  182.8 2.4 %add_convert_fusion.1 = bf16[256,1024]{1,0:T(8,128)(2,1)S(1)} fusion(bf16[256,1024]{1,0:T(8,128)(2,1)} %collective-permute-done.19, bf16[4096,1024]{1,0:T(8,128)(2,1)} %param.11, s32[]{:T(128)S(6)} %select_n.89, bf16[512,1024]{1,0:T(8,128)(2,1)S(1)} %copy-done.11), kind=kOutput, calls=%fused_computation.55 | convolution fusion | flops 537657344 | bytes 3670020 | tf_op jit(solution)/shard_map/dot_general | solution.py:17
  185.2 2.9 %collective-permute-start.27 = (bf16[32,1024]{1,0:T(8,128)(2,1)S(1)}, bf16[32,1024]{1,0:T(8,128)(2,1)S(1)}, u32[]{:S(2)}, u32[]{:S(2)}) collective-permute-start(bf16[32,1024]{1,0:T(8,128)(2,1)S(1)} %add_convert_fusion.3), channel_id=1, source_target_pairs={{0,24},{4,28},{8,0},{12,4},{16,8},{20,12},{24,16},{28,20},{32,56},... | collective-permute-start | bytes 196616 | tf_op jit(solution)/shard_map/ppermute | solution.py:259
  188.1 2.4 %add_convert_fusion.2 = bf16[256,1024]{1,0:T(8,128)(2,1)S(1)} fusion(bf16[256,1024]{1,0:T(8,128)(2,1)} %collective-permute-done.15, bf16[4096,1024]{1,0:T(8,128)(2,1)} %param.11, s32[]{:T(128)S(6)} %select_n.91, bf16[512,1024]{1,0:T(8,128)(2,1)S(1)} %copy-done.11), kind=kOutput, calls=%fused_computation.56 | convolution fusion | flops 537657344 | bytes 3670020 | tf_op jit(solution)/shard_map/dot_general | solution.py:17
  190.5 0.9 collective-permute-start.20
  191.4 1.2 collective-permute-start.16
  192.6 1.2 fusion.82
  194.5 8.0 %collective-permute-done.20 = bf16[256,1024]{1,0:T(8,128)(2,1)S(1)} collective-permute-done((bf16[256,1024]{1,0:T(8,128)(2,1)S(1)}, bf16[256,1024]{1,0:T(8,128)(2,1)S(1)}, u32[]{:S(2)}, u32[]{:S(2)}) %collective-permute-start.20) | collective-permute-done | bytes 524320 | tf_op jit(solution)/shard_map/ppermute | solution.py:236
  202.6 1.7 collective-permute-done.16
  204.3 4.0 %add_convert_fusion = bf16[512,1024]{1,0:T(8,128)(2,1)} fusion(f32[512,1024]{1,0:T(8,128)S(1)} %fusion.82, bf16[256,1024]{1,0:T(8,128)(2,1)S(1)} %collective-permute-done.17, bf16[256,1024]{1,0:T(8,128)(2,1)S(1)} %collective-permute-done.16, bf16[256,1024]{1,0:T(8,128)(2,1)S(1)} %collective-permute-done.20, ...), kind=kOutput, calls=%fused_computation.2 | convolution fusion | flops 1080033280 | bytes 8388612 | tf_op jit(solution)/shard_map/dot_general | solution.py:17
  208.3 2.1 %convolution_bitcast_fusion = f32[32,1024]{1,0:T(8,128)S(1)} fusion(bf16[32,32,1024]{2,1,0:T(8,128)(2,1)} %all-to-all-done.3, s32[32,32]{1,0:T(8,128)S(1)} %copy-done.15, pred[32,32]{1,0:T(8,128)(4,1)S(1)} %copy-done.19), kind=kOutput, calls=%fused_computation.36 | convolution fusion | flops 67174400 | bytes 2233344 | tf_op jit(solution)/shard_map/dot_general | solution.py:17
  210.4 0.8 fusion.31
  (118 shorter events, 12.9 us)
Async XLA Ops:
  0.6 29.5 %copy-start = (bf16[512,1024]{1,0:T(8,128)(2,1)S(1)}, bf16[512,1024]{1,0:T(8,128)(2,1)}, u32[]{:S(2)}) copy-start(bf16[512,1024]{1,0:T(8,128)(2,1)} %param.10) | copy-start | bytes 3145732
  0.6 6.5 %copy-start.9 = (bf16[512,1024]{1,0:T(8,128)(2,1)S(1)}, bf16[512,1024]{1,0:T(8,128)(2,1)}, u32[]{:S(2)}) copy-start(bf16[512,1024]{1,0:T(8,128)(2,1)} %param.9) | copy-start | bytes 3145732
  0.7 12.8 %copy-start.20 = (s32[32,17]{0,1:T(8,128)S(1)}, s32[32,17]{0,1:T(8,128)}, u32[]{:S(2)}) copy-start(s32[32,17]{0,1:T(8,128)} %param.16) | copy-start | bytes 6532
  0.7 14.3 %copy-start.3 = (bf16[32,1024]{1,0:T(8,128)(2,1)S(1)}, bf16[32,1024]{1,0:T(8,128)(2,1)}, u32[]{:S(2)}) copy-start(bf16[32,1024]{1,0:T(8,128)(2,1)} %qown.3) | copy-start | bytes 196612
  3.1 43.7 %collective-permute-start.5 = (bf16[256,1024]{1,0:T(8,128)(2,1)}, bf16[256,1024]{1,0:T(8,128)(2,1)}, u32[]{:S(2)}, u32[]{:S(2)}) collective-permute-start(bf16[256,1024]{1,0:T(8,128)(2,1)} %get-tuple-element.26), channel_id=1, source_target_pairs={{0,3},{1,0},{2,1},{3,2},{4,7},{5,4},{6,5},{7,6},{8,11},{9,8},{10,9... | collective-permute-start | bytes 1572872 | tf_op jit(solution)/shard_map/ppermute | solution.py:236
  7.2 36.3 %collective-permute-start.3 = (bf16[256,1024]{1,0:T(8,128)(2,1)}, bf16[256,1024]{1,0:T(8,128)(2,1)}, u32[]{:S(2)}, u32[]{:S(2)}) collective-permute-start(bf16[256,1024]{1,0:T(8,128)(2,1)} %get-tuple-element.26), channel_id=1, source_target_pairs={{0,1},{1,2},{2,3},{3,0},{4,5},{5,6},{6,7},{7,4},{8,9},{9,10},{10,1... | collective-permute-start | bytes 1572872 | tf_op jit(solution)/shard_map/ppermute | solution.py:236
  8.3 31.1 %collective-permute-start = (f32[16,512]{1,0:T(8,128)S(1)}, f32[16,512]{1,0:T(8,128)S(1)}, u32[]{:S(2)}, u32[]{:S(2)}) collective-permute-start(f32[16,512]{1,0:T(8,128)S(1)} %fusion.84), channel_id=1, source_target_pairs={{0,2},{1,3},{2,0},{3,1},{4,6},{5,7},{6,4},{7,5},{8,10},{9,11},{10,... | collective-permute-start | bytes 98312 | tf_op jit(solution)/shard_map/ppermute | solution.py:236
  10.2 29.6 %collective-permute-start.1 = (f32[16,512]{1,0:T(8,128)S(1)}, f32[16,512]{1,0:T(8,128)S(1)}, u32[]{:S(2)}, u32[]{:S(2)}) collective-permute-start(f32[16,512]{1,0:T(8,128)S(1)} %fusion.84), channel_id=1, source_target_pairs={{0,1},{1,2},{2,3},{3,0},{4,5},{5,6},{6,7},{7,4},{8,9},{9,10},{10,1... | collective-permute-start | bytes 98312 | tf_op jit(solution)/shard_map/ppermute | solution.py:236
  12.4 32.1 %collective-permute-start.6 = (bf16[256,1024]{1,0:T(8,128)(2,1)}, bf16[256,1024]{1,0:T(8,128)(2,1)}, u32[]{:S(2)}, u32[]{:S(2)}) collective-permute-start(bf16[256,1024]{1,0:T(8,128)(2,1)} %get-tuple-element.27), channel_id=1, source_target_pairs={{0,3},{1,0},{2,1},{3,2},{4,7},{5,4},{6,5},{7,6},{8,11},{9,8},{10,9... | collective-permute-start | bytes 1572872 | tf_op jit(solution)/shard_map/ppermute | solution.py:236
  14.7 15.4 %copy-start.14 = (s32[32,32]{1,0:T(8,128)}, s32[32,32]{1,0:T(8,128)S(1)}, u32[]{:S(2)}) copy-start(s32[32,32]{1,0:T(8,128)S(1)} %get-tuple-element.36) | copy-start | bytes 12292
  14.8 15.4 %copy-start.18 = (pred[32,32]{1,0:T(8,128)(4,1)}, pred[32,32]{1,0:T(8,128)(4,1)S(1)}, u32[]{:S(2)}) copy-start(pred[32,32]{1,0:T(8,128)(4,1)S(1)} %broadcast_compare_fusion) | copy-start | bytes 3076
  15.9 16.0 %all-to-all-start.1 = ((f32[32,1,64]{2,1,0:T(1,128)}), f32[32,1,64]{2,1,0:T(1,128)S(1)}, u32[]{:S(2)}, u32[]{:S(2)}) async-start(f32[32,1,64]{2,1,0:T(1,128)} %bitcast.3), calls=%async_computation.1 | async-start | bytes 32768 | tf_op jit(solution)/shard_map/all_to_all | solution.py:315
  30.1 1.7 copy-start.21
  31.9 45.8 %all-to-all-start = ((bf16[32,32,1024]{2,1,0:T(8,128)(2,1)}), bf16[32,32,1024]{2,1,0:T(8,128)(2,1)S(1)}, u32[]{:S(2)}, u32[]{:S(2)}) async-start(bf16[32,32,1024]{2,1,0:T(8,128)(2,1)} %bitcast.51), calls=%async_computation | async-start | bytes 4194304 | tf_op jit(solution)/shard_map/all_to_all | solution.py:322
  39.5 4.0 %collective-permute-start.2 = (f32[16,512]{1,0:T(8,128)S(1)}, f32[16,512]{1,0:T(8,128)S(1)}, u32[]{:S(2)}, u32[]{:S(2)}) collective-permute-start(f32[16,512]{1,0:T(8,128)S(1)} %fusion.84), channel_id=1, source_target_pairs={{0,3},{1,0},{2,1},{3,2},{4,7},{5,4},{6,5},{7,6},{8,11},{9,8},{10,9... | collective-permute-start | bytes 98312 | tf_op jit(solution)/shard_map/ppermute | solution.py:236
  39.8 16.4 %collective-permute-start.4 = (bf16[256,1024]{1,0:T(8,128)(2,1)}, bf16[256,1024]{1,0:T(8,128)(2,1)}, u32[]{:S(2)}, u32[]{:S(2)}) collective-permute-start(bf16[256,1024]{1,0:T(8,128)(2,1)} %get-tuple-element.27), channel_id=1, source_target_pairs={{0,1},{1,2},{2,3},{3,0},{4,5},{5,6},{6,7},{7,4},{8,9},{9,10},{10,1... | collective-permute-start | bytes 1572872 | tf_op jit(solution)/shard_map/ppermute | solution.py:236
  43.4 28.2 %copy-start.12 = (bf16[16,512]{1,0:T(8,128)(2,1)}, bf16[16,512]{1,0:T(8,128)(2,1)S(1)}, u32[]{:S(2)}) copy-start(bf16[16,512]{1,0:T(8,128)(2,1)S(1)} %add_convert_fusion.5) | copy-start | bytes 49156
  43.5 23.1 %collective-permute-start.7 = (bf16[256,1024]{1,0:T(8,128)(2,1)}, bf16[256,1024]{1,0:T(8,128)(2,1)}, u32[]{:S(2)}, u32[]{:S(2)}) collective-permute-start(bf16[256,1024]{1,0:T(8,128)(2,1)} %collective-permute-done.3), channel_id=1, source_target_pairs={{0,1},{1,2},{2,3},{3,0},{4,5},{5,6},{6,7},{7,4},{8,9},{9,10},{10,1... | collective-permute-start | bytes 1572872 | tf_op jit(solution)/shard_map/ppermute | solution.py:236
  44.5 22.0 %collective-permute-start.8 = (bf16[256,1024]{1,0:T(8,128)(2,1)}, bf16[256,1024]{1,0:T(8,128)(2,1)}, u32[]{:S(2)}, u32[]{:S(2)}) collective-permute-start(bf16[256,1024]{1,0:T(8,128)(2,1)} %collective-permute-done.6), channel_id=1, source_target_pairs={{0,3},{1,0},{2,1},{3,2},{4,7},{5,4},{6,5},{7,6},{8,11},{9,8},{10,9... | collective-permute-start | bytes 1572872 | tf_op jit(solution)/shard_map/ppermute | solution.py:236
  61.3 10.3 %copy-start.16 = (bf16[16,1024]{1,0:T(8,128)(2,1)S(1)}, bf16[16,1024]{1,0:T(8,128)(2,1)}, u32[]{:S(2)}) copy-start(bf16[16,1024]{1,0:T(8,128)(2,1)} %param.13) | copy-start | bytes 98308
  77.7 1.6 copy-start.1
  79.3 7.1 %copy-start.23 = (s32[128]{0:T(128)S(1)}, s32[128]{0:T(128)}, u32[]{:S(2)}) copy-start(s32[128]{0:T(128)} %param.17) | copy-start | bytes 1540
  82.7 7.1 %collective-permute-start.10 = (f32[24,1024]{1,0:T(8,128)S(1)}, f32[24,1024]{1,0:T(8,128)S(1)}, u32[]{:S(2)}, u32[]{:S(2)}) collective-permute-start(f32[24,1024]{1,0:T(8,128)S(1)} %shard_map.136.p0), channel_id=1, source_target_pairs={{0,2},{1,3},{2,0},{3,1},{4,6},{5,7},{6,4},{7,5},{8,10},{9,11},{10,... | collective-permute-start | bytes 294920 | tf_op jit(solution)/shard_map/ppermute | solution.py:236
  84.4 5.4 %collective-permute-start.11 = (f32[24,1024]{1,0:T(8,128)S(1)}, f32[24,1024]{1,0:T(8,128)S(1)}, u32[]{:S(2)}, u32[]{:S(2)}) collective-permute-start(f32[24,1024]{1,0:T(8,128)S(1)} %shard_map.136.p0), channel_id=1, source_target_pairs={{0,3},{1,0},{2,1},{3,2},{4,7},{5,4},{6,5},{7,6},{8,11},{9,8},{10,9... | collective-permute-start | bytes 294920 | tf_op jit(solution)/shard_map/ppermute | solution.py:236
  86.0 5.9 %collective-permute-start.9 = (f32[24,1024]{1,0:T(8,128)S(1)}, f32[24,1024]{1,0:T(8,128)}, u32[]{:S(2)}, u32[]{:S(2)}) collective-permute-start(f32[24,1024]{1,0:T(8,128)S(1)} %shard_map.136.p0), channel_id=1, source_target_pairs={{0,1},{1,2},{2,3},{3,0},{4,5},{5,6},{6,7},{7,4},{8,9},{9,10},{10,1... | collective-permute-start | bytes 294920 | tf_op jit(solution)/shard_map/ppermute | solution.py:236
  91.9 0.7 copy-start.8
  92.6 2.3 %copy-start.6 = (s32[1,128]{1,0:T(1,128)}, s32[1,128]{1,0:T(1,128)S(1)}, u32[]{:S(2)}) copy-start(s32[1,128]{1,0:T(1,128)S(1)} %broadcast_in_dim.54.home) | copy-start | bytes 1540
  94.8 0.6 copy-start.4
  98.6 15.3 %all-to-all-start.2 = ((f32[32,1,1088]{2,1,0:T(1,128)}), f32[32,1,1088]{2,1,0:T(1,128)S(1)}, u32[]{:S(2)}, u32[]{:S(2)}) async-start(f32[32,1,1088]{2,1,0:T(1,128)} %all_to_all.34), calls=%async_computation.2 | async-start | bytes 294912 | tf_op jit(solution)/shard_map/all_to_all | solution.py:358
  113.9 1.6 copy-start.2
  115.5 0.9 copy-start.5
  116.4 0.7 copy-start.7
  117.1 3.7 %copy-start.17 = (bf16[16,1024]{1,0:T(8,128)(2,1)S(1)}, bf16[16,1024]{1,0:T(8,128)(2,1)}, u32[]{:S(2)}) copy-start(bf16[16,1024]{1,0:T(8,128)(2,1)} %param.13) | copy-start | bytes 98308
  117.1 9.3 %copy-start.13 = (bf16[16,512]{1,0:T(8,128)(2,1)S(1)}, bf16[16,512]{1,0:T(8,128)(2,1)}, u32[]{:S(2)}) copy-start(bf16[16,512]{1,0:T(8,128)(2,1)} %copy-done.12) | copy-start | bytes 49156
  120.8 7.0 %copy-start.11 = (bf16[512,1024]{1,0:T(8,128)(2,1)S(1)}, bf16[512,1024]{1,0:T(8,128)(2,1)}, u32[]{:S(2)}) copy-start(bf16[512,1024]{1,0:T(8,128)(2,1)} %get-tuple-element.11) | copy-start | bytes 3145732
  123.1 24.0 %collective-permute-start.12 = (f32[16,512]{1,0:T(8,128)}, f32[16,512]{1,0:T(8,128)}, u32[]{:S(2)}, u32[]{:S(2)}) collective-permute-start(f32[16,512]{1,0:T(8,128)} %convolution_bitcast_fusion.1), channel_id=1, source_target_pairs={{0,2},{1,3},{2,0},{3,1},{4,6},{5,7},{6,4},{7,5},{8,10},{9,11},{10,... | collective-permute-start | bytes 98312 | tf_op jit(solution)/shard_map/ppermute | solution.py:236
  123.1 24.0 %collective-permute-start.13 = (f32[16,512]{1,0:T(8,128)}, f32[16,512]{1,0:T(8,128)}, u32[]{:S(2)}, u32[]{:S(2)}) collective-permute-start(f32[16,512]{1,0:T(8,128)} %convolution_bitcast_fusion.1), channel_id=1, source_target_pairs={{0,1},{1,2},{2,3},{3,0},{4,5},{5,6},{6,7},{7,4},{8,9},{9,10},{10,1... | collective-permute-start | bytes 98312 | tf_op jit(solution)/shard_map/ppermute | solution.py:236
  123.9 23.3 %collective-permute-start.14 = (f32[16,512]{1,0:T(8,128)}, f32[16,512]{1,0:T(8,128)}, u32[]{:S(2)}, u32[]{:S(2)}) collective-permute-start(f32[16,512]{1,0:T(8,128)} %convolution_bitcast_fusion.1), channel_id=1, source_target_pairs={{0,3},{1,0},{2,1},{3,2},{4,7},{5,4},{6,5},{7,6},{8,11},{9,8},{10,9... | collective-permute-start | bytes 98312 | tf_op jit(solution)/shard_map/ppermute | solution.py:236
  138.1 44.0 %collective-permute-start.19 = (bf16[256,1024]{1,0:T(8,128)(2,1)}, bf16[256,1024]{1,0:T(8,128)(2,1)}, u32[]{:S(2)}, u32[]{:S(2)}) collective-permute-start(bf16[256,1024]{1,0:T(8,128)(2,1)} %get-tuple-element.24), channel_id=1, source_target_pairs={{0,3},{1,0},{2,1},{3,2},{4,7},{5,4},{6,5},{7,6},{8,11},{9,8},{10,9... | collective-permute-start | bytes 1572872 | tf_op jit(solution)/shard_map/ppermute | solution.py:236
  138.9 46.2 %collective-permute-start.15 = (bf16[256,1024]{1,0:T(8,128)(2,1)}, bf16[256,1024]{1,0:T(8,128)(2,1)}, u32[]{:S(2)}, u32[]{:S(2)}) collective-permute-start(bf16[256,1024]{1,0:T(8,128)(2,1)} %get-tuple-element.25), channel_id=1, source_target_pairs={{0,1},{1,2},{2,3},{3,0},{4,5},{5,6},{6,7},{7,4},{8,9},{9,10},{10,1... | collective-permute-start | bytes 1572872 | tf_op jit(solution)/shard_map/ppermute | solution.py:236
  142.2 5.8 %copy-start.10 = (bf16[512,1024]{1,0:T(8,128)(2,1)S(1)}, bf16[512,1024]{1,0:T(8,128)(2,1)}, u32[]{:S(2)}) copy-start(bf16[512,1024]{1,0:T(8,128)(2,1)} %param.9) | copy-start | bytes 3145732
  142.2 13.9 %copy-start.22 = (f32[32]{0:T(128)S(1)}, f32[32]{0:T(128)}, u32[]{:S(2)}) copy-start(f32[32]{0:T(128)} %slice_reduce_fusion.1) | copy-start | bytes 388
  142.2 66.1 %all-to-all-start.3 = ((bf16[32,32,1024]{2,1,0:T(8,128)(2,1)}), bf16[32,32,1024]{2,1,0:T(8,128)(2,1)}, u32[]{:S(2)}, u32[]{:S(2)}) async-start(bf16[32,32,1024]{2,1,0:T(8,128)(2,1)} %bitcast.50), calls=%async_computation.3 | async-start | bytes 4194304 | tf_op jit(solution)/shard_map/all_to_all | solution.py:380
  148.2 1.3 collective-permute-start.21
  149.6 26.2 %collective-permute-start.22 = (bf16[32,1024]{1,0:T(8,128)(2,1)S(1)}, bf16[32,1024]{1,0:T(8,128)(2,1)S(1)}, u32[]{:S(2)}, u32[]{:S(2)}) collective-permute-start(bf16[32,1024]{1,0:T(8,128)(2,1)S(1)} %add_convert_fusion.4), channel_id=1, source_target_pairs={{0,64},{4,68},{8,72},{12,76},{16,80},{20,84},{24,88},{28,92},{32,9... | collective-permute-start | bytes 196616 | tf_op jit(solution)/shard_map/ppermute | solution.py:259
  152.9 23.5 %collective-permute-start.23 = (bf16[32,1024]{1,0:T(8,128)(2,1)S(1)}, bf16[32,1024]{1,0:T(8,128)(2,1)S(1)}, u32[]{:S(2)}, u32[]{:S(2)}) collective-permute-start(bf16[32,1024]{1,0:T(8,128)(2,1)S(1)} %add_convert_fusion.4), channel_id=1, source_target_pairs={{0,32},{4,36},{8,40},{12,44},{16,48},{20,52},{24,56},{28,60},{32,6... | collective-permute-start | bytes 196616 | tf_op jit(solution)/shard_map/ppermute | solution.py:259
  153.5 25.6 %collective-permute-start.24 = (bf16[32,1024]{1,0:T(8,128)(2,1)S(1)}, bf16[32,1024]{1,0:T(8,128)(2,1)S(1)}, u32[]{:S(2)}, u32[]{:S(2)}) collective-permute-start(bf16[32,1024]{1,0:T(8,128)(2,1)S(1)} %add_convert_fusion.4), channel_id=1, source_target_pairs={{0,96},{4,100},{8,104},{12,108},{16,112},{20,116},{24,120},{28,124... | collective-permute-start | bytes 196616 | tf_op jit(solution)/shard_map/ppermute | solution.py:259
  175.8 18.7 %collective-permute-start.17 = (bf16[256,1024]{1,0:T(8,128)(2,1)}, bf16[256,1024]{1,0:T(8,128)(2,1)S(1)}, u32[]{:S(2)}, u32[]{:S(2)}) collective-permute-start(bf16[256,1024]{1,0:T(8,128)(2,1)} %fusion.27), channel_id=1, source_target_pairs={{0,1},{1,2},{2,3},{3,0},{4,5},{5,6},{6,7},{7,4},{8,9},{9,10},{10,1... | collective-permute-start | bytes 1572872 | tf_op jit(solution)/shard_map/ppermute | solution.py:236
  176.4 18.1 %collective-permute-start.18 = (bf16[256,1024]{1,0:T(8,128)(2,1)}, bf16[256,1024]{1,0:T(8,128)(2,1)S(1)}, u32[]{:S(2)}, u32[]{:S(2)}) collective-permute-start(bf16[256,1024]{1,0:T(8,128)(2,1)} %fusion.24), channel_id=1, source_target_pairs={{0,3},{1,0},{2,1},{3,2},{4,7},{5,4},{6,5},{7,6},{8,11},{9,8},{10,9... | collective-permute-start | bytes 1572872 | tf_op jit(solution)/shard_map/ppermute | solution.py:236
  179.1 11.4 %collective-permute-start.25 = (bf16[32,1024]{1,0:T(8,128)(2,1)S(1)}, bf16[32,1024]{1,0:T(8,128)(2,1)S(1)}, u32[]{:S(2)}, u32[]{:S(2)}) collective-permute-start(bf16[32,1024]{1,0:T(8,128)(2,1)S(1)} %add_convert_fusion.3), channel_id=1, source_target_pairs={{0,16},{4,20},{8,24},{12,28},{16,0},{20,4},{24,8},{28,12},{32,48},... | collective-permute-start | bytes 196616 | tf_op jit(solution)/shard_map/ppermute | solution.py:259
  182.1 9.3 %collective-permute-start.26 = (bf16[32,1024]{1,0:T(8,128)(2,1)S(1)}, bf16[32,1024]{1,0:T(8,128)(2,1)S(1)}, u32[]{:S(2)}, u32[]{:S(2)}) collective-permute-start(bf16[32,1024]{1,0:T(8,128)(2,1)S(1)} %add_convert_fusion.3), channel_id=1, source_target_pairs={{0,8},{4,12},{8,16},{12,20},{16,24},{20,28},{24,0},{28,4},{32,40},... | collective-permute-start | bytes 196616 | tf_op jit(solution)/shard_map/ppermute | solution.py:259
  185.2 8.6 %collective-permute-start.27 = (bf16[32,1024]{1,0:T(8,128)(2,1)S(1)}, bf16[32,1024]{1,0:T(8,128)(2,1)S(1)}, u32[]{:S(2)}, u32[]{:S(2)}) collective-permute-start(bf16[32,1024]{1,0:T(8,128)(2,1)S(1)} %add_convert_fusion.3), channel_id=1, source_target_pairs={{0,24},{4,28},{8,0},{12,4},{16,8},{20,12},{24,16},{28,20},{32,56},... | collective-permute-start | bytes 196616 | tf_op jit(solution)/shard_map/ppermute | solution.py:259
  190.5 12.1 %collective-permute-start.20 = (bf16[256,1024]{1,0:T(8,128)(2,1)S(1)}, bf16[256,1024]{1,0:T(8,128)(2,1)S(1)}, u32[]{:S(2)}, u32[]{:S(2)}) collective-permute-start(bf16[256,1024]{1,0:T(8,128)(2,1)S(1)} %add_convert_fusion.1), channel_id=1, source_target_pairs={{0,3},{1,0},{2,1},{3,2},{4,7},{5,4},{6,5},{7,6},{8,11},{9,8},{10,9... | collective-permute-start | bytes 1572872 | tf_op jit(solution)/shard_map/ppermute | solution.py:236
  191.4 12.9 %collective-permute-start.16 = (bf16[256,1024]{1,0:T(8,128)(2,1)S(1)}, bf16[256,1024]{1,0:T(8,128)(2,1)S(1)}, u32[]{:S(2)}, u32[]{:S(2)}) collective-permute-start(bf16[256,1024]{1,0:T(8,128)(2,1)S(1)} %add_convert_fusion.2), channel_id=1, source_target_pairs={{0,1},{1,2},{2,3},{3,0},{4,5},{5,6},{6,7},{7,4},{8,9},{9,10},{10,1... | collective-permute-start | bytes 1572872 | tf_op jit(solution)/shard_map/ppermute | solution.py:236
  194.5 13.8 %copy-start.15 = (s32[32,32]{1,0:T(8,128)S(1)}, s32[32,32]{1,0:T(8,128)}, u32[]{:S(2)}) copy-start(s32[32,32]{1,0:T(8,128)} %copy-done.14) | copy-start | bytes 12292
  194.5 13.8 %copy-start.19 = (pred[32,32]{1,0:T(8,128)(4,1)S(1)}, pred[32,32]{1,0:T(8,128)(4,1)}, u32[]{:S(2)}) copy-start(pred[32,32]{1,0:T(8,128)(4,1)} %copy-done.18) | copy-start | bytes 3076

commit v2 on v1

v2 whole, which is shorter than its diff:
```python
import jax
import jax.numpy as jnp
from jax import lax
from jax.experimental import pallas as pl
from jax.experimental.pallas import tpu as pltpu
from jax.sharding import PartitionSpec as P

F32 = jnp.float32
BF16 = jnp.bfloat16
INV_TEMPER = 1.0 / 0.02
LOSS_SCALE = 1024.0
SLOTS = 32
HARD = 17
PAIRS = [(a, b) for a in range(4) for b in range(a, 4)]


def dot(a, b, dims):
    return lax.dot_general(a, b, ((dims[0], dims[1]), ((), ())), preferred_element_type=F32)


def split3(x):
    a = x.astype(BF16).astype(F32)
    b = (x - a).astype(BF16).astype(F32)
    return [a, b, x - a - b]


def iota(shape, dim):
    return lax.broadcasted_iota(jnp.int32, shape, dim)


def stack_rows(rows, height):
    where = iota((height, rows[0].shape[1]), 0)
    total = jnp.zeros((height, rows[0].shape[1]), F32)
    for place, row in enumerate(rows):
        total = jnp.where(where == place, row, total)
    return total


def step_of(offset):
    return lax.rem(lax.axis_index("mp") + offset, 4)


class Fetch:
    def __init__(self, weight, buffer, sems, offset):
        base = step_of(offset) * 1024
        self.buffer = buffer
        self.copies = [
            pltpu.make_async_copy(
                weight.at[pl.ds(pl.multiple_of(base + k * 256, 256), 256), :],
                buffer.at[pl.ds(k * 256, 256), :],
                sems.at[k],
            )
            for k in range(4)
        ]
        for copy in self.copies:
            copy.start()

    def wait(self, k):
        self.copies[k].wait()


def move(source, target, sems, part):
    rows = pl.ds(part * 128, 128)
    copy = pltpu.make_async_copy(source.at[rows, :], target.at[rows, :], sems.at[part])
    copy.start()
    return copy


def down_rows(down, offset):
    return down[:, pl.ds(pl.multiple_of(step_of(offset) * 1024, 1024), 1024)]


def forward_dot(blocks, fetch, first):
    out = list(first)
    for k in range(4):
        fetch.wait(k)
        part = fetch.buffer[k * 256 : k * 256 + 256, :]
        for i, block in enumerate(blocks):
            out[i] = out[i] + dot(block[:, k * 256 : k * 256 + 256], part, ((1,), (0,)))
    return out


def order_kernel(tokens, top, low):
    for i, out in enumerate((top, low)):
        row = iota((256, 512), 0) + i * 256
        order = ((row & 127) * 4 + (row >> 7) == iota((256, 512), 1)).astype(F32).astype(BF16)
        out[...] = dot(order, tokens[...], ((1,), (0,))).astype(BF16)


def slot_kernel(ids_row, ids_col, queries, out, home):
    ids = ids_row[...]
    owner = iota((32, 640), 0)
    owned = (ids >> 7) == owner
    before = (iota((640, 640), 0) < iota((640, 640), 1)).astype(F32).astype(BF16)
    rank = dot(owned.astype(F32).astype(BF16), before, ((1,), (0,)))
    slot = jnp.sum(jnp.where(owned, rank + (owner * SLOTS).astype(F32), 0.0), axis=0, keepdims=True)
    slot = jnp.where(ids < 0, -1.0, slot).astype(jnp.int32)
    listed = (iota((1024, 640), 0) == slot).astype(F32).astype(BF16)
    entry, lane = iota((640, 128), 0), iota((640, 128), 1)
    query = (entry * 241) >> 12
    values = jnp.where(lane < 32, (query == lane).astype(F32), 0.0)
    values = jnp.where(lane == 32, (ids_col[...] & 127).astype(F32), values)
    values = jnp.where((lane == 33) & (query * HARD == entry), 1.0, values)
    values = jnp.where(lane == 34, 1.0, values)
    picked = dot(listed, values.astype(BF16), ((1,), (0,)))
    q = queries[...].astype(F32)
    squares = jnp.sum(q * q, axis=1, keepdims=True)
    square_row = jnp.sum(
        jnp.where(iota((32, 128), 0) == iota((32, 128), 1), squares, 0.0), axis=0, keepdims=True
    )
    lane = iota((1024, 128), 1)
    mine = jnp.where(lane < 32, picked, 0.0)
    square = jnp.sum(mine * square_row, axis=1, keepdims=True)
    for i, part in enumerate(split3(square)):
        picked = jnp.where(lane == 35 + i, part, picked)
    home[...] = picked.T[0:40, :]
    padded = jnp.concatenate([queries[...], jnp.zeros((96, 1024), BF16)], axis=0)
    out[:, 0:1024] = dot(mine.astype(BF16), padded, ((1,), (0,))).astype(BF16)
    out[:, 1024:1152] = picked.astype(BF16)


def meta_kernel(qslot, meta, turned):
    turned[...] = qslot[:, 0:1024].astype(F32).T.astype(BF16)
    table = qslot[:, 1024:1152].astype(F32).T
    meta[0:40, :] = table[0:40, :]
    meta[35:36, :] = table[35:36, :] + table[36:37, :] + table[37:38, :]


def own_kernel(top, low, residual, weight, down, stream, middle, buffer, sems):
    fetch = Fetch(weight, buffer, sems, 0)
    first = []
    for i in range(2):
        row = iota((256, 512), 0) + i * 256
        order = ((row & 127) * 4 + (row >> 7) == iota((256, 512), 1)).astype(F32).astype(BF16)
        first.append(dot(order, residual[...], ((1,), (0,))))
    d = down_rows(down, 0)
    middle[:, 0:256] = dot(d, top[...], ((1,), (1,)))
    middle[:, 256:512] = dot(d, low[...], ((1,), (1,)))
    out = forward_dot([top, low], fetch, first)
    stream[0:256, :] = out[0]
    stream[256:512, :] = out[1]


def sides_kernel(
    left_top, left_low, right_top, right_low, before, middle_before, weight, down,
    stream, middle, buffer, buffer2, sems, sems2,
):
    fetch = Fetch(weight, buffer, sems, 3)
    fetch2 = Fetch(weight, buffer2, sems2, 1)
    d, d2 = down_rows(down, 3), down_rows(down, 1)
    middle[:, 0:256] = (
        middle_before[:, 0:256]
        + dot(d, left_top[...], ((1,), (1,)))
        + dot(d2, right_top[...], ((1,), (1,)))
    )
    middle[:, 256:512] = (
        middle_before[:, 256:512]
        + dot(d, left_low[...], ((1,), (1,)))
        + dot(d2, right_low[...], ((1,), (1,)))
    )
    out = forward_dot([left_top, left_low], fetch, [before[0:256, :], before[256:512, :]])
    out = forward_dot([right_top, right_low], fetch2, out)
    stream[0:256, :] = out[0]
    stream[256:512, :] = out[1]


def listed_onehot(meta):
    return (iota((128, 1024), 0).astype(F32) == meta[32:33, :]) & (meta[34:35, :] > 0.0)


def partial_kernel(
    far_top, far_low, before, middle_before, weight, down, up, turned, qown, meta, gain,
    pack, stream_out, middle, buffer, sems, tokens, stream, out_sems,
):
    fetch = Fetch(weight, buffer, sems, 2)
    d = down_rows(down, 2)
    mid = [
        (middle_before[:, i * 256 : i * 256 + 256] + dot(d, far[...], ((1,), (1,)))).astype(BF16)
        for i, far in enumerate((far_top, far_low))
    ]
    out = [
        before[i * 256 : i * 256 + 256, :] + 2.0 * dot(mid[i], up[...], ((0,), (0,)))
        for i in range(2)
    ]
    middle[:, 0:256] = mid[0]
    middle[:, 256:512] = mid[1]
    out = forward_dot([far_top, far_low], fetch, out)
    onehot = listed_onehot(meta)
    g = gain[...]
    columns = []
    scaled = []
    sent = []
    for s in range(4):
        x = out[s // 2][(s % 2) * 128 : (s % 2) * 128 + 128]
        stream[s * 128 : s * 128 + 128, :] = x
        sent.append(move(stream, stream_out, out_sems, s))
        u = x * g
        scaled.append(u)
        columns.append(jnp.sum(x * x, axis=1, keepdims=True))
        tokens[s * 128 : s * 128 + 128, :] = u.astype(BF16)
    batch = dot(qown[...], tokens[...], ((1,), (1,)))
    pack[0:16, 0:512] = batch[0:16]
    pack[0:16, 512:1024] = batch[16:32]
    for j in range(4):
        lanes = slice(j * 256, j * 256 + 256)
        scores = dot(tokens[...], turned[:, lanes], ((1,), (0,)))
        for s in range(4):
            pack[16 + s : 17 + s, lanes] = jnp.sum(
                jnp.where(onehot[:, lanes], scores[s * 128 : s * 128 + 128], 0.0),
                axis=0,
                keepdims=True,
            )
    for a, b in PAIRS:
        columns.append(jnp.sum(scaled[a] * scaled[b], axis=1, keepdims=True))
    lane = iota((128, 128), 1)
    table = jnp.zeros((128, 128), F32)
    for place, column in enumerate(columns):
        table = jnp.where(lane == place, column, table)
    table = table.T
    pack[20:21, :] = meta[35:36, :]
    pack[21:23, :] = jnp.zeros((2, 1024), F32)
    for place in range(len(columns)):
        row, off = 21 + place // 8, (place % 8) * 128
        pack[row : row + 1, off : off + 128] = table[place : place + 1, :]
    q = qown[...].astype(F32)
    squares = jnp.sum(q * q, axis=1, keepdims=True)
    pack[23:24, 0:128] = jnp.sum(
        jnp.where(iota((32, 128), 0) == iota((32, 128), 1), squares, 0.0), axis=0, keepdims=True
    )
    pack[23:24, 128:1024] = jnp.zeros((1, 896), F32)
    for copy in sent:
        copy.wait()


def score_kernel(p0, p1, p2, p3, meta, lens, slot, batch, stats, sums):
    def total(rows, lanes):
        return (p0[rows, lanes] + p2[rows, lanes]) + (p1[rows, lanes] + p3[rows, lanes])

    def stat(place):
        row, off = 21 + place // 8, (place % 8) * 128
        return total(slice(row, row + 1), slice(off, off + 128))

    every = slice(0, 1024)
    used = meta[34:35, :] > 0.0
    length = lens[...].astype(F32)
    inv = [lax.rsqrt(stat(s) / 4096.0 + 1e-05) for s in range(4)]
    a = [jnp.where(s < length, inv[s] / length, 0.0) for s in range(4)]
    gram = {pair: stat(4 + i) for i, pair in enumerate(PAIRS)}
    toward = [
        sum(a[t] * gram[(min(s, t), max(s, t))] for t in range(4)) for s in range(4)
    ]
    square = sum(a[s] * toward[s] for s in range(4))
    pinv = lax.rsqrt(square + 1e-06)
    rows = []
    for row in a + [pinv]:
        rows += split3(row)
    onehot = jnp.where(listed_onehot(meta), 1.0, 0.0).astype(BF16)
    picked = dot(stack_rows(rows, 16).astype(BF16), onehot, ((1,), (0,)))
    pick = [
        picked[3 * i : 3 * i + 1] + picked[3 * i + 1 : 3 * i + 2] + picked[3 * i + 2 : 3 * i + 3]
        for i in range(5)
    ]
    dots = [total(slice(16 + s, 17 + s), every) for s in range(4)]
    product = pick[0] * dots[0] + pick[1] * dots[1] + pick[2] * dots[2] + pick[3] * dots[3]
    qinv = lax.rsqrt(total(slice(20, 21), every) + 1e-06)
    pre = qinv * pick[4] * INV_TEMPER
    score = product * pre
    grown = jnp.where(used, jnp.exp(score), 0.0)
    slot[0:1, :] = score
    slot[1:2, :] = pre
    for s in range(4):
        slot[2 + s : 3 + s, :] = dots[s]
    slot[6:8, :] = jnp.zeros((2, 1024), F32)

    own = total(slice(23, 24), slice(0, 128))
    lane = iota((32, 128), 1)
    qcol = lax.rsqrt(
        jnp.sum(jnp.where(lane == iota((32, 128), 0), own, 0.0), axis=1, keepdims=True) + 1e-06
    )
    pieces = []
    for s in range(4):
        top = total(slice(0, 16), slice(s * 128, s * 128 + 128))
        low = total(slice(0, 16), slice(512 + s * 128, 640 + s * 128))
        pieces.append(jnp.concatenate([top, low], axis=0))
        batch[:, 256 + s * 128 : 384 + s * 128] = pieces[s]
    bpre = qcol * pinv * INV_TEMPER
    bscore = sum(a[s] * pieces[s] for s in range(4)) * bpre
    bgrown = jnp.exp(bscore)
    batch[:, 0:128] = bscore
    batch[:, 128:256] = bpre
    batch[:, 768:896] = jnp.broadcast_to(qcol, (32, 128))

    stats[...] = stack_rows(a + inv + toward + [pinv], 16)

    mine = meta[0:32, :]
    block = ((iota((1024, 128), 0) >> 5) == iota((1024, 128), 1)).astype(F32).astype(BF16)

    def by_query(row):
        out = jnp.zeros((32, 128), F32)
        for part in split3(row):
            out += dot((mine * part).astype(BF16), block, ((1,), (0,)))
        return out

    at_home = lane == lax.axis_index("dp")
    exp_sum = by_query(grown) + jnp.where(at_home, jnp.sum(bgrown, axis=1, keepdims=True), 0.0)
    place = ((iota((128, 1024), 1) & 31) == iota((128, 1024), 0)).astype(F32).astype(BF16)
    wide = jnp.zeros((32, 1024), F32)
    for part in split3(exp_sum):
        wide += dot(part.astype(BF16), place, ((1,), (0,)))
    spread = iota((32, 1024), 0) == (iota((32, 1024), 1) >> 5)
    exp_row = jnp.sum(jnp.where(spread, wide, 0.0), axis=0, keepdims=True)
    for b in range(32):
        group = slice(b // 4 * 128, b // 4 * 128 + 128)
        sums[b, :, 0:1024] = exp_row
        sums[b, :, 1024:1152] = score[:, group]
        sums[b, :, 1152:1280] = pre[:, group]


def pooled_kernel(stream_in, stats, gain, qslot, pooled, rows, stream, sems):
    for copy in [move(stream_in, stream, sems, s) for s in range(4)]:
        copy.wait()
    cols = jnp.concatenate([stats[...], jnp.zeros((112, 128), F32)], axis=0).T
    g = gain[...]
    mean = sum(cols[:, s : s + 1] * (stream[s * 128 : s * 128 + 128, :] * g) for s in range(4))
    pooled[...] = mean.astype(BF16)
    meta = qslot[:, 1024:1152].astype(F32)
    lane = iota((1024, 128), 1).astype(F32)
    listed = ((meta[:, 32:33] == lane) & (meta[:, 34:35] > 0.0)).astype(F32).astype(BF16)
    rows[...] = dot(listed, pooled[...], ((1,), (0,))).astype(BF16)


def gradient_kernel(
    recv, stream_in, qslot, qown, gain, meta, slot, batch, stats, pooled, up, middle, weight,
    grad_out, far_top, far_low, lora, extras_out, up_part,
    buffer, sems, stream, in_sems, grad, out_sems, extras, extras_sem, ordered,
):
    arriving = [move(stream_in, stream, in_sems, s) for s in range(4)]
    fetch = Fetch(weight, buffer, sems, 2)
    total = recv[0, :, 0:1024]
    for b in range(1, 32):
        total = total + recv[b, :, 0:1024]
    log_row = jnp.log(total)
    spread = iota((32, 1024), 0) == (iota((32, 1024), 1) >> 5)
    place = ((iota((1024, 128), 0) & 31) == iota((1024, 128), 1)).astype(F32).astype(BF16)
    table = jnp.zeros((32, 128), F32)
    for part in split3(log_row):
        table += dot(jnp.where(spread, part, 0.0).astype(BF16), place, ((1,), (0,)))
    block = (iota((128, 1024), 0) == (iota((128, 1024), 1) >> 5)).astype(F32).astype(BF16)
    wide = jnp.zeros((32, 1024), F32)
    for part in split3(table):
        wide += dot(part.astype(BF16), block, ((1,), (0,)))
    log_slot = jnp.sum(meta[0:32, :] * wide, axis=0, keepdims=True)
    lane = iota((32, 128), 1)
    log_col = jnp.sum(
        jnp.where(lane == lax.axis_index("dp"), table, 0.0), axis=1, keepdims=True
    )
    extras[:, 0:128] = jnp.broadcast_to(log_col, (32, 128))
    used, first = meta[34:35, :] > 0.0, meta[33:34, :]
    score = slot[0:1, :]
    coef = jnp.where(used, LOSS_SCALE * (jnp.exp(score - log_slot) - first), 0.0)
    value = (coef * slot[1:2, :]).astype(BF16).astype(F32)
    bscore = batch[:, 0:128]
    bcoef = LOSS_SCALE * jnp.exp(bscore - log_col)
    bweight = (bcoef * batch[:, 128:256]).astype(BF16).astype(F32)
    extras[:, 128:256] = bweight
    extras[:, 256:384] = bcoef * bscore
    extras_copy = pltpu.make_async_copy(extras, extras_out, extras_sem.at[0])
    extras_copy.start()
    onehot = listed_onehot(meta)
    spread_weight = jnp.where(onehot, value, 0.0)
    wb = spread_weight.astype(BF16)
    scalar = jnp.sum(jnp.where(onehot, coef * score, 0.0), axis=1, keepdims=True)

    rows = [jnp.sum(bcoef * bscore, axis=0, keepdims=True)]
    for s in range(4):
        rows.append(
            jnp.sum(bweight * batch[:, 256 + s * 128 : 384 + s * 128], axis=0, keepdims=True)
        )
    rows += [stats[i : i + 1, :] for i in range(13)]
    cols = stack_rows(rows, 128).T

    def col(i):
        return cols[:, i : i + 1]

    pinv = col(17)
    scale = (scalar + col(0)) * pinv * pinv
    g = gain[...]
    gp = dot(wb, qslot[:, 0:1024], ((1,), (0,)))
    bt = jnp.concatenate([bweight, jnp.zeros((96, 128), F32)], axis=0).T.astype(BF16)
    qpad = jnp.concatenate([qown[...], jnp.zeros((96, 1024), BF16)], axis=0)
    gp = gp + dot(bt, qpad, ((1,), (0,))) - scale * pooled[...].astype(F32)
    gg = gp * g
    leaving = [extras_copy]
    for s in range(4):
        arriving[s].wait()
        x = stream[s * 128 : s * 128 + 128, :]
        a, inv = col(5 + s), col(9 + s)
        inner = (
            jnp.sum(spread_weight * slot[2 + s : 3 + s, :], axis=1, keepdims=True)
            + col(1 + s)
            - scale * col(13 + s)
        )
        beta = inv * inv * a * inner / 4096.0
        ordered[s * 128 : s * 128 + 128, :] = (a * gg - beta * x).astype(BF16)
    token = iota((512, 512), 0)
    order = ((token & 3) * 128 + (token >> 2) == iota((512, 512), 1)).astype(F32).astype(BF16)
    grad[...] = dot(order, ordered[...], ((1,), (0,))).astype(BF16)
    leaving += [move(grad, grad_out, out_sems, s) for s in range(4)]
    lora[...] = dot(up[...], grad[...], ((1,), (1,)))
    up_part[...] = dot(middle[...], ordered[...], ((1,), (0,)))
    for k in range(4):
        fetch.wait(k)
        for i, out in enumerate((far_top, far_low)):
            out[:, k * 256 : k * 256 + 256] = dot(
                grad[i * 256 : i * 256 + 256, :], buffer[k * 256 : k * 256 + 256, :], ((1,), (1,))
            ).astype(BF16)
    for copy in leaving:
        copy.wait()


def sides_back_kernel(
    grad_in, weight,
    right_low, left_top, right_top, left_low,
    buffer, buffer2, sems, sems2, grad, in_sems,
):
    arriving = [move(grad_in, grad, in_sems, s) for s in range(4)]
    fetch = Fetch(weight, buffer, sems, 1)
    fetch2 = Fetch(weight, buffer2, sems2, 3)
    for copy in arriving:
        copy.wait()
    for fetched, low, top in ((fetch, right_low, right_top), (fetch2, left_low, left_top)):
        for k in range(4):
            fetched.wait(k)
            part = fetched.buffer[k * 256 : k * 256 + 256, :]
            columns = slice(k * 256, k * 256 + 256)
            top[:, columns] = dot(grad[0:256, :], part, ((1,), (1,))).astype(top.dtype)
            low[:, columns] = dot(grad[256:512, :], part, ((1,), (1,))).astype(low.dtype)


def join_kernel(l0, l1, l2, l3, tokens, up_part, adapter, lora_back):
    lora = (2.0 * ((l0[...] + l2[...]) + (l1[...] + l3[...]))).astype(BF16)
    lora_back[...] = lora
    adapter[0:16, :] = dot(lora, tokens[...], ((1,), (0,))).astype(BF16)
    adapter[16:32, :] = up_part[...].astype(BF16)


def add_kernel(right_top, left_low, via_right, via_left, to_right, to_left):
    to_right[...] = (right_top[...].astype(F32) + via_right[...].astype(F32)).astype(BF16)
    to_left[...] = (left_low[...].astype(F32) + via_left[...].astype(F32)).astype(BF16)


def pair_kernel(a, b, out):
    out[...] = (a[...].astype(F32) + b[...].astype(F32)).astype(BF16)


def four_sum(parts):
    a, b, c, d = [part[...].astype(F32) for part in parts]
    return (a + c) + (b + d)


def four_kernel(a, b, c, d, out):
    out[...] = four_sum((a, b, c, d)).astype(BF16)


def last_kernel(a, b, c, d, down, up):
    total = four_sum((a, b, c, d))
    down[...] = total[0:16]
    up[...] = 2.0 * total[16:32]


def finish_kernel(before, from_left, from_right, out):
    out[0:256, :] = (before[0:256, :] + from_left[...].astype(F32)).astype(BF16)
    out[256:512, :] = (before[256:512, :] + from_right[...].astype(F32)).astype(BF16)


def own_back_kernel(
    grad_in, weight, down, lora_back, from_right, from_left, out, buffer, sems, grad, in_sems
):
    arriving = [move(grad_in, grad, in_sems, s) for s in range(4)]
    fetch = Fetch(weight, buffer, sems, 0)
    local = dot(lora_back[...], down_rows(down, 0), ((0,), (0,)))
    for copy in arriving:
        copy.wait()
    for k in range(4):
        fetch.wait(k)
        lanes = slice(k * 256, k * 256 + 256)
        own = local[:, lanes] + dot(grad[...], buffer[k * 256 : k * 256 + 256, :], ((1,), (1,)))
        out[0:256, lanes] = own[0:256] + from_right[:, lanes].astype(F32)
        out[256:512, lanes] = own[256:512] + from_left[:, lanes].astype(F32)


def query_kernel(
    recv, home, extras, batch, pooled, qown, arrived, gradient, loss
):
    group = lax.rem(lax.axis_index("dp"), 4) * 32
    place = iota((128, 1024), 0) == (iota((128, 1024), 1) & 31) + group
    place = place.astype(F32).astype(BF16)
    spread = iota((32, 1024), 0) == (iota((32, 1024), 1) >> 5)
    sub = iota((32, 128), 0)

    def by_slot(lanes):
        table = jnp.zeros((32, 128), F32)
        for d in range(32):
            table = jnp.where(sub == d, recv[d, :, lanes], table)
        wide = jnp.zeros((32, 1024), F32)
        for part in split3(table):
            wide += dot(part.astype(BF16), place, ((1,), (0,)))
        return jnp.sum(jnp.where(spread, wide, 0.0), axis=0, keepdims=True)

    score, pre = by_slot(slice(1024, 1152)), by_slot(slice(1152, 1280))
    mine, first, used = home[0:32, :], home[33:34, :], home[34:35, :] > 0.0
    log_col = extras[:, 0:1]
    log_slot = jnp.sum(mine * log_col, axis=0, keepdims=True)
    coef = jnp.where(used, LOSS_SCALE * (jnp.exp(score - log_slot) - first), 0.0)
    value = jnp.where(used, coef * pre, 0.0).astype(BF16).astype(F32)
    score = jnp.where(used, score, 0.0)
    positive = jnp.sum(mine * (first * score), axis=1, keepdims=True)
    scalar = jnp.sum(mine * (coef * score), axis=1, keepdims=True)
    scalar = scalar + jnp.sum(extras[:, 256:384], axis=1, keepdims=True)
    eye = iota((32, 128), 0) == iota((32, 128), 1)
    row = jnp.sum(jnp.where(eye, log_col - positive, 0.0), axis=0, keepdims=True)
    loss[...] = row[:, 0:32]
    qinv = batch[:, 768:769]
    total = dot((mine * value).astype(BF16), arrived[...], ((1,), (0,)))
    total = total + dot(extras[:, 128:256].astype(BF16), pooled[...], ((1,), (0,)))
    gradient[...] = (total - (scalar * qinv * qinv) * qown[...].astype(F32)).astype(BF16)


ANY, HOLD, LOAD, STORE = "any", "hold", "load", "store"


def call(kernel, outs, args, scratch=(), limit=16, cost=None):
    in_specs, values, moved = [], [], []
    for place, arg in enumerate(args):
        space = pltpu.VMEM
        if isinstance(arg, tuple):
            arg, mark = arg
            space = pltpu.HBM
            if mark != ANY:
                arg = pltpu.with_memory_space_constraint(arg, pltpu.HBM)
            if mark == LOAD:
                moved.append((place, arg.shape, arg.dtype))
        values.append(arg)
        in_specs.append(pl.BlockSpec(memory_space=space))
    loads = len(moved)
    for place, (shape, dtype, *mark) in enumerate(outs):
        if mark == [STORE]:
            moved.append((len(args) + place, shape, dtype))
    count, extra = len(args) + len(outs), len(moved)

    def whole(*refs):
        refs = list(refs)
        if not extra:
            return kernel(*refs)
        sems = refs.pop()
        buffers = [refs.pop() for _ in range(extra)][::-1]
        copies = []
        for i, (place, _, _) in enumerate(moved):
            ends = (refs[place], buffers[i]) if i < loads else (buffers[i], refs[place])
            copies.append(pltpu.make_async_copy(*ends, sems.at[i]))
            refs[place] = buffers[i]
        for copy in copies[:loads]:
            copy.start()
        for copy in copies[:loads]:
            copy.wait()
        kernel(*refs)
        for copy in copies[loads:]:
            copy.start()
        for copy in copies[loads:]:
            copy.wait()

    scratch = list(scratch)
    if extra:
        scratch += [pltpu.VMEM(shape, dtype) for _, shape, dtype in moved]
        scratch.append(pltpu.SemaphoreType.DMA((extra,)))
    if cost is not None:
        cost = pl.CostEstimate(flops=int(cost * 1.15e9), bytes_accessed=0, transcendentals=0)
    return pl.pallas_call(
        whole,
        cost_estimate=cost,
        name=kernel.__name__,
        out_shape=[
            (pltpu.HBM if mark else jax.ShapeDtypeStruct)(s, t) for s, t, *mark in outs
        ],
        in_specs=in_specs,
        out_specs=[
            pl.BlockSpec(memory_space=pltpu.HBM if mark else pltpu.VMEM) for _, _, *mark in outs
        ],
        scratch_shapes=scratch,
        compiler_params=pltpu.CompilerParams(vmem_limit_bytes=limit * 2**20),
    )(*values)


COST_OWN = 20.0
COST_PAIR = 3.0
COST_JOIN = 16.0
COST_GRAD = 1.0
COST_SIDES = 1.0
WEIGHT_BUFFER = pltpu.VMEM((1024, 1024), BF16)
FOUR = pltpu.SemaphoreType.DMA((4,))


def ring(x, step):
    return lax.ppermute(x, "mp", [(i, (i + step) % 4) for i in range(4)])


def ring_sum(x):
    return (x + ring(x, 2)) + (ring(x, 1) + ring(x, 3))


def grid_index(x, y, core):
    return (x * 4 + y) * 2 + core


def grid_shift(v, axis, step):
    pairs = []
    for x in range(4):
        for y in range(4):
            for core in range(2):
                if axis == "core":
                    to = (x, y, 1 - core)
                elif axis == "x":
                    to = ((x + step) % 4, y, core)
                else:
                    to = (x, (y + step) % 4, core)
                pairs.append((grid_index(x, y, core), grid_index(*to)))
    return lax.ppermute(v, "dp", pairs)


def grid_sum(x, own, query):
    shape = x.shape
    tie = lax.optimization_barrier
    (x,) = call(pair_kernel, [(shape, BF16)], [x, grid_shift(x, "core", 1)], cost=COST_PAIR)
    parts = [x] + [grid_shift(x, "x", step) for step in (1, 2, 3)]
    own, *parts = tie((own, *parts))
    (x,) = call(four_kernel, [(shape, BF16)], parts)
    parts = [x] + [grid_shift(x, "y", step) for step in (1, 2, 3)]
    query, own, *parts = tie((query, own, *parts))
    down, up = call(last_kernel, [((16, 1024), F32), ((16, 1024), F32)], parts)
    return down, up, own, query


def body(
    attention_output,
    residual,
    output_projection_weight,
    adapter_down_matrix,
    adapter_up_matrix,
    final_norm_gain,
    query_hidden_states,
    pair_passage_index,
    lengths,
):
    weight = (output_projection_weight, HOLD)
    down = adapter_down_matrix.T
    up = adapter_up_matrix
    qown = query_hidden_states
    half, full = (256, 1024), (512, 1024)
    tie = lax.optimization_barrier

    top, low = call(
        order_kernel, [(half, BF16), (half, BF16)], [(attention_output, LOAD)]
    )
    with jax.named_scope("leg1"):
        left_top, right_low = ring(top, 1), ring(low, 3)

    ids, _, _ = tie((pair_passage_index, top, low))
    flat = jnp.pad(ids.reshape(-1), (0, 640 - 544), constant_values=-1)
    qslot_out, home = call(
        slot_kernel,
        [((1024, 1152), BF16, STORE), ((40, 1024), F32, STORE)],
        [flat.reshape(1, 640), flat.reshape(640, 1), qown],
    )
    with jax.named_scope("a2a_queries"):
        qslot = lax.all_to_all(qslot_out, "dp", 0, 0, tiled=True)
    with jax.named_scope("leg2"):
        left_low, right_top = ring(low, 1), ring(top, 3)
    with jax.named_scope("leg3"):
        far_top, far_low = ring(left_top, 1), ring(right_low, 3)

    residual_tied, left_top, right_low = tie((residual, left_top, right_low))
    stream, middle = call(
        own_kernel,
        [(full, F32), ((16, 512), F32)],
        [top, low, residual_tied, weight, down],
        [WEIGHT_BUFFER, FOUR], limit=24, cost=COST_OWN,
    )
    stream, middle = call(
        sides_kernel,
        [(full, F32), ((16, 512), F32)],
        [left_top, left_low, right_top, right_low, stream, middle, weight, down],
        [WEIGHT_BUFFER, WEIGHT_BUFFER, FOUR, FOUR], limit=24,
    )
    gain = final_norm_gain.astype(F32).reshape(1, 1024)
    meta, turned = call(
        meta_kernel,
        [((40, 1024), F32), ((1024, 1024), BF16)],
        [qslot],
    )
    pack, stream, middle = call(
        partial_kernel,
        [((24, 1024), F32), (full, F32, ANY), ((16, 512), BF16)],
        [far_top, far_low, stream, middle, weight, down, up, turned, qown, meta, gain],
        [WEIGHT_BUFFER, FOUR, pltpu.VMEM((512, 1024), BF16), pltpu.VMEM(full, F32), FOUR], limit=24,
    )
    with jax.named_scope("packs"):
        packs = [pack, ring(pack, 1), ring(pack, 2), ring(pack, 3)]
    slot, batch, stats, sums = call(
        score_kernel,
        [((8, 1024), F32), ((32, 896), F32), ((16, 128), F32), ((32, 1, 1280), F32)],
        [*packs, meta, lengths.reshape(1, 128)],
    )
    with jax.named_scope("a2a_sums"):
        recv = lax.all_to_all(sums, "dp", 0, 0, tiled=True)
    pooled, rows = call(
        pooled_kernel,
        [((128, 1024), BF16), ((1024, 1024), BF16)],
        [(stream, ANY), stats, gain, qslot],
        [pltpu.VMEM(full, F32), FOUR],
    )
    grad, far_top, far_low, lora, extras, up_part = call(
        gradient_kernel,
        [
            (full, BF16, ANY), (half, BF16), (half, BF16), ((16, 512), F32),
            ((32, 384), F32, ANY), ((16, 1024), F32),
        ],
        [recv, (stream, ANY), qslot, qown, gain, meta, slot, batch, stats, pooled, up, middle, weight],
        [
            WEIGHT_BUFFER, FOUR, pltpu.VMEM(full, F32), FOUR, pltpu.VMEM(full, BF16), FOUR,
            pltpu.VMEM((32, 384), F32), pltpu.SemaphoreType.DMA((1,)), pltpu.VMEM(full, BF16),
        ],
        limit=24, cost=COST_GRAD,
    )

    far_top, far_low, rows = tie((far_top, far_low, rows))
    with jax.named_scope("back1"):
        via_right, via_left = ring(far_top, 1), ring(far_low, 3)
    with jax.named_scope("lora_sum"):
        loras = [lora, ring(lora, 1), ring(lora, 2), ring(lora, 3)]
    with jax.named_scope("a2a_rows"):
        arrived = lax.all_to_all(rows, "dp", 0, 0, tiled=True)
    right_low, left_top, right_top, left_low = call(
        sides_back_kernel,
        [(half, BF16), (half, BF16), (half, BF16), (half, BF16)],
        [(grad, ANY), weight],
        [WEIGHT_BUFFER, WEIGHT_BUFFER, FOUR, FOUR, pltpu.VMEM(full, BF16), FOUR],
        limit=24,
        cost=COST_SIDES,
    )
    with jax.named_scope("back2"):
        to_right_low, to_left_top = ring(right_low, 1), ring(left_top, 3)
    right_top, left_low = call(
        add_kernel,
        [(half, BF16), (half, BF16)],
        [right_top, left_low, via_right, via_left],
    )
    right_top, left_low, up_part = tie((right_top, left_low, up_part))
    adapter, lora_back = call(
        join_kernel,
        [((32, 1024), BF16), ((16, 512), BF16)],
        [*loras, (attention_output, LOAD), up_part],
        cost=COST_JOIN,
    )
    with jax.named_scope("back3"):
        to_right_top, to_left_low = ring(right_top, 1), ring(left_low, 3)
    (before,) = call(
        own_back_kernel,
        [(full, F32)],
        [(grad, ANY), weight, down, lora_back, to_left_top, to_right_low],
        [WEIGHT_BUFFER, FOUR, pltpu.VMEM(full, BF16), FOUR],
        limit=24,
    )
    query_gradient, loss = call(
        query_kernel,
        [((32, 1024), BF16), ((1, 32), F32)],
        [
            (recv, LOAD), (home, LOAD), (extras, LOAD), (batch, LOAD), (pooled, LOAD),
            (qown, LOAD), arrived,
        ],
    )
    with jax.named_scope("adapters"):
        down_grad, up_grad, before, query_gradient = grid_sum(adapter, before, query_gradient)
    (attention_gradient,) = call(
        finish_kernel,
        [(full, BF16)],
        [before, to_right_top, to_left_low],
    )
    return (
        loss.reshape(32),
        query_gradient,
        grad,
        attention_gradient,
        down_grad.T,
        up_grad,
    )


def solution(mesh):
    in_specs = (
        P("dp", "mp"),
        P("dp", "mp"),
        P(None, "mp"),
        P(),
        P(None, "mp"),
        P("mp"),
        P("dp", "mp"),
        P("dp", None),
        P("dp"),
    )
    out_specs = (P("dp"), P("dp", "mp"), P("dp", "mp"), P("dp", "mp"), P("mp", None), P(None, "mp"))
    return jax.shard_map(body, mesh=mesh, in_specs=in_specs, out_specs=out_specs, check_vma=False)
```

time: 213 us -> 144 us (0.68)
  matrix products: 59.6 us -> 0 us
  Pallas kernels: 9.41 us -> 50.7 us
  waiting for transfers between devices: 53 us -> 29.8 us
  starting transfers between devices: 68.9 us -> 51.5 us
  local copies, waits for them, and re-layouts: 15 us -> 9.93 us
  other arithmetic: 4.37 us -> 0.01 us
    dot_general x22 -> x0, matrix products: 59.6 us -> none  [dot(): lax.dot_general(a, b, ((dims[0], dims[1]), ((), ())), preferred_element_t...]
    pallas_call x3 -> x18, Pallas kernels: 9.41 us -> 50.7 us  [call(): pl.pallas_call(whole, cost_estimate=cost, name=kernel.__name__, out_shape...]
    ppermute x7, waiting for transfers between devices: 20.5 us -> 1.8 us  [grid_shift(): return lax.ppermute(v, 'dp', pairs)]
    all_to_all x2 -> x1, starting transfers between devices: 14.8 us -> 4.08 us  [body(): recv = lax.all_to_all(sums, 'dp', 0, 0, tiled=True)]
    ppermute x21 -> x18, waiting for transfers between devices: 26 us -> 17.4 us  [ring(): return lax.ppermute(x, 'mp', [(i, (i + step) % 4) for i in range(4)])]
    all_to_all x1, waiting for transfers between devices: 0.01 us -> 6.86 us  [body(): qslot = lax.all_to_all(qslot_out, 'dp', 0, 0, tiled=True)]
    slice x4 -> x0, local copies, waits for them, and re-layouts: 4.93 us -> none  [the longest x1 2.39 us: body(): top, low = (attention_output[:half], attention_output[half:])]
    ppermute x21 -> x18, starting transfers between devices: 28.6 us -> 23.7 us  [ring(): return lax.ppermute(x, 'mp', [(i, (i + step) % 4) for i in range(4)])]
  transfers between devices with their start and end apart: 32 -> 28, of which waited for: 11 -> 12; matrix products, arithmetic and copies ran while one was open for 29% -> 1% of each run, Pallas kernels for 0% -> 22%
where the time goes in v2:
time: 144 us; the launch traced here: 143 us
  starting transfers between devices  51.5 us (36%)
  Pallas kernels  50.7 us (35%)
  waiting for transfers between devices  29.8 us (21%)
  local copies, waits for them, and re-layouts  9.93 us (7%)
    pallas_call x18, Pallas kernels, call(): pl.pallas_call(whole, cost_estimate=cost, name=kernel.__name__, out_shape...  50.7 us
    ppermute x18, starting transfers between devices, ring(): return lax.ppermute(x, 'mp', [(i, (i + step) % 4) for i in range(4)])  23.7 us
    ppermute x18, waiting for transfers between devices, ring(): return lax.ppermute(x, 'mp', [(i, (i + step) % 4) for i in range(4)])  17.4 us
    ppermute x7, starting transfers between devices, grid_shift(): return lax.ppermute(v, 'dp', pairs)  11.4 us
    unnamed x36, local copies, waits for them, and re-layouts  8.9 us
    all_to_all x1, starting transfers between devices, body(): qslot = lax.all_to_all(qslot_out, 'dp', 0, 0, tiled=True)  7.47 us
    all_to_all x1, waiting for transfers between devices, body(): qslot = lax.all_to_all(qslot_out, 'dp', 0, 0, tiled=True)  6.86 us
    all_to_all x1, starting transfers between devices, body(): arrived = lax.all_to_all(rows, 'dp', 0, 0, tiled=True)  4.9 us
  transfers between devices with their start and end apart: 28, of which 12 were waited for; matrix products, arithmetic and copies ran while one was open for 1% of the time, Pallas kernels for 22%

profile of v2, /device:TPU:0, one launch (start us, length us, event | category | flops | bytes accessed | tf_op | source)
XLA Modules:
  0.0 143.0 jit_solution(12467207700818730443)
XLA Ops:
  0.6 2.7 %order_kernel.1 = (bf16[256,1024]{1,0:T(8,128)(2,1)}, bf16[256,1024]{1,0:T(8,128)(2,1)}) custom-call(bf16[512,1024]{1,0:T(8,128)(2,1)} %refs_4_.3), custom_call_target="tpu_custom_call" | custom-call | tf_op jit(solution)/shard_map/order_kernel/pallas_call | solution.py:578
  3.4 2.1 %collective-permute-start = (bf16[256,1024]{1,0:T(8,128)(2,1)}, bf16[256,1024]{1,0:T(8,128)(2,1)S(1)}, u32[]{:S(2)}, u32[]{:S(2)}) collective-permute-start(bf16[256,1024]{1,0:T(8,128)(2,1)} %get-tuple-element.64.refs_0_), channel_id=1, source_target_pairs={{0,1},{1,2},{2,3},{3,0},{4,5},{5,6},{6,7},{7,4},{8,9},{9,10},{10,1... | collective-permute-start | bytes 1572872 | tf_op jit(solution)/shard_map/leg1/ppermute | solution.py:604
  5.5 2.2 %collective-permute-start.2 = (bf16[256,1024]{1,0:T(8,128)(2,1)}, bf16[256,1024]{1,0:T(8,128)(2,1)}, u32[]{:S(2)}, u32[]{:S(2)}) collective-permute-start(bf16[256,1024]{1,0:T(8,128)(2,1)} %get-tuple-element.65.refs_1_), channel_id=1, source_target_pairs={{0,3},{1,0},{2,1},{3,2},{4,7},{5,4},{6,5},{7,6},{8,11},{9,8},{10,9... | collective-permute-start | bytes 1572872 | tf_op jit(solution)/shard_map/leg1/ppermute | solution.py:604
  7.7 0.8 copy.15
  8.4 0.1 reshape.36
  8.6 0.1 reshape.45.refs_1_
  8.7 0.8 copy-done.9
  9.6 3.4 %slot_kernel.1 = (bf16[1024,1152]{1,0:T(8,128)(2,1)}, f32[40,1024]{1,0:T(8,128)}) custom-call(s32[1,640]{1,0:T(1,128)S(1)} %reshape.37.refs_0_, s32[640,1]{1,0:T(8,128)S(1)} %reshape.45.refs_1_, bf16[32,1024]{1,0:T(8,128)(2,1)S(1)} %copy-done.9), custom_call_target="tpu_custom_call" | custom-call | tf_op jit(solution)/shard_map/slot_kernel/pallas_call | solution.py:578
  13.0 7.5 %all-to-all-start = ((bf16[32,32,1152]{2,1,0:T(8,128)(2,1)}), bf16[32,32,1152]{2,1,0:T(8,128)(2,1)S(1)}, u32[]{:S(2)}, u32[]{:S(2)}) async-start(bf16[32,32,1152]{2,1,0:T(8,128)(2,1)} %bitcast.21), calls=%async_computation | async-start | bytes 4718592 | tf_op jit(solution)/shard_map/a2a_queries/all_to_all | solution.py:675
  20.5 2.0 %collective-permute-start.5 = (bf16[256,1024]{1,0:T(8,128)(2,1)}, bf16[256,1024]{1,0:T(8,128)(2,1)S(1)}, u32[]{:S(2)}, u32[]{:S(2)}) collective-permute-start(bf16[256,1024]{1,0:T(8,128)(2,1)} %get-tuple-element.64.refs_0_), channel_id=1, source_target_pairs={{0,3},{1,0},{2,1},{3,2},{4,7},{5,4},{6,5},{7,6},{8,11},{9,8},{10,9... | collective-permute-start | bytes 1572872 | tf_op jit(solution)/shard_map/leg2/ppermute | solution.py:604
  22.5 0.1 collective-permute-start.4
  22.6 0.1 collective-permute-start.1
  22.7 3.4 %collective-permute-start.3 = (bf16[256,1024]{1,0:T(8,128)(2,1)}, bf16[256,1024]{1,0:T(8,128)(2,1)}, u32[]{:S(2)}, u32[]{:S(2)}) collective-permute-start(bf16[256,1024]{1,0:T(8,128)(2,1)} %collective-permute-done.2.refs_3_), channel_id=1, source_target_pairs={{0,3},{1,0},{2,1},{3,2},{4,7},{5,4},{6,5},{7,6},{8,11},{9,8},{10,9... | collective-permute-start | bytes 1572872 | tf_op jit(solution)/shard_map/leg3/ppermute | solution.py:604
  26.1 1.2 copy-done.14
  27.3 4.3 %own_kernel.1 = (f32[512,1024]{1,0:T(8,128)S(1)}, f32[16,512]{1,0:T(8,128)S(1)}) custom-call(bf16[256,1024]{1,0:T(8,128)(2,1)} %get-tuple-element.64.refs_0_, bf16[256,1024]{1,0:T(8,128)(2,1)} %get-tuple-element.65.refs_1_, bf16[512,1024]{1,0:T(8,128)(2,1)S(1)} %copy-done.14, bf16[4096,1024]{1,0:T(8,128)(2,1)} %refs_1_.3, bf16[16,4096]{1,0:T(8,128)(2,1)S(1)} %bitcast.13), custom_call_target="tpu_custom_call" | custom-call | flops 23000000512 | tf_op jit(solution)/shard_map/own_kernel/pallas_call | solution.py:578
  31.7 3.8 %collective-permute-done.5.refs_2_ = bf16[256,1024]{1,0:T(8,128)(2,1)S(1)} collective-permute-done((bf16[256,1024]{1,0:T(8,128)(2,1)}, bf16[256,1024]{1,0:T(8,128)(2,1)S(1)}, u32[]{:S(2)}, u32[]{:S(2)}) %collective-permute-start.5) | collective-permute-done | bytes 524320 | tf_op jit(solution)/shard_map/leg2/ppermute | solution.py:604
  35.5 3.2 %collective-permute-done.4.refs_1_ = bf16[256,1024]{1,0:T(8,128)(2,1)S(1)} collective-permute-done((bf16[256,1024]{1,0:T(8,128)(2,1)}, bf16[256,1024]{1,0:T(8,128)(2,1)S(1)}, u32[]{:S(2)}, u32[]{:S(2)}) %collective-permute-start.4) | collective-permute-done | bytes 524320 | tf_op jit(solution)/shard_map/leg2/ppermute | solution.py:604
  38.7 5.3 %sides_kernel.1 = (f32[512,1024]{1,0:T(8,128)S(1)}, f32[16,512]{1,0:T(8,128)S(1)}) custom-call(bf16[256,1024]{1,0:T(8,128)(2,1)S(1)} %collective-permute-done.refs_0_, bf16[256,1024]{1,0:T(8,128)(2,1)S(1)} %collective-permute-done.4.refs_1_, bf16[256,1024]{1,0:T(8,128)(2,1)S(1)} %collective-permute-done.5.refs_2_, ...), custom_call_target="tpu_custom_call" | custom-call | tf_op jit(solution)/shard_map/sides_kernel/pallas_call | solution.py:578
  44.0 1.4 copy-done.4
  45.4 6.9 %all-to-all-done = bf16[32,32,1152]{2,1,0:T(8,128)(2,1)S(1)} async-done(((bf16[32,32,1152]{2,1,0:T(8,128)(2,1)}), bf16[32,32,1152]{2,1,0:T(8,128)(2,1)S(1)}, u32[]{:S(2)}, u32[]{:S(2)}) %all-to-all-start) | async-done | bytes 2359328 | tf_op jit(solution)/shard_map/a2a_queries/all_to_all | solution.py:675
  52.3 0.7 meta_kernel.1
  53.0 0.8 copy-done.5
  53.9 5.7 %partial_kernel.1 = (f32[24,1024]{1,0:T(8,128)S(1)}, f32[512,1024]{1,0:T(8,128)}, bf16[16,512]{1,0:T(8,128)(2,1)S(1)}) custom-call(bf16[256,1024]{1,0:T(8,128)(2,1)} %collective-permute-done.1.refs_0_, bf16[256,1024]{1,0:T(8,128)(2,1)} %collective-permute-done.3.refs_1_, f32[512,1024]{1,0:T(8,128)S(1)} %copy-done.5, ...), custom_call_target="tpu_custom_call" | custom-call | tf_op jit(solution)/shard_map/partial_kernel/pallas_call | solution.py:578
  59.6 2.0 %collective-permute-start.8 = (f32[24,1024]{1,0:T(8,128)S(1)}, f32[24,1024]{1,0:T(8,128)S(1)}, u32[]{:S(2)}, u32[]{:S(2)}) collective-permute-start(f32[24,1024]{1,0:T(8,128)S(1)} %get-tuple-element.77.refs_0_), channel_id=1, source_target_pairs={{0,3},{1,0},{2,1},{3,2},{4,7},{5,4},{6,5},{7,6},{8,11},{9,8},{10,9... | collective-permute-start | bytes 294920 | tf_op jit(solution)/shard_map/packs/ppermute | solution.py:604
  61.6 1.3 collective-permute-start.6
  62.8 2.7 %collective-permute-done.8.refs_3_ = f32[24,1024]{1,0:T(8,128)S(1)} collective-permute-done((f32[24,1024]{1,0:T(8,128)S(1)}, f32[24,1024]{1,0:T(8,128)S(1)}, u32[]{:S(2)}, u32[]{:S(2)}) %collective-permute-start.8) | collective-permute-done | bytes 98336 | tf_op jit(solution)/shard_map/packs/ppermute | solution.py:604
  65.5 2.7 %collective-permute-done.7.refs_2_ = f32[24,1024]{1,0:T(8,128)S(1)} collective-permute-done((f32[24,1024]{1,0:T(8,128)S(1)}, f32[24,1024]{1,0:T(8,128)S(1)}, u32[]{:S(2)}, u32[]{:S(2)}) %collective-permute-start.7) | collective-permute-done | bytes 98336 | tf_op jit(solution)/shard_map/packs/ppermute | solution.py:604
  68.3 0.7 collective-permute-done.6.refs_1_
  68.9 1.4 score_kernel.1
  70.3 4.1 %all-to-all-start.1 = ((f32[32,1,1280]{2,1,0:T(1,128)}), f32[32,1,1280]{2,1,0:T(1,128)S(1)}, u32[]{:S(2)}, u32[]{:S(2)}) async-start(f32[32,1,1280]{2,1,0:T(1,128)} %get-tuple-element.78), calls=%async_computation.1 | async-start | bytes 327680 | tf_op jit(solution)/shard_map/a2a_sums/all_to_all | solution.py:714
  74.4 1.6 %copy-done = f32[512,1024]{1,0:T(8,128)S(1)} copy-done((f32[512,1024]{1,0:T(8,128)S(1)}, f32[512,1024]{1,0:T(8,128)}, u32[]{:S(2)}) %copy-start) | copy-done | bytes 2097176
  76.0 1.2 pooled_kernel.1
  77.2 1.4 copy-done.3
  78.6 3.7 %all-to-all-done.1.refs_0_ = f32[32,1,1280]{2,1,0:T(1,128)S(1)} async-done(((f32[32,1,1280]{2,1,0:T(1,128)}), f32[32,1,1280]{2,1,0:T(1,128)S(1)}, u32[]{:S(2)}, u32[]{:S(2)}) %all-to-all-start.1) | async-done | bytes 163872 | tf_op jit(solution)/shard_map/a2a_sums/all_to_all | solution.py:714
  82.3 1.6 %copy-done.1 = f32[512,1024]{1,0:T(8,128)S(1)} copy-done((f32[512,1024]{1,0:T(8,128)S(1)}, f32[512,1024]{1,0:T(8,128)}, u32[]{:S(2)}) %copy-start.1) | copy-done | bytes 2097176
  84.0 6.6 %gradient_kernel.1 = (bf16[512,1024]{1,0:T(8,128)(2,1)}, bf16[256,1024]{1,0:T(8,128)(2,1)}, bf16[256,1024]{1,0:T(8,128)(2,1)}, f32[16,512]{1,0:T(8,128)S(1)}, f32[32,384]{1,0:T(8,128)}, /*index=5*/f32[16,1024]{1,0:T(8,128)S(1)}) custom-call(f32[32,1,1280]{2,1,0:T(1,128)S(1)} %all-to-all-done.1.refs_0_, f32[512,1024]{1,0:T(8,128)S(1)} %copy-done.1, ...), custom_call_target="tpu_custom_call" | custom-call | flops 1150000000 | tf_op jit(solution)/shard_map/gradient_kernel/pallas_call | solution.py:578
  90.6 0.1 collective-permute-start.12
  90.7 3.2 %collective-permute-start.13 = (bf16[256,1024]{1,0:T(8,128)(2,1)}, bf16[256,1024]{1,0:T(8,128)(2,1)S(1)}, u32[]{:S(2)}, u32[]{:S(2)}) collective-permute-start(bf16[256,1024]{1,0:T(8,128)(2,1)} %get-tuple-element.98), channel_id=1, source_target_pairs={{0,3},{1,0},{2,1},{3,2},{4,7},{5,4},{6,5},{7,6},{8,11},{9,8},{10,9... | collective-permute-start | bytes 1572872 | tf_op jit(solution)/shard_map/back1/ppermute | solution.py:604
  94.0 0.9 collective-permute-start.10
  94.9 1.1 collective-permute-start.9
  96.0 4.9 %all-to-all-start.2 = ((bf16[32,32,1024]{2,1,0:T(8,128)(2,1)}), bf16[32,32,1024]{2,1,0:T(8,128)(2,1)}, u32[]{:S(2)}, u32[]{:S(2)}) async-start(bf16[32,32,1024]{2,1,0:T(8,128)(2,1)} %bitcast.12), calls=%async_computation.2 | async-start | bytes 4194304 | tf_op jit(solution)/shard_map/a2a_rows/all_to_all | solution.py:741
  100.9 5.1 %sides_back_kernel.1 = (bf16[256,1024]{1,0:T(8,128)(2,1)S(1)}, bf16[256,1024]{1,0:T(8,128)(2,1)S(1)}, bf16[256,1024]{1,0:T(8,128)(2,1)S(1)}, bf16[256,1024]{1,0:T(8,128)(2,1)S(1)}) custom-call(bf16[512,1024]{1,0:T(8,128)(2,1)S(1)} %copy-done.2, bf16[4096,1024]{1,0:T(8,128)(2,1)} %refs_1_.3), custom_call_target="tpu_custom_call" | custom-call | flops 1150000000 | tf_op jit(solution)/shard_map/sides_back_kernel/pallas_call | solution.py:578
  106.0 1.2 collective-permute-done.12.refs_2_
  107.2 1.6 %collective-permute-start.14 = (bf16[256,1024]{1,0:T(8,128)(2,1)S(1)}, bf16[256,1024]{1,0:T(8,128)(2,1)S(1)}, u32[]{:S(2)}, u32[]{:S(2)}) collective-permute-start(bf16[256,1024]{1,0:T(8,128)(2,1)S(1)} %get-tuple-element.104), channel_id=1, source_target_pairs={{0,3},{1,0},{2,1},{3,2},{4,7},{5,4},{6,5},{7,6},{8,11},{9,8},{10,9... | collective-permute-start | bytes 1572872 | tf_op jit(solution)/shard_map/back2/ppermute | solution.py:604
  108.8 0.4 collective-permute-start.15
  109.2 1.2 add_kernel.1
  110.3 1.1 collective-permute-start.23
  111.4 2.1 %collective-permute-start.24 = (bf16[256,1024]{1,0:T(8,128)(2,1)}, bf16[256,1024]{1,0:T(8,128)(2,1)}, u32[]{:S(2)}, u32[]{:S(2)}) collective-permute-start(bf16[256,1024]{1,0:T(8,128)(2,1)} %get-tuple-element.115), channel_id=1, source_target_pairs={{0,3},{1,0},{2,1},{3,2},{4,7},{5,4},{6,5},{7,6},{8,11},{9,8},{10,9... | collective-permute-start | bytes 1572872 | tf_op jit(solution)/shard_map/back3/ppermute | solution.py:604
  113.6 1.5 %join_kernel.1 = (bf16[32,1024]{1,0:T(8,128)(2,1)S(1)}, bf16[16,512]{1,0:T(8,128)(2,1)S(1)}) custom-call(f32[16,512]{1,0:T(8,128)S(1)} %get-tuple-element.94.refs_0_, f32[16,512]{1,0:T(8,128)S(1)} %collective-permute-done.9.refs_1_, f32[16,512]{1,0:T(8,128)S(1)} %collective-permute-done.10.refs_2_, f32[16,512]{1,0:T(8,128)S(1)} %collective-permute-done.11.refs_3_, ...), custom_call_target="tpu_custom_call" | custom-call | flops 18400000000 | tf_op jit(solution)/shard_map/join_kernel/pallas_call | solution.py:578
  115.1 0.1 collective-permute-start.16
  115.2 1.2 collective-permute-done.16.refs_1_
  116.4 3.0 %collective-permute-start.19 = (bf16[32,1024]{1,0:T(8,128)(2,1)S(1)}, bf16[32,1024]{1,0:T(8,128)(2,1)S(1)}, u32[]{:S(2)}, u32[]{:S(2)}) collective-permute-start(bf16[32,1024]{1,0:T(8,128)(2,1)S(1)} %pair_kernel.1.refs_0_), channel_id=1, source_target_pairs={{0,96},{4,100},{8,104},{12,108},{16,112},{20,116},{24,120},{28,124... | collective-permute-start | bytes 196616 | tf_op jit(solution)/shard_map/adapters/ppermute | solution.py:627
  119.4 2.6 %collective-permute-done.14.refs_4_ = bf16[256,1024]{1,0:T(8,128)(2,1)S(1)} collective-permute-done((bf16[256,1024]{1,0:T(8,128)(2,1)S(1)}, bf16[256,1024]{1,0:T(8,128)(2,1)S(1)}, u32[]{:S(2)}, u32[]{:S(2)}) %collective-permute-start.14) | collective-permute-done | bytes 524320 | tf_op jit(solution)/shard_map/back2/ppermute | solution.py:604
  122.0 2.2 %collective-permute-start.18 = (bf16[32,1024]{1,0:T(8,128)(2,1)S(1)}, bf16[32,1024]{1,0:T(8,128)(2,1)S(1)}, u32[]{:S(2)}, u32[]{:S(2)}) collective-permute-start(bf16[32,1024]{1,0:T(8,128)(2,1)S(1)} %pair_kernel.1.refs_0_), channel_id=1, source_target_pairs={{0,64},{4,68},{8,72},{12,76},{16,80},{20,84},{24,88},{28,92},{32,9... | collective-permute-start | bytes 196616 | tf_op jit(solution)/shard_map/adapters/ppermute | solution.py:627
  124.2 0.6 collective-permute-done.15.refs_5_
  124.8 1.6 %collective-permute-start.17 = (bf16[32,1024]{1,0:T(8,128)(2,1)S(1)}, bf16[32,1024]{1,0:T(8,128)(2,1)S(1)}, u32[]{:S(2)}, u32[]{:S(2)}) collective-permute-start(bf16[32,1024]{1,0:T(8,128)(2,1)S(1)} %pair_kernel.1.refs_0_), channel_id=1, source_target_pairs={{0,32},{4,36},{8,40},{12,44},{16,48},{20,52},{24,56},{28,60},{32,6... | collective-permute-start | bytes 196616 | tf_op jit(solution)/shard_map/adapters/ppermute | solution.py:627
  126.4 4.1 %own_back_kernel.1.refs_0_ = f32[512,1024]{1,0:T(8,128)S(1)} custom-call(bf16[512,1024]{1,0:T(8,128)(2,1)S(1)} %copy-done.2, bf16[4096,1024]{1,0:T(8,128)(2,1)} %refs_1_.3, bf16[16,4096]{1,0:T(8,128)(2,1)S(1)} %bitcast.16, bf16[16,512]{1,0:T(8,128)(2,1)S(1)} %get-tuple-element.103.refs_3_, bf16[256,1024]{1,0:T(8,128)(2,1)S(1)} %collective-permute-done.14.refs_4_, ...), custom_call_target="tpu_custom_call" | custom-call | tf_op jit(solution)/shard_map/own_back_kernel/pallas_call | solution.py:578
  130.6 2.8 %collective-permute-start.22 = (bf16[32,1024]{1,0:T(8,128)(2,1)S(1)}, bf16[32,1024]{1,0:T(8,128)(2,1)S(1)}, u32[]{:S(2)}, u32[]{:S(2)}) collective-permute-start(bf16[32,1024]{1,0:T(8,128)(2,1)S(1)} %four_kernel.1.refs_0_), channel_id=1, source_target_pairs={{0,24},{4,28},{8,0},{12,4},{16,8},{20,12},{24,16},{28,20},{32,56},... | collective-permute-start | bytes 196616 | tf_op jit(solution)/shard_map/adapters/ppermute | solution.py:627
  133.4 1.1 collective-permute-start.21
  134.5 0.6 collective-permute-start.20
  135.1 4.3 %query_kernel.1 = (bf16[32,1024]{1,0:T(8,128)(2,1)}, f32[1,32]{1,0:T(1,128)}) custom-call(f32[32,1,1280]{2,1,0:T(1,128)} %copy-done.6, f32[40,1024]{1,0:T(8,128)} %get-tuple-element.79.refs_1_, f32[32,384]{1,0:T(8,128)} %get-tuple-element.86.refs_2_, f32[32,896]{1,0:T(8,128)} %copy-done.11, bf16[128,1024]{1,0:T(8,128)(2,1)} %copy-done.8, ...), custom_call_target="tpu_custom_call" | custom-call | tf_op jit(solution)/shard_map/query_kernel/pallas_call | solution.py:578
  139.4 0.6 collective-permute-done.20.refs_1_
  140.0 0.7 last_kernel.1
  140.6 2.3 %finish_kernel.1 = bf16[512,1024]{1,0:T(8,128)(2,1)} custom-call(f32[512,1024]{1,0:T(8,128)S(1)} %own_back_kernel.1.refs_0_, bf16[256,1024]{1,0:T(8,128)(2,1)} %collective-permute-done.23.refs_1_, bf16[256,1024]{1,0:T(8,128)(2,1)} %collective-permute-done.24.refs_2_), custom_call_target="tpu_custom_call" | custom-call | tf_op jit(solution)/shard_map/finish_kernel/pallas_call | solution.py:578
  (52 shorter events, 0.2 us)
Async XLA Ops:
  3.4 19.2 %collective-permute-start = (bf16[256,1024]{1,0:T(8,128)(2,1)}, bf16[256,1024]{1,0:T(8,128)(2,1)S(1)}, u32[]{:S(2)}, u32[]{:S(2)}) collective-permute-start(bf16[256,1024]{1,0:T(8,128)(2,1)} %get-tuple-element.64.refs_0_), channel_id=1, source_target_pairs={{0,1},{1,2},{2,3},{3,0},{4,5},{5,6},{6,7},{7,4},{8,9},{9,10},{10,1... | collective-permute-start | bytes 1572872 | tf_op jit(solution)/shard_map/leg1/ppermute | solution.py:604
  5.5 17.1 %collective-permute-start.2 = (bf16[256,1024]{1,0:T(8,128)(2,1)}, bf16[256,1024]{1,0:T(8,128)(2,1)}, u32[]{:S(2)}, u32[]{:S(2)}) collective-permute-start(bf16[256,1024]{1,0:T(8,128)(2,1)} %get-tuple-element.65.refs_1_), channel_id=1, source_target_pairs={{0,3},{1,0},{2,1},{3,2},{4,7},{5,4},{6,5},{7,6},{8,11},{9,8},{10,9... | collective-permute-start | bytes 1572872 | tf_op jit(solution)/shard_map/leg1/ppermute | solution.py:604
  8.7 0.8 copy-start.9
  13.0 9.6 %copy-start.17 = (bf16[1024]{0:T(1024)(128)(2,1)S(1)}, bf16[1024]{0:T(1024)(128)(2,1)}, u32[]{:S(2)}) copy-start(bf16[1024]{0:T(1024)(128)(2,1)} %param.14) | copy-start | bytes 6148
  13.0 13.1 %copy-start.7 = (bf16[4096,16]{0,1:T(8,128)(2,1)S(1)}, bf16[4096,16]{0,1:T(8,128)(2,1)}, u32[]{:S(2)}) copy-start(bf16[4096,16]{0,1:T(8,128)(2,1)} %param.12) | copy-start | bytes 393220
  13.0 39.3 %all-to-all-start = ((bf16[32,32,1152]{2,1,0:T(8,128)(2,1)}), bf16[32,32,1152]{2,1,0:T(8,128)(2,1)S(1)}, u32[]{:S(2)}, u32[]{:S(2)}) async-start(bf16[32,32,1152]{2,1,0:T(8,128)(2,1)} %bitcast.21), calls=%async_computation | async-start | bytes 4718592 | tf_op jit(solution)/shard_map/a2a_queries/all_to_all | solution.py:675
  20.5 15.0 %collective-permute-start.5 = (bf16[256,1024]{1,0:T(8,128)(2,1)}, bf16[256,1024]{1,0:T(8,128)(2,1)S(1)}, u32[]{:S(2)}, u32[]{:S(2)}) collective-permute-start(bf16[256,1024]{1,0:T(8,128)(2,1)} %get-tuple-element.64.refs_0_), channel_id=1, source_target_pairs={{0,3},{1,0},{2,1},{3,2},{4,7},{5,4},{6,5},{7,6},{8,11},{9,8},{10,9... | collective-permute-start | bytes 1572872 | tf_op jit(solution)/shard_map/leg2/ppermute | solution.py:604
  22.5 16.2 %collective-permute-start.4 = (bf16[256,1024]{1,0:T(8,128)(2,1)}, bf16[256,1024]{1,0:T(8,128)(2,1)S(1)}, u32[]{:S(2)}, u32[]{:S(2)}) collective-permute-start(bf16[256,1024]{1,0:T(8,128)(2,1)} %get-tuple-element.65.refs_1_), channel_id=1, source_target_pairs={{0,1},{1,2},{2,3},{3,0},{4,5},{5,6},{6,7},{7,4},{8,9},{9,10},{10,1... | collective-permute-start | bytes 1572872 | tf_op jit(solution)/shard_map/leg2/ppermute | solution.py:604
  22.6 30.4 %collective-permute-start.1 = (bf16[256,1024]{1,0:T(8,128)(2,1)S(1)}, bf16[256,1024]{1,0:T(8,128)(2,1)}, u32[]{:S(2)}, u32[]{:S(2)}) collective-permute-start(bf16[256,1024]{1,0:T(8,128)(2,1)S(1)} %collective-permute-done.refs_0_), channel_id=1, source_target_pairs={{0,1},{1,2},{2,3},{3,0},{4,5},{5,6},{6,7},{7,4},{8,9},{9,10},{10,1... | collective-permute-start | bytes 1572872 | tf_op jit(solution)/shard_map/leg3/ppermute | solution.py:604
  22.7 30.3 %collective-permute-start.3 = (bf16[256,1024]{1,0:T(8,128)(2,1)}, bf16[256,1024]{1,0:T(8,128)(2,1)}, u32[]{:S(2)}, u32[]{:S(2)}) collective-permute-start(bf16[256,1024]{1,0:T(8,128)(2,1)} %collective-permute-done.2.refs_3_), channel_id=1, source_target_pairs={{0,3},{1,0},{2,1},{3,2},{4,7},{5,4},{6,5},{7,6},{8,11},{9,8},{10,9... | collective-permute-start | bytes 1572872 | tf_op jit(solution)/shard_map/leg3/ppermute | solution.py:604
  26.1 1.2 copy-start.14
  44.0 1.4 copy-start.4
  45.4 7.6 %copy-start.10 = (bf16[32,1024]{1,0:T(8,128)(2,1)S(1)}, bf16[32,1024]{1,0:T(8,128)(2,1)}, u32[]{:S(2)}) copy-start(bf16[32,1024]{1,0:T(8,128)(2,1)} %refs_5_.1) | copy-start | bytes 196612
  45.4 7.6 %copy-start.12 = (bf16[16,1024]{1,0:T(8,128)(2,1)S(1)}, bf16[16,1024]{1,0:T(8,128)(2,1)}, u32[]{:S(2)}) copy-start(bf16[16,1024]{1,0:T(8,128)(2,1)} %refs_10_.1) | copy-start | bytes 98308
  52.3 1.6 %copy-start.5 = (f32[512,1024]{1,0:T(8,128)S(1)}, f32[512,1024]{1,0:T(8,128)}, u32[]{:S(2)}) copy-start(f32[512,1024]{1,0:T(8,128)} %copy-done.4) | copy-start | bytes 6291460
  53.9 15.1 %copy-start.13 = (s32[128]{0:T(128)S(1)}, s32[128]{0:T(128)}, u32[]{:S(2)}) copy-start(s32[128]{0:T(128)} %param.17) | copy-start | bytes 1540
  59.6 6.0 %collective-permute-start.8 = (f32[24,1024]{1,0:T(8,128)S(1)}, f32[24,1024]{1,0:T(8,128)S(1)}, u32[]{:S(2)}, u32[]{:S(2)}) collective-permute-start(f32[24,1024]{1,0:T(8,128)S(1)} %get-tuple-element.77.refs_0_), channel_id=1, source_target_pairs={{0,3},{1,0},{2,1},{3,2},{4,7},{5,4},{6,5},{7,6},{8,11},{9,8},{10,9... | collective-permute-start | bytes 294920 | tf_op jit(solution)/shard_map/packs/ppermute | solution.py:604
  61.6 6.7 %collective-permute-start.7 = (f32[24,1024]{1,0:T(8,128)S(1)}, f32[24,1024]{1,0:T(8,128)S(1)}, u32[]{:S(2)}, u32[]{:S(2)}) collective-permute-start(f32[24,1024]{1,0:T(8,128)S(1)} %get-tuple-element.77.refs_0_), channel_id=1, source_target_pairs={{0,2},{1,3},{2,0},{3,1},{4,6},{5,7},{6,4},{7,5},{8,10},{9,11},{10,... | collective-permute-start | bytes 294920 | tf_op jit(solution)/shard_map/packs/ppermute | solution.py:604
  61.6 7.3 %collective-permute-start.6 = (f32[24,1024]{1,0:T(8,128)S(1)}, f32[24,1024]{1,0:T(8,128)S(1)}, u32[]{:S(2)}, u32[]{:S(2)}) collective-permute-start(f32[24,1024]{1,0:T(8,128)S(1)} %get-tuple-element.77.refs_0_), channel_id=1, source_target_pairs={{0,1},{1,2},{2,3},{3,0},{4,5},{5,6},{6,7},{7,4},{8,9},{9,10},{10,1... | collective-permute-start | bytes 294920 | tf_op jit(solution)/shard_map/packs/ppermute | solution.py:604
  70.3 12.0 %copy-start.11 = (f32[32,896]{1,0:T(8,128)}, f32[32,896]{1,0:T(8,128)S(1)}, u32[]{:S(2)}) copy-start(f32[32,896]{1,0:T(8,128)S(1)} %get-tuple-element.82.refs_7_.refs_3_) | copy-start | bytes 344068
  70.3 12.0 %all-to-all-start.1 = ((f32[32,1,1280]{2,1,0:T(1,128)}), f32[32,1,1280]{2,1,0:T(1,128)S(1)}, u32[]{:S(2)}, u32[]{:S(2)}) async-start(f32[32,1,1280]{2,1,0:T(1,128)} %get-tuple-element.78), calls=%async_computation.1 | async-start | bytes 327680 | tf_op jit(solution)/shard_map/a2a_sums/all_to_all | solution.py:714
  74.4 1.6 %copy-start = (f32[512,1024]{1,0:T(8,128)S(1)}, f32[512,1024]{1,0:T(8,128)}, u32[]{:S(2)}) copy-start(f32[512,1024]{1,0:T(8,128)} %get-tuple-element.80.refs_0_.refs_1_) | copy-start | bytes 6291460
  77.2 1.4 copy-start.3
  78.6 12.0 %copy-start.8 = (bf16[128,1024]{1,0:T(8,128)(2,1)}, bf16[128,1024]{1,0:T(8,128)(2,1)S(1)}, u32[]{:S(2)}) copy-start(bf16[128,1024]{1,0:T(8,128)(2,1)S(1)} %get-tuple-element.84.refs_9_.refs_4_) | copy-start | bytes 786436
  82.3 8.3 %copy-start.6 = (f32[32,1,1280]{2,1,0:T(1,128)}, f32[32,1,1280]{2,1,0:T(1,128)S(1)}, u32[]{:S(2)}) copy-start(f32[32,1,1280]{2,1,0:T(1,128)S(1)} %all-to-all-done.1.refs_0_) | copy-start | bytes 491524
  82.3 1.7 %copy-start.1 = (f32[512,1024]{1,0:T(8,128)S(1)}, f32[512,1024]{1,0:T(8,128)}, u32[]{:S(2)}) copy-start(f32[512,1024]{1,0:T(8,128)} %get-tuple-element.80.refs_0_.refs_1_) | copy-start | bytes 6291460
  90.6 5.4 %copy-start.15 = (f32[16,1024]{1,0:T(8,128)}, f32[16,1024]{1,0:T(8,128)S(1)}, u32[]{:S(2)}) copy-start(f32[16,1024]{1,0:T(8,128)S(1)} %get-tuple-element.102.refs_5_) | copy-start | bytes 196612
  90.6 16.5 %collective-permute-start.12 = (bf16[256,1024]{1,0:T(8,128)(2,1)}, bf16[256,1024]{1,0:T(8,128)(2,1)S(1)}, u32[]{:S(2)}, u32[]{:S(2)}) collective-permute-start(bf16[256,1024]{1,0:T(8,128)(2,1)} %get-tuple-element.97), channel_id=1, source_target_pairs={{0,1},{1,2},{2,3},{3,0},{4,5},{5,6},{6,7},{7,4},{8,9},{9,10},{10,1... | collective-permute-start | bytes 1572872 | tf_op jit(solution)/shard_map/back1/ppermute | solution.py:604
  90.7 18.0 %collective-permute-start.13 = (bf16[256,1024]{1,0:T(8,128)(2,1)}, bf16[256,1024]{1,0:T(8,128)(2,1)S(1)}, u32[]{:S(2)}, u32[]{:S(2)}) collective-permute-start(bf16[256,1024]{1,0:T(8,128)(2,1)} %get-tuple-element.98), channel_id=1, source_target_pairs={{0,3},{1,0},{2,1},{3,2},{4,7},{5,4},{6,5},{7,6},{8,11},{9,8},{10,9... | collective-permute-start | bytes 1572872 | tf_op jit(solution)/shard_map/back1/ppermute | solution.py:604
  94.0 16.4 %collective-permute-start.11 = (f32[16,512]{1,0:T(8,128)S(1)}, f32[16,512]{1,0:T(8,128)S(1)}, u32[]{:S(2)}, u32[]{:S(2)}) collective-permute-start(f32[16,512]{1,0:T(8,128)S(1)} %get-tuple-element.94.refs_0_), channel_id=1, source_target_pairs={{0,3},{1,0},{2,1},{3,2},{4,7},{5,4},{6,5},{7,6},{8,11},{9,8},{10,9... | collective-permute-start | bytes 98312 | tf_op jit(solution)/shard_map/lora_sum/ppermute | solution.py:604
  94.0 17.5 %collective-permute-start.10 = (f32[16,512]{1,0:T(8,128)S(1)}, f32[16,512]{1,0:T(8,128)S(1)}, u32[]{:S(2)}, u32[]{:S(2)}) collective-permute-start(f32[16,512]{1,0:T(8,128)S(1)} %get-tuple-element.94.refs_0_), channel_id=1, source_target_pairs={{0,2},{1,3},{2,0},{3,1},{4,6},{5,7},{6,4},{7,5},{8,10},{9,11},{10,... | collective-permute-start | bytes 98312 | tf_op jit(solution)/shard_map/lora_sum/ppermute | solution.py:604
  94.9 18.7 %collective-permute-start.9 = (f32[16,512]{1,0:T(8,128)S(1)}, f32[16,512]{1,0:T(8,128)S(1)}, u32[]{:S(2)}, u32[]{:S(2)}) collective-permute-start(f32[16,512]{1,0:T(8,128)S(1)} %get-tuple-element.94.refs_0_), channel_id=1, source_target_pairs={{0,1},{1,2},{2,3},{3,0},{4,5},{5,6},{6,7},{7,4},{8,9},{9,10},{10,1... | collective-permute-start | bytes 98312 | tf_op jit(solution)/shard_map/lora_sum/ppermute | solution.py:604
  96.0 4.9 %copy-start.2 = (bf16[512,1024]{1,0:T(8,128)(2,1)S(1)}, bf16[512,1024]{1,0:T(8,128)(2,1)}, u32[]{:S(2)}) copy-start(bf16[512,1024]{1,0:T(8,128)(2,1)} %get-tuple-element.60.refs_0_) | copy-start | bytes 3145732
  96.0 39.1 %all-to-all-start.2 = ((bf16[32,32,1024]{2,1,0:T(8,128)(2,1)}), bf16[32,32,1024]{2,1,0:T(8,128)(2,1)}, u32[]{:S(2)}, u32[]{:S(2)}) async-start(bf16[32,32,1024]{2,1,0:T(8,128)(2,1)} %bitcast.12), calls=%async_computation.2 | async-start | bytes 4194304 | tf_op jit(solution)/shard_map/a2a_rows/all_to_all | solution.py:741
  106.0 7.6 %copy-start.16 = (f32[16,1024]{1,0:T(8,128)S(1)}, f32[16,1024]{1,0:T(8,128)}, u32[]{:S(2)}) copy-start(f32[16,1024]{1,0:T(8,128)} %copy-done.15) | copy-start | bytes 196612
  107.2 14.9 %collective-permute-start.14 = (bf16[256,1024]{1,0:T(8,128)(2,1)S(1)}, bf16[256,1024]{1,0:T(8,128)(2,1)S(1)}, u32[]{:S(2)}, u32[]{:S(2)}) collective-permute-start(bf16[256,1024]{1,0:T(8,128)(2,1)S(1)} %get-tuple-element.104), channel_id=1, source_target_pairs={{0,3},{1,0},{2,1},{3,2},{4,7},{5,4},{6,5},{7,6},{8,11},{9,8},{10,9... | collective-permute-start | bytes 1572872 | tf_op jit(solution)/shard_map/back2/ppermute | solution.py:604
  108.8 16.0 %collective-permute-start.15 = (bf16[256,1024]{1,0:T(8,128)(2,1)S(1)}, bf16[256,1024]{1,0:T(8,128)(2,1)S(1)}, u32[]{:S(2)}, u32[]{:S(2)}) collective-permute-start(bf16[256,1024]{1,0:T(8,128)(2,1)S(1)} %get-tuple-element.105), channel_id=1, source_target_pairs={{0,1},{1,2},{2,3},{3,0},{4,5},{5,6},{6,7},{7,4},{8,9},{9,10},{10,1... | collective-permute-start | bytes 1572872 | tf_op jit(solution)/shard_map/back2/ppermute | solution.py:604
  110.3 30.3 %collective-permute-start.23 = (bf16[256,1024]{1,0:T(8,128)(2,1)}, bf16[256,1024]{1,0:T(8,128)(2,1)}, u32[]{:S(2)}, u32[]{:S(2)}) collective-permute-start(bf16[256,1024]{1,0:T(8,128)(2,1)} %get-tuple-element.114), channel_id=1, source_target_pairs={{0,1},{1,2},{2,3},{3,0},{4,5},{5,6},{6,7},{7,4},{8,9},{9,10},{10,1... | collective-permute-start | bytes 1572872 | tf_op jit(solution)/shard_map/back3/ppermute | solution.py:604
  111.4 29.2 %collective-permute-start.24 = (bf16[256,1024]{1,0:T(8,128)(2,1)}, bf16[256,1024]{1,0:T(8,128)(2,1)}, u32[]{:S(2)}, u32[]{:S(2)}) collective-permute-start(bf16[256,1024]{1,0:T(8,128)(2,1)} %get-tuple-element.115), channel_id=1, source_target_pairs={{0,3},{1,0},{2,1},{3,2},{4,7},{5,4},{6,5},{7,6},{8,11},{9,8},{10,9... | collective-permute-start | bytes 1572872 | tf_op jit(solution)/shard_map/back3/ppermute | solution.py:604
  115.1 1.3 collective-permute-start.16
  116.4 14.1 %collective-permute-start.19 = (bf16[32,1024]{1,0:T(8,128)(2,1)S(1)}, bf16[32,1024]{1,0:T(8,128)(2,1)S(1)}, u32[]{:S(2)}, u32[]{:S(2)}) collective-permute-start(bf16[32,1024]{1,0:T(8,128)(2,1)S(1)} %pair_kernel.1.refs_0_), channel_id=1, source_target_pairs={{0,96},{4,100},{8,104},{12,108},{16,112},{20,116},{24,120},{28,124... | collective-permute-start | bytes 196616 | tf_op jit(solution)/shard_map/adapters/ppermute | solution.py:627
  122.0 8.5 %collective-permute-start.18 = (bf16[32,1024]{1,0:T(8,128)(2,1)S(1)}, bf16[32,1024]{1,0:T(8,128)(2,1)S(1)}, u32[]{:S(2)}, u32[]{:S(2)}) collective-permute-start(bf16[32,1024]{1,0:T(8,128)(2,1)S(1)} %pair_kernel.1.refs_0_), channel_id=1, source_target_pairs={{0,64},{4,68},{8,72},{12,76},{16,80},{20,84},{24,88},{28,92},{32,9... | collective-permute-start | bytes 196616 | tf_op jit(solution)/shard_map/adapters/ppermute | solution.py:627
  124.8 5.8 %collective-permute-start.17 = (bf16[32,1024]{1,0:T(8,128)(2,1)S(1)}, bf16[32,1024]{1,0:T(8,128)(2,1)S(1)}, u32[]{:S(2)}, u32[]{:S(2)}) collective-permute-start(bf16[32,1024]{1,0:T(8,128)(2,1)S(1)} %pair_kernel.1.refs_0_), channel_id=1, source_target_pairs={{0,32},{4,36},{8,40},{12,44},{16,48},{20,52},{24,56},{28,60},{32,6... | collective-permute-start | bytes 196616 | tf_op jit(solution)/shard_map/adapters/ppermute | solution.py:627
  130.6 8.8 %collective-permute-start.22 = (bf16[32,1024]{1,0:T(8,128)(2,1)S(1)}, bf16[32,1024]{1,0:T(8,128)(2,1)S(1)}, u32[]{:S(2)}, u32[]{:S(2)}) collective-permute-start(bf16[32,1024]{1,0:T(8,128)(2,1)S(1)} %four_kernel.1.refs_0_), channel_id=1, source_target_pairs={{0,24},{4,28},{8,0},{12,4},{16,8},{20,12},{24,16},{28,20},{32,56},... | collective-permute-start | bytes 196616 | tf_op jit(solution)/shard_map/adapters/ppermute | solution.py:627
  133.4 6.0 %collective-permute-start.21 = (bf16[32,1024]{1,0:T(8,128)(2,1)S(1)}, bf16[32,1024]{1,0:T(8,128)(2,1)S(1)}, u32[]{:S(2)}, u32[]{:S(2)}) collective-permute-start(bf16[32,1024]{1,0:T(8,128)(2,1)S(1)} %four_kernel.1.refs_0_), channel_id=1, source_target_pairs={{0,16},{4,20},{8,24},{12,28},{16,0},{20,4},{24,8},{28,12},{32,48},... | collective-permute-start | bytes 196616 | tf_op jit(solution)/shard_map/adapters/ppermute | solution.py:627
  134.5 5.5 %collective-permute-start.20 = (bf16[32,1024]{1,0:T(8,128)(2,1)S(1)}, bf16[32,1024]{1,0:T(8,128)(2,1)S(1)}, u32[]{:S(2)}, u32[]{:S(2)}) collective-permute-start(bf16[32,1024]{1,0:T(8,128)(2,1)S(1)} %four_kernel.1.refs_0_), channel_id=1, source_target_pairs={{0,8},{4,12},{8,16},{12,20},{16,24},{20,28},{24,0},{28,4},{32,40},... | collective-permute-start | bytes 196616 | tf_op jit(solution)/shard_map/adapters/ppermute | solution.py:627

commit v3 on v2

--- a/solution.py
+++ b/solution.py
@@ -85,6 +85,42 @@
         row = iota((256, 512), 0) + i * 256
         order = ((row & 127) * 4 + (row >> 7) == iota((256, 512), 1)).astype(F32).astype(BF16)
         out[...] = dot(order, tokens[...], ((1,), (0,))).astype(BF16)
+
+
+def fold_map(shape, slot_dim):
+    part = iota(shape, 1 - slot_dim)
+    return iota(shape, slot_dim) == (part & 31) * 24 + (part >> 5)
+
+
+def fold(pieces, last, out):
+    width = last.shape[1]
+    off = 0
+    for piece in pieces:
+        lanes = slice(off, off + piece.shape[1])
+        for o in range(32):
+            out[o * 24 : o * 24 + 24, lanes] = piece[o * 32 : o * 32 + 24].astype(BF16)
+        off += piece.shape[1]
+    stack = jnp.concatenate([last[:, i : i + 128] for i in range(0, width, 128)], axis=0)
+    table = fold_map((768, stack.shape[0]), 0).astype(F32).astype(BF16)
+    out[:, width : width + 128] = dot(table, stack, ((1,), (0,))).astype(BF16)
+
+
+def unfold(arrived, full):
+    width = full.shape[1]
+    parts = width // 128
+    table = fold_map((parts * 32, 768), 1).astype(F32).astype(BF16)
+    stack = dot(table, arrived[:, width : width + 128], ((1,), (0,))).astype(BF16)
+    last = jnp.concatenate([stack[c * 32 : c * 32 + 32] for c in range(parts)], axis=1)
+    last = jnp.concatenate([last, jnp.zeros((96, width), BF16)], axis=0)
+    place = (iota((256, 128), 0) == iota((256, 128), 1) * 8).astype(F32).astype(BF16)
+    rows = dot(place, last, ((1,), (0,))).astype(BF16)
+    for b in range(32):
+        full[b * 32 : b * 32 + 24, :] = arrived[b * 24 : b * 24 + 24, 0:width]
+        full[b * 32 + 24 : b * 32 + 32, :] = rows[b * 8 : b * 8 + 8]
+
+
+def last_slots():
+    return (iota((32, 1024), 1) == iota((32, 1024), 0) * 32 + 24).astype(F32).astype(BF16)
 
 
 def slot_kernel(ids_row, ids_col, queries, out, home):
@@ -115,11 +151,15 @@
         picked = jnp.where(lane == 35 + i, part, picked)
     home[...] = picked.T[0:40, :]
     padded = jnp.concatenate([queries[...], jnp.zeros((96, 1024), BF16)], axis=0)
-    out[:, 0:1024] = dot(mine.astype(BF16), padded, ((1,), (0,))).astype(BF16)
-    out[:, 1024:1152] = picked.astype(BF16)
-
-
-def meta_kernel(qslot, meta, turned):
+    rows = dot(mine.astype(BF16), padded, ((1,), (0,)))
+    last = dot(last_slots(), mine.astype(BF16), ((1,), (0,))).astype(BF16)
+    last = dot(last, padded, ((1,), (0,))).astype(BF16)
+    last_values = dot(last_slots(), picked.astype(BF16), ((1,), (0,))).astype(BF16)
+    fold([rows, picked], jnp.concatenate([last, last_values], axis=1), out)
+
+
+def meta_kernel(arrived, qslot, meta, turned):
+    unfold(arrived, qslot)
     turned[...] = qslot[:, 0:1024].astype(F32).T.astype(BF16)
     table = qslot[:, 1024:1152].astype(F32).T
     meta[0:40, :] = table[0:40, :]
@@ -168,36 +208,47 @@
     return (iota((128, 1024), 0).astype(F32) == meta[32:33, :]) & (meta[34:35, :] > 0.0)
 
 
-def partial_kernel(
-    far_top, far_low, before, middle_before, weight, down, up, turned, qown, meta, gain,
-    pack, stream_out, middle, buffer, sems, tokens, stream, out_sems,
+def far_kernel(
+    far_top, far_low, before_in, middle_before, weight, down, up, gain,
+    stream_out, middle, tokens, table_out, buffer, sems, stream, out_sems, before, in_sems,
 ):
     fetch = Fetch(weight, buffer, sems, 2)
+    arriving = [move(before_in, before, in_sems, s) for s in range(4)]
     d = down_rows(down, 2)
     mid = [
         (middle_before[:, i * 256 : i * 256 + 256] + dot(d, far[...], ((1,), (1,)))).astype(BF16)
         for i, far in enumerate((far_top, far_low))
     ]
-    out = [
-        before[i * 256 : i * 256 + 256, :] + 2.0 * dot(mid[i], up[...], ((0,), (0,)))
-        for i in range(2)
-    ]
+    out = [2.0 * dot(mid[i], up[...], ((0,), (0,))) for i in range(2)]
     middle[:, 0:256] = mid[0]
     middle[:, 256:512] = mid[1]
     out = forward_dot([far_top, far_low], fetch, out)
-    onehot = listed_onehot(meta)
     g = gain[...]
     columns = []
     scaled = []
     sent = []
     for s in range(4):
-        x = out[s // 2][(s % 2) * 128 : (s % 2) * 128 + 128]
+        arriving[s].wait()
+        x = out[s // 2][(s % 2) * 128 : (s % 2) * 128 + 128] + before[s * 128 : s * 128 + 128, :]
         stream[s * 128 : s * 128 + 128, :] = x
         sent.append(move(stream, stream_out, out_sems, s))
         u = x * g
         scaled.append(u)
         columns.append(jnp.sum(x * x, axis=1, keepdims=True))
         tokens[s * 128 : s * 128 + 128, :] = u.astype(BF16)
+    for a, b in PAIRS:
+        columns.append(jnp.sum(scaled[a] * scaled[b], axis=1, keepdims=True))
+    lane = iota((128, 128), 1)
+    table = jnp.zeros((128, 128), F32)
+    for place, column in enumerate(columns):
+        table = jnp.where(lane == place, column, table)
+    table_out[...] = table.T[0:16]
+    for copy in sent:
+        copy.wait()
+
+
+def partial_kernel(tokens, turned, qown, meta, table, pack):
+    onehot = listed_onehot(meta)
     batch = dot(qown[...], tokens[...], ((1,), (1,)))
     pack[0:16, 0:512] = batch[0:16]
     pack[0:16, 512:1024] = batch[16:32]
@@ -210,16 +261,9 @@
                 axis=0,
                 keepdims=True,
             )
-    for a, b in PAIRS:
-        columns.append(jnp.sum(scaled[a] * scaled[b], axis=1, keepdims=True))
-    lane = iota((128, 128), 1)
-    table = jnp.zeros((128, 128), F32)
-    for place, column in enumerate(columns):
-        table = jnp.where(lane == place, column, table)
-    table = table.T
     pack[20:21, :] = meta[35:36, :]
     pack[21:23, :] = jnp.zeros((2, 1024), F32)
-    for place in range(len(columns)):
+    for place in range(4 + len(PAIRS)):
         row, off = 21 + place // 8, (place % 8) * 128
         pack[row : row + 1, off : off + 128] = table[place : place + 1, :]
     q = qown[...].astype(F32)
@@ -228,8 +272,6 @@
         jnp.where(iota((32, 128), 0) == iota((32, 128), 1), squares, 0.0), axis=0, keepdims=True
     )
     pack[23:24, 128:1024] = jnp.zeros((1, 896), F32)
-    for copy in sent:
-        copy.wait()
 
 
 def score_kernel(p0, p1, p2, p3, meta, lens, slot, batch, stats, sums):
@@ -326,7 +368,9 @@
     meta = qslot[:, 1024:1152].astype(F32)
     lane = iota((1024, 128), 1).astype(F32)
     listed = ((meta[:, 32:33] == lane) & (meta[:, 34:35] > 0.0)).astype(F32).astype(BF16)
-    rows[...] = dot(listed, pooled[...], ((1,), (0,))).astype(BF16)
+    full = dot(listed, pooled[...], ((1,), (0,)))
+    last = dot(last_slots(), listed, ((1,), (0,))).astype(BF16)
+    fold([full], dot(last, pooled[...], ((1,), (0,))).astype(BF16), rows)
 
 
 def gradient_kernel(
@@ -490,7 +534,7 @@
 
 
 def query_kernel(
-    recv, home, extras, batch, pooled, qown, arrived, gradient, loss
+    recv, home, extras, batch, pooled, qown, arrived, gradient, loss, listed
 ):
     group = lax.rem(lax.axis_index("dp"), 4) * 32
     place = iota((128, 1024), 0) == (iota((128, 1024), 1) & 31) + group
@@ -521,7 +565,8 @@
     row = jnp.sum(jnp.where(eye, log_col - positive, 0.0), axis=0, keepdims=True)
     loss[...] = row[:, 0:32]
     qinv = batch[:, 768:769]
-    total = dot((mine * value).astype(BF16), arrived[...], ((1,), (0,)))
+    unfold(arrived, listed)
+    total = dot((mine * value).astype(BF16), listed[...], ((1,), (0,)))
     total = total + dot(extras[:, 128:256].astype(BF16), pooled[...], ((1,), (0,)))
     gradient[...] = (total - (scalar * qinv * qinv) * qown[...].astype(F32)).astype(BF16)
 
@@ -591,10 +636,11 @@
     )(*values)
 
 
-COST_OWN = 20.0
+COST_OWN = 15.0
 COST_PAIR = 3.0
 COST_JOIN = 16.0
 COST_GRAD = 1.0
+COST_FAR = 4.0
 COST_SIDES = 1.0
 WEIGHT_BUFFER = pltpu.VMEM((1024, 1024), BF16)
 FOUR = pltpu.SemaphoreType.DMA((4,))
@@ -668,7 +714,7 @@
     flat = jnp.pad(ids.reshape(-1), (0, 640 - 544), constant_values=-1)
     qslot_out, home = call(
         slot_kernel,
-        [((1024, 1152), BF16, STORE), ((40, 1024), F32, STORE)],
+        [((768, 1280), BF16, STORE), ((40, 1024), F32, STORE)],
         [flat.reshape(1, 640), flat.reshape(640, 1), qown],
     )
     with jax.named_scope("a2a_queries"):
@@ -687,22 +733,26 @@
     )
     stream, middle = call(
         sides_kernel,
-        [(full, F32), ((16, 512), F32)],
+        [(full, F32, STORE), ((16, 512), F32)],
         [left_top, left_low, right_top, right_low, stream, middle, weight, down],
         [WEIGHT_BUFFER, WEIGHT_BUFFER, FOUR, FOUR], limit=24,
     )
     gain = final_norm_gain.astype(F32).reshape(1, 1024)
-    meta, turned = call(
+    stream, middle, tokens, table = call(
+        far_kernel,
+        [(full, F32, ANY), ((16, 512), BF16), (full, BF16), ((16, 128), F32)],
+        [far_top, far_low, (stream, HOLD), middle, weight, down, up, gain],
+        [WEIGHT_BUFFER, FOUR, pltpu.VMEM(full, F32), FOUR, pltpu.VMEM(full, F32), FOUR],
+        limit=24,
+        cost=COST_FAR,
+    )
+    qslot, table = tie((qslot, table))
+    qslot, meta, turned = call(
         meta_kernel,
-        [((40, 1024), F32), ((1024, 1024), BF16)],
-        [qslot],
-    )
-    pack, stream, middle = call(
-        partial_kernel,
-        [((24, 1024), F32), (full, F32, ANY), ((16, 512), BF16)],
-        [far_top, far_low, stream, middle, weight, down, up, turned, qown, meta, gain],
-        [WEIGHT_BUFFER, FOUR, pltpu.VMEM((512, 1024), BF16), pltpu.VMEM(full, F32), FOUR], limit=24,
-    )
+        [((1024, 1152), BF16), ((40, 1024), F32), ((1024, 1024), BF16)],
+        [(qslot, LOAD)],
+    )
+    (pack,) = call(partial_kernel, [((24, 1024), F32)], [tokens, turned, qown, meta, table])
     with jax.named_scope("packs"):
         packs = [pack, ring(pack, 1), ring(pack, 2), ring(pack, 3)]
     slot, batch, stats, sums = call(
@@ -714,8 +764,8 @@
         recv = lax.all_to_all(sums, "dp", 0, 0, tiled=True)
     pooled, rows = call(
         pooled_kernel,
-        [((128, 1024), BF16), ((1024, 1024), BF16)],
-        [(stream, ANY), stats, gain, qslot],
+        [((128, 1024), BF16), ((768, 1152), BF16)],
+        [(stream, HOLD), stats, gain, qslot],
         [pltpu.VMEM(full, F32), FOUR],
     )
     grad, far_top, far_low, lora, extras, up_part = call(
@@ -724,7 +774,7 @@
             (full, BF16, ANY), (half, BF16), (half, BF16), ((16, 512), F32),
             ((32, 384), F32, ANY), ((16, 1024), F32),
         ],
-        [recv, (stream, ANY), qslot, qown, gain, meta, slot, batch, stats, pooled, up, middle, weight],
+        [recv, (stream, HOLD), qslot, qown, gain, meta, slot, batch, stats, pooled, up, middle, weight],
         [
             WEIGHT_BUFFER, FOUR, pltpu.VMEM(full, F32), FOUR, pltpu.VMEM(full, BF16), FOUR,
             pltpu.VMEM((32, 384), F32), pltpu.SemaphoreType.DMA((1,)), pltpu.VMEM(full, BF16),
@@ -777,6 +827,7 @@
             (recv, LOAD), (home, LOAD), (extras, LOAD), (batch, LOAD), (pooled, LOAD),
             (qown, LOAD), arrived,
         ],
+        [pltpu.VMEM((1024, 1024), BF16)],
     )
     with jax.named_scope("adapters"):
         down_grad, up_grad, before, query_gradient = grid_sum(adapter, before, query_gradient)

time: 144 us -> 138 us (0.958)
  waiting for transfers between devices: 29.8 us -> 23.6 us
  Pallas kernels: 50.7 us -> 55.4 us
  local copies, waits for them, and re-layouts: 9.93 us -> 5.35 us
    pallas_call x18 -> x19, Pallas kernels: 50.7 us -> 55.4 us  [call(): pl.pallas_call(whole, cost_estimate=cost, name=kernel.__name__, out_shape...]
    unnamed x36 -> x32, local copies, waits for them, and re-layouts: 8.9 us -> 4.32 us
    all_to_all x1, waiting for transfers between devices: 6.86 us -> 2.5 us  [body(): qslot = lax.all_to_all(qslot_out, 'dp', 0, 0, tiled=True)]
  transfers between devices with their start and end apart: 28 -> 28, of which waited for: 12 -> 12; matrix products, arithmetic and copies ran while one was open for 1% -> 1% of each run, Pallas kernels for 22% -> 28%
where the time goes in v3:
time: 138 us
  Pallas kernels  55.4 us (40%)
  starting transfers between devices  52.2 us (38%)
  waiting for transfers between devices  23.6 us (17%)
  local copies, waits for them, and re-layouts  5.35 us (4%)
    pallas_call x19, Pallas kernels, call(): pl.pallas_call(whole, cost_estimate=cost, name=kernel.__name__, out_shape...  55.4 us
    ppermute x18, starting transfers between devices, ring(): return lax.ppermute(x, 'mp', [(i, (i + step) % 4) for i in range(4)])  24.5 us
    ppermute x18, waiting for transfers between devices, ring(): return lax.ppermute(x, 'mp', [(i, (i + step) % 4) for i in range(4)])  16.3 us
    ppermute x7, starting transfers between devices, grid_shift(): return lax.ppermute(v, 'dp', pairs)  11.1 us
    all_to_all x1, starting transfers between devices, body(): qslot = lax.all_to_all(qslot_out, 'dp', 0, 0, tiled=True)  7.45 us
    all_to_all x1, starting transfers between devices, body(): arrived = lax.all_to_all(rows, 'dp', 0, 0, tiled=True)  4.74 us
    all_to_all x1, starting transfers between devices, body(): recv = lax.all_to_all(sums, 'dp', 0, 0, tiled=True)  4.45 us
    unnamed x32, local copies, waits for them, and re-layouts  4.32 us
  transfers between devices with their start and end apart: 28, of which 12 were waited for; matrix products, arithmetic and copies ran while one was open for 1% of the time, Pallas kernels for 28%

profile of v3, /device:TPU:0, one launch (start us, length us, event | category | flops | bytes accessed | tf_op | source)
XLA Modules:
  0.0 137.6 jit_solution(7689543716637327398)
XLA Ops:
  0.6 2.5 %order_kernel.1 = (bf16[256,1024]{1,0:T(8,128)(2,1)}, bf16[256,1024]{1,0:T(8,128)(2,1)S(1)}) custom-call(bf16[512,1024]{1,0:T(8,128)(2,1)} %refs_4_.3), custom_call_target="tpu_custom_call" | custom-call | tf_op jit(solution)/shard_map/order_kernel/pallas_call | solution.py:623
  3.1 2.1 %collective-permute-start = (bf16[256,1024]{1,0:T(8,128)(2,1)}, bf16[256,1024]{1,0:T(8,128)(2,1)S(1)}, u32[]{:S(2)}, u32[]{:S(2)}) collective-permute-start(bf16[256,1024]{1,0:T(8,128)(2,1)} %get-tuple-element.68.refs_0_), channel_id=1, source_target_pairs={{0,1},{1,2},{2,3},{3,0},{4,5},{5,6},{6,7},{7,4},{8,9},{9,10},{10,1... | collective-permute-start | bytes 1572872 | tf_op jit(solution)/shard_map/leg1/ppermute | solution.py:650
  5.2 2.2 %collective-permute-start.2 = (bf16[256,1024]{1,0:T(8,128)(2,1)S(1)}, bf16[256,1024]{1,0:T(8,128)(2,1)S(1)}, u32[]{:S(2)}, u32[]{:S(2)}) collective-permute-start(bf16[256,1024]{1,0:T(8,128)(2,1)S(1)} %get-tuple-element.69.refs_1_), channel_id=1, source_target_pairs={{0,3},{1,0},{2,1},{3,2},{4,7},{5,4},{6,5},{7,6},{8,11},{9,8},{10,9... | collective-permute-start | bytes 1572872 | tf_op jit(solution)/shard_map/leg1/ppermute | solution.py:650
  7.4 1.9 %collective-permute-start.5 = (bf16[256,1024]{1,0:T(8,128)(2,1)}, bf16[256,1024]{1,0:T(8,128)(2,1)S(1)}, u32[]{:S(2)}, u32[]{:S(2)}) collective-permute-start(bf16[256,1024]{1,0:T(8,128)(2,1)} %get-tuple-element.68.refs_0_), channel_id=1, source_target_pairs={{0,3},{1,0},{2,1},{3,2},{4,7},{5,4},{6,5},{7,6},{8,11},{9,8},{10,9... | collective-permute-start | bytes 1572872 | tf_op jit(solution)/shard_map/leg2/ppermute | solution.py:650
  9.3 0.1 collective-permute-start.4
  9.4 0.8 copy.15
  10.2 0.1 reshape.38
  10.3 0.1 reshape.45.refs_1_
  10.5 0.8 copy-done.3
  11.3 3.6 %slot_kernel.1 = (bf16[768,1280]{1,0:T(8,128)(2,1)}, f32[40,1024]{1,0:T(8,128)}) custom-call(s32[1,640]{1,0:T(1,128)S(1)} %reshape.39.refs_0_, s32[640,1]{1,0:T(8,128)S(1)} %reshape.45.refs_1_, bf16[32,1024]{1,0:T(8,128)(2,1)S(1)} %copy-done.3), custom_call_target="tpu_custom_call" | custom-call | tf_op jit(solution)/shard_map/slot_kernel/pallas_call | solution.py:623
  14.9 7.4 %all-to-all-start = ((bf16[32,24,1280]{2,1,0:T(8,128)(2,1)}), bf16[32,24,1280]{2,1,0:T(8,128)(2,1)}, u32[]{:S(2)}, u32[]{:S(2)}) async-start(bf16[32,24,1280]{2,1,0:T(8,128)(2,1)} %bitcast.18), calls=%async_computation | async-start | bytes 3932160 | tf_op jit(solution)/shard_map/a2a_queries/all_to_all | solution.py:721
  22.4 0.1 collective-permute-start.1
  22.5 3.4 %collective-permute-start.3 = (bf16[256,1024]{1,0:T(8,128)(2,1)S(1)}, bf16[256,1024]{1,0:T(8,128)(2,1)S(1)}, u32[]{:S(2)}, u32[]{:S(2)}) collective-permute-start(bf16[256,1024]{1,0:T(8,128)(2,1)S(1)} %collective-permute-done.2.refs_3_), channel_id=1, source_target_pairs={{0,3},{1,0},{2,1},{3,2},{4,7},{5,4},{6,5},{7,6},{8,11},{9,8},{10,9... | collective-permute-start | bytes 1572872 | tf_op jit(solution)/shard_map/leg3/ppermute | solution.py:650
  25.9 1.2 copy-done.12
  27.1 4.2 %own_kernel.1 = (f32[512,1024]{1,0:T(8,128)S(1)}, f32[16,512]{1,0:T(8,128)S(1)}) custom-call(bf16[256,1024]{1,0:T(8,128)(2,1)} %get-tuple-element.68.refs_0_, bf16[256,1024]{1,0:T(8,128)(2,1)S(1)} %get-tuple-element.69.refs_1_, bf16[512,1024]{1,0:T(8,128)(2,1)S(1)} %copy-done.12, bf16[4096,1024]{1,0:T(8,128)(2,1)} %refs_1_.3, bf16[16,4096]{1,0:T(8,128)(2,1)S(1)} %bitcast.10), custom_call_target="tpu_custom_call" | custom-call | flops 17250000896 | tf_op jit(solution)/shard_map/own_kernel/pallas_call | solution.py:623
  31.3 0.2 collective-permute-done.4.refs_1_
  31.5 5.5 %sides_kernel.1 = (f32[512,1024]{1,0:T(8,128)}, f32[16,512]{1,0:T(8,128)S(1)}) custom-call(bf16[256,1024]{1,0:T(8,128)(2,1)S(1)} %collective-permute-done.refs_0_, bf16[256,1024]{1,0:T(8,128)(2,1)S(1)} %collective-permute-done.4.refs_1_, bf16[256,1024]{1,0:T(8,128)(2,1)S(1)} %collective-permute-done.5.refs_2_, ...), custom_call_target="tpu_custom_call" | custom-call | tf_op jit(solution)/shard_map/sides_kernel/pallas_call | solution.py:623
  37.0 4.9 %collective-permute-done.1.refs_0_ = bf16[256,1024]{1,0:T(8,128)(2,1)S(1)} collective-permute-done((bf16[256,1024]{1,0:T(8,128)(2,1)S(1)}, bf16[256,1024]{1,0:T(8,128)(2,1)S(1)}, u32[]{:S(2)}, u32[]{:S(2)}) %collective-permute-start.1) | collective-permute-done | bytes 524320 | tf_op jit(solution)/shard_map/leg3/ppermute | solution.py:650
  41.9 4.4 %far_kernel.1 = (f32[512,1024]{1,0:T(8,128)}, bf16[16,512]{1,0:T(8,128)(2,1)S(1)}, bf16[512,1024]{1,0:T(8,128)(2,1)S(1)}, f32[16,128]{1,0:T(8,128)S(1)}) custom-call(bf16[256,1024]{1,0:T(8,128)(2,1)S(1)} %collective-permute-done.1.refs_0_, bf16[256,1024]{1,0:T(8,128)(2,1)S(1)} %collective-permute-done.3.refs_1_, f32[512,1024]{1,0:T(8,128)} %get-tuple-element.75.refs_2_, ...), custom_call_target="tpu_custom_call" | custom-call | flops 4600000000 | tf_op jit(solution)/shard_map/far_kernel/pallas_call | solution.py:623
  46.4 1.0 copy-done.6
  47.3 2.5 %all-to-all-done = bf16[32,24,1280]{2,1,0:T(8,128)(2,1)} async-done(((bf16[32,24,1280]{2,1,0:T(8,128)(2,1)}), bf16[32,24,1280]{2,1,0:T(8,128)(2,1)}, u32[]{:S(2)}, u32[]{:S(2)}) %all-to-all-start) | async-done | bytes 1966112 | tf_op jit(solution)/shard_map/a2a_queries/all_to_all | solution.py:721
  49.8 2.8 %meta_kernel.1 = (bf16[1024,1152]{1,0:T(8,128)(2,1)S(1)}, f32[40,1024]{1,0:T(8,128)S(1)}, bf16[1024,1024]{1,0:T(8,128)(2,1)S(1)}) custom-call(bf16[768,1280]{1,0:T(8,128)(2,1)} %bitcast.3.refs_0_), custom_call_target="tpu_custom_call" | custom-call | tf_op jit(solution)/shard_map/meta_kernel/pallas_call | solution.py:623
  52.7 1.6 %partial_kernel.1.refs_0_ = f32[24,1024]{1,0:T(8,128)S(1)} custom-call(bf16[512,1024]{1,0:T(8,128)(2,1)S(1)} %copy-done.7, bf16[1024,1024]{1,0:T(8,128)(2,1)S(1)} %get-tuple-element.82.refs_1_, bf16[32,1024]{1,0:T(8,128)(2,1)S(1)} %copy-done.4, f32[40,1024]{1,0:T(8,128)S(1)} %get-tuple-element.83.refs_3_.refs_4_.refs_5_, f32[16,128]{1,0:T(8,128)S(1)} %get-tuple-element.84.refs_4_), custom_call_target="tpu_custom_call" | custom-call | tf_op jit(solution)/shard_map/partial_kernel/pallas_call | solution.py:623
  54.3 3.2 %collective-permute-start.8 = (f32[24,1024]{1,0:T(8,128)S(1)}, f32[24,1024]{1,0:T(8,128)S(1)}, u32[]{:S(2)}, u32[]{:S(2)}) collective-permute-start(f32[24,1024]{1,0:T(8,128)S(1)} %partial_kernel.1.refs_0_), channel_id=1, source_target_pairs={{0,3},{1,0},{2,1},{3,2},{4,7},{5,4},{6,5},{7,6},{8,11},{9,8},{10,9... | collective-permute-start | bytes 294920 | tf_op jit(solution)/shard_map/packs/ppermute | solution.py:650
  57.5 0.9 collective-permute-start.6
  58.5 3.1 %collective-permute-done.8.refs_3_ = f32[24,1024]{1,0:T(8,128)S(1)} collective-permute-done((f32[24,1024]{1,0:T(8,128)S(1)}, f32[24,1024]{1,0:T(8,128)S(1)}, u32[]{:S(2)}, u32[]{:S(2)}) %collective-permute-start.8) | collective-permute-done | bytes 98336 | tf_op jit(solution)/shard_map/packs/ppermute | solution.py:650
  61.5 2.8 %collective-permute-done.7.refs_2_ = f32[24,1024]{1,0:T(8,128)S(1)} collective-permute-done((f32[24,1024]{1,0:T(8,128)S(1)}, f32[24,1024]{1,0:T(8,128)S(1)}, u32[]{:S(2)}, u32[]{:S(2)}) %collective-permute-start.7) | collective-permute-done | bytes 98336 | tf_op jit(solution)/shard_map/packs/ppermute | solution.py:650
  64.3 0.7 collective-permute-done.6.refs_1_
  65.0 1.4 score_kernel.1
  66.3 4.4 %all-to-all-start.1 = ((f32[32,1,1280]{2,1,0:T(1,128)}), f32[32,1,1280]{2,1,0:T(1,128)S(1)}, u32[]{:S(2)}, u32[]{:S(2)}) async-start(f32[32,1,1280]{2,1,0:T(1,128)} %get-tuple-element.85), calls=%async_computation.1 | async-start | bytes 327680 | tf_op jit(solution)/shard_map/a2a_sums/all_to_all | solution.py:764
  70.8 3.2 %pooled_kernel.1 = (bf16[128,1024]{1,0:T(8,128)(2,1)S(1)}, bf16[768,1152]{1,0:T(8,128)(2,1)S(1)}) custom-call(f32[512,1024]{1,0:T(8,128)} %get-tuple-element.87.refs_0_.refs_1_, f32[16,128]{1,0:T(8,128)S(1)} %get-tuple-element.91.refs_1_.refs_8_, f32[1,1024]{1,0:T(1,128)S(1)} %bitcast.15, bf16[1024,1152]{1,0:T(8,128)(2,1)S(1)} %get-tuple-element.88.refs_3_.refs_2_), custom_call_target="tpu_custom_call" | custom-call | tf_op jit(solution)/shard_map/pooled_kernel/pallas_call | solution.py:623
  74.0 1.2 copy-done.1
  75.2 3.5 %all-to-all-done.1.refs_0_ = f32[32,1,1280]{2,1,0:T(1,128)S(1)} async-done(((f32[32,1,1280]{2,1,0:T(1,128)}), f32[32,1,1280]{2,1,0:T(1,128)S(1)}, u32[]{:S(2)}, u32[]{:S(2)}) %all-to-all-start.1) | async-done | bytes 163872 | tf_op jit(solution)/shard_map/a2a_sums/all_to_all | solution.py:764
  78.7 6.7 %gradient_kernel.1 = (bf16[512,1024]{1,0:T(8,128)(2,1)}, bf16[256,1024]{1,0:T(8,128)(2,1)}, bf16[256,1024]{1,0:T(8,128)(2,1)}, f32[16,512]{1,0:T(8,128)S(1)}, f32[32,384]{1,0:T(8,128)}, /*index=5*/f32[16,1024]{1,0:T(8,128)S(1)}) custom-call(f32[32,1,1280]{2,1,0:T(1,128)S(1)} %all-to-all-done.1.refs_0_, f32[512,1024]{1,0:T(8,128)} %get-tuple-element.87.refs_0_.refs_1_, ...), custom_call_target="tpu_custom_call" | custom-call | flops 1150000000 | tf_op jit(solution)/shard_map/gradient_kernel/pallas_call | solution.py:623
  85.5 0.0 copy-start
  85.5 0.1 collective-permute-start.12
  85.5 3.2 %collective-permute-start.13 = (bf16[256,1024]{1,0:T(8,128)(2,1)}, bf16[256,1024]{1,0:T(8,128)(2,1)S(1)}, u32[]{:S(2)}, u32[]{:S(2)}) collective-permute-start(bf16[256,1024]{1,0:T(8,128)(2,1)} %get-tuple-element.106), channel_id=1, source_target_pairs={{0,3},{1,0},{2,1},{3,2},{4,7},{5,4},{6,5},{7,6},{8,11},{9,8},{10,9... | collective-permute-start | bytes 1572872 | tf_op jit(solution)/shard_map/back1/ppermute | solution.py:650
  88.8 0.0 collective-permute-start.11
  88.8 0.9 collective-permute-start.10
  89.7 1.1 collective-permute-start.9
  90.8 4.7 %all-to-all-start.2 = ((bf16[32,24,1152]{2,1,0:T(8,128)(2,1)}), bf16[32,24,1152]{2,1,0:T(8,128)(2,1)}, u32[]{:S(2)}, u32[]{:S(2)}) async-start(bf16[32,24,1152]{2,1,0:T(8,128)(2,1)} %bitcast.9), calls=%async_computation.2 | async-start | bytes 3538944 | tf_op jit(solution)/shard_map/a2a_rows/all_to_all | solution.py:791
  95.6 5.1 %sides_back_kernel.1 = (bf16[256,1024]{1,0:T(8,128)(2,1)S(1)}, bf16[256,1024]{1,0:T(8,128)(2,1)S(1)}, bf16[256,1024]{1,0:T(8,128)(2,1)S(1)}, bf16[256,1024]{1,0:T(8,128)(2,1)S(1)}) custom-call(bf16[512,1024]{1,0:T(8,128)(2,1)S(1)} %copy-done, bf16[4096,1024]{1,0:T(8,128)(2,1)} %refs_1_.3), custom_call_target="tpu_custom_call" | custom-call | flops 1150000000 | tf_op jit(solution)/shard_map/sides_back_kernel/pallas_call | solution.py:623
  100.7 1.3 collective-permute-done.12.refs_2_
  102.0 1.4 %collective-permute-start.14 = (bf16[256,1024]{1,0:T(8,128)(2,1)S(1)}, bf16[256,1024]{1,0:T(8,128)(2,1)S(1)}, u32[]{:S(2)}, u32[]{:S(2)}) collective-permute-start(bf16[256,1024]{1,0:T(8,128)(2,1)S(1)} %get-tuple-element.112), channel_id=1, source_target_pairs={{0,3},{1,0},{2,1},{3,2},{4,7},{5,4},{6,5},{7,6},{8,11},{9,8},{10,9... | collective-permute-start | bytes 1572872 | tf_op jit(solution)/shard_map/back2/ppermute | solution.py:650
  103.4 0.6 collective-permute-start.15
  104.0 1.1 add_kernel.1
  105.2 0.9 collective-permute-start.23
  106.1 2.3 %collective-permute-start.24 = (bf16[256,1024]{1,0:T(8,128)(2,1)}, bf16[256,1024]{1,0:T(8,128)(2,1)}, u32[]{:S(2)}, u32[]{:S(2)}) collective-permute-start(bf16[256,1024]{1,0:T(8,128)(2,1)} %get-tuple-element.123), channel_id=1, source_target_pairs={{0,3},{1,0},{2,1},{3,2},{4,7},{5,4},{6,5},{7,6},{8,11},{9,8},{10,9... | collective-permute-start | bytes 1572872 | tf_op jit(solution)/shard_map/back3/ppermute | solution.py:650
  108.4 1.5 %join_kernel.1 = (bf16[32,1024]{1,0:T(8,128)(2,1)S(1)}, bf16[16,512]{1,0:T(8,128)(2,1)S(1)}) custom-call(f32[16,512]{1,0:T(8,128)S(1)} %get-tuple-element.102.refs_0_, f32[16,512]{1,0:T(8,128)S(1)} %collective-permute-done.9.refs_1_, f32[16,512]{1,0:T(8,128)S(1)} %collective-permute-done.10.refs_2_, f32[16,512]{1,0:T(8,128)S(1)} %collective-permute-done.11.refs_3_, ...), custom_call_target="tpu_custom_call" | custom-call | flops 18400000000 | tf_op jit(solution)/shard_map/join_kernel/pallas_call | solution.py:623
  109.9 0.1 collective-permute-start.16
  110.0 1.2 collective-permute-done.16.refs_1_
  111.3 2.8 %collective-permute-start.19 = (bf16[32,1024]{1,0:T(8,128)(2,1)S(1)}, bf16[32,1024]{1,0:T(8,128)(2,1)S(1)}, u32[]{:S(2)}, u32[]{:S(2)}) collective-permute-start(bf16[32,1024]{1,0:T(8,128)(2,1)S(1)} %pair_kernel.1.refs_0_), channel_id=1, source_target_pairs={{0,96},{4,100},{8,104},{12,108},{16,112},{20,116},{24,120},{28,124... | collective-permute-start | bytes 196616 | tf_op jit(solution)/shard_map/adapters/ppermute | solution.py:673
  114.1 2.8 %collective-permute-done.14.refs_4_ = bf16[256,1024]{1,0:T(8,128)(2,1)S(1)} collective-permute-done((bf16[256,1024]{1,0:T(8,128)(2,1)S(1)}, bf16[256,1024]{1,0:T(8,128)(2,1)S(1)}, u32[]{:S(2)}, u32[]{:S(2)}) %collective-permute-start.14) | collective-permute-done | bytes 524320 | tf_op jit(solution)/shard_map/back2/ppermute | solution.py:650
  116.9 2.0 %collective-permute-start.18 = (bf16[32,1024]{1,0:T(8,128)(2,1)S(1)}, bf16[32,1024]{1,0:T(8,128)(2,1)S(1)}, u32[]{:S(2)}, u32[]{:S(2)}) collective-permute-start(bf16[32,1024]{1,0:T(8,128)(2,1)S(1)} %pair_kernel.1.refs_0_), channel_id=1, source_target_pairs={{0,64},{4,68},{8,72},{12,76},{16,80},{20,84},{24,88},{28,92},{32,9... | collective-permute-start | bytes 196616 | tf_op jit(solution)/shard_map/adapters/ppermute | solution.py:673
  118.9 0.5 collective-permute-done.15.refs_5_
  119.4 1.7 %collective-permute-start.17 = (bf16[32,1024]{1,0:T(8,128)(2,1)S(1)}, bf16[32,1024]{1,0:T(8,128)(2,1)S(1)}, u32[]{:S(2)}, u32[]{:S(2)}) collective-permute-start(bf16[32,1024]{1,0:T(8,128)(2,1)S(1)} %pair_kernel.1.refs_0_), channel_id=1, source_target_pairs={{0,32},{4,36},{8,40},{12,44},{16,48},{20,52},{24,56},{28,60},{32,6... | collective-permute-start | bytes 196616 | tf_op jit(solution)/shard_map/adapters/ppermute | solution.py:673
  121.1 4.1 %own_back_kernel.1.refs_0_ = f32[512,1024]{1,0:T(8,128)S(1)} custom-call(bf16[512,1024]{1,0:T(8,128)(2,1)S(1)} %copy-done, bf16[4096,1024]{1,0:T(8,128)(2,1)} %refs_1_.3, bf16[16,4096]{1,0:T(8,128)(2,1)S(1)} %bitcast.13, bf16[16,512]{1,0:T(8,128)(2,1)S(1)} %get-tuple-element.111.refs_3_, bf16[256,1024]{1,0:T(8,128)(2,1)S(1)} %collective-permute-done.14.refs_4_, ...), custom_call_target="tpu_custom_call" | custom-call | tf_op jit(solution)/shard_map/own_back_kernel/pallas_call | solution.py:623
  125.3 2.8 %collective-permute-start.22 = (bf16[32,1024]{1,0:T(8,128)(2,1)S(1)}, bf16[32,1024]{1,0:T(8,128)(2,1)S(1)}, u32[]{:S(2)}, u32[]{:S(2)}) collective-permute-start(bf16[32,1024]{1,0:T(8,128)(2,1)S(1)} %four_kernel.1.refs_0_), channel_id=1, source_target_pairs={{0,24},{4,28},{8,0},{12,4},{16,8},{20,12},{24,16},{28,20},{32,56},... | collective-permute-start | bytes 196616 | tf_op jit(solution)/shard_map/adapters/ppermute | solution.py:673
  128.1 0.8 collective-permute-start.21
  128.9 0.9 collective-permute-start.20
  129.8 4.7 %query_kernel.1 = (bf16[32,1024]{1,0:T(8,128)(2,1)}, f32[1,32]{1,0:T(1,128)}) custom-call(f32[32,1,1280]{2,1,0:T(1,128)} %copy-done.2, f32[40,1024]{1,0:T(8,128)} %get-tuple-element.86.refs_1_, f32[32,384]{1,0:T(8,128)} %get-tuple-element.94.refs_2_, f32[32,896]{1,0:T(8,128)} %copy-done.9, bf16[128,1024]{1,0:T(8,128)(2,1)} %copy-done.5, ...), custom_call_target="tpu_custom_call" | custom-call | tf_op jit(solution)/shard_map/query_kernel/pallas_call | solution.py:623
  134.4 0.1 collective-permute-done.20.refs_1_
  134.5 0.7 last_kernel.1
  135.2 2.3 %finish_kernel.1 = bf16[512,1024]{1,0:T(8,128)(2,1)} custom-call(f32[512,1024]{1,0:T(8,128)S(1)} %own_back_kernel.1.refs_0_, bf16[256,1024]{1,0:T(8,128)(2,1)} %collective-permute-done.23.refs_1_, bf16[256,1024]{1,0:T(8,128)(2,1)} %collective-permute-done.24.refs_2_), custom_call_target="tpu_custom_call" | custom-call | tf_op jit(solution)/shard_map/finish_kernel/pallas_call | solution.py:623
  (49 shorter events, 0.2 us)
Async XLA Ops:
  3.1 19.3 %collective-permute-start = (bf16[256,1024]{1,0:T(8,128)(2,1)}, bf16[256,1024]{1,0:T(8,128)(2,1)S(1)}, u32[]{:S(2)}, u32[]{:S(2)}) collective-permute-start(bf16[256,1024]{1,0:T(8,128)(2,1)} %get-tuple-element.68.refs_0_), channel_id=1, source_target_pairs={{0,1},{1,2},{2,3},{3,0},{4,5},{5,6},{6,7},{7,4},{8,9},{9,10},{10,1... | collective-permute-start | bytes 1572872 | tf_op jit(solution)/shard_map/leg1/ppermute | solution.py:650
  5.2 17.2 %collective-permute-start.2 = (bf16[256,1024]{1,0:T(8,128)(2,1)S(1)}, bf16[256,1024]{1,0:T(8,128)(2,1)S(1)}, u32[]{:S(2)}, u32[]{:S(2)}) collective-permute-start(bf16[256,1024]{1,0:T(8,128)(2,1)S(1)} %get-tuple-element.69.refs_1_), channel_id=1, source_target_pairs={{0,3},{1,0},{2,1},{3,2},{4,7},{5,4},{6,5},{7,6},{8,11},{9,8},{10,9... | collective-permute-start | bytes 1572872 | tf_op jit(solution)/shard_map/leg1/ppermute | solution.py:650
  7.4 23.9 %collective-permute-start.5 = (bf16[256,1024]{1,0:T(8,128)(2,1)}, bf16[256,1024]{1,0:T(8,128)(2,1)S(1)}, u32[]{:S(2)}, u32[]{:S(2)}) collective-permute-start(bf16[256,1024]{1,0:T(8,128)(2,1)} %get-tuple-element.68.refs_0_), channel_id=1, source_target_pairs={{0,3},{1,0},{2,1},{3,2},{4,7},{5,4},{6,5},{7,6},{8,11},{9,8},{10,9... | collective-permute-start | bytes 1572872 | tf_op jit(solution)/shard_map/leg2/ppermute | solution.py:650
  9.3 22.2 %collective-permute-start.4 = (bf16[256,1024]{1,0:T(8,128)(2,1)S(1)}, bf16[256,1024]{1,0:T(8,128)(2,1)S(1)}, u32[]{:S(2)}, u32[]{:S(2)}) collective-permute-start(bf16[256,1024]{1,0:T(8,128)(2,1)S(1)} %get-tuple-element.69.refs_1_), channel_id=1, source_target_pairs={{0,1},{1,2},{2,3},{3,0},{4,5},{5,6},{6,7},{7,4},{8,9},{9,10},{10,1... | collective-permute-start | bytes 1572872 | tf_op jit(solution)/shard_map/leg2/ppermute | solution.py:650
  10.5 0.8 copy-start.3
  11.3 11.1 %copy-start.15 = (bf16[1024]{0:T(1024)(128)(2,1)S(1)}, bf16[1024]{0:T(1024)(128)(2,1)}, u32[]{:S(2)}) copy-start(bf16[1024]{0:T(1024)(128)(2,1)} %param.14) | copy-start | bytes 6148
  11.3 14.6 %copy-start.8 = (bf16[4096,16]{0,1:T(8,128)(2,1)S(1)}, bf16[4096,16]{0,1:T(8,128)(2,1)}, u32[]{:S(2)}) copy-start(bf16[4096,16]{0,1:T(8,128)(2,1)} %param.12) | copy-start | bytes 393220
  14.9 34.9 %all-to-all-start = ((bf16[32,24,1280]{2,1,0:T(8,128)(2,1)}), bf16[32,24,1280]{2,1,0:T(8,128)(2,1)}, u32[]{:S(2)}, u32[]{:S(2)}) async-start(bf16[32,24,1280]{2,1,0:T(8,128)(2,1)} %bitcast.18), calls=%async_computation | async-start | bytes 3932160 | tf_op jit(solution)/shard_map/a2a_queries/all_to_all | solution.py:721
  22.4 19.5 %collective-permute-start.1 = (bf16[256,1024]{1,0:T(8,128)(2,1)S(1)}, bf16[256,1024]{1,0:T(8,128)(2,1)S(1)}, u32[]{:S(2)}, u32[]{:S(2)}) collective-permute-start(bf16[256,1024]{1,0:T(8,128)(2,1)S(1)} %collective-permute-done.refs_0_), channel_id=1, source_target_pairs={{0,1},{1,2},{2,3},{3,0},{4,5},{5,6},{6,7},{7,4},{8,9},{9,10},{10,1... | collective-permute-start | bytes 1572872 | tf_op jit(solution)/shard_map/leg3/ppermute | solution.py:650
  22.5 19.4 %collective-permute-start.3 = (bf16[256,1024]{1,0:T(8,128)(2,1)S(1)}, bf16[256,1024]{1,0:T(8,128)(2,1)S(1)}, u32[]{:S(2)}, u32[]{:S(2)}) collective-permute-start(bf16[256,1024]{1,0:T(8,128)(2,1)S(1)} %collective-permute-done.2.refs_3_), channel_id=1, source_target_pairs={{0,3},{1,0},{2,1},{3,2},{4,7},{5,4},{6,5},{7,6},{8,11},{9,8},{10,9... | collective-permute-start | bytes 1572872 | tf_op jit(solution)/shard_map/leg3/ppermute | solution.py:650
  25.9 1.2 copy-start.12
  31.5 10.4 %copy-start.10 = (bf16[16,1024]{1,0:T(8,128)(2,1)S(1)}, bf16[16,1024]{1,0:T(8,128)(2,1)}, u32[]{:S(2)}) copy-start(bf16[16,1024]{1,0:T(8,128)(2,1)} %refs_10_.1) | copy-start | bytes 98308
  41.9 10.8 %copy-start.4 = (bf16[32,1024]{1,0:T(8,128)(2,1)S(1)}, bf16[32,1024]{1,0:T(8,128)(2,1)}, u32[]{:S(2)}) copy-start(bf16[32,1024]{1,0:T(8,128)(2,1)} %refs_5_.1) | copy-start | bytes 196612
  46.4 1.0 copy-start.6
  49.8 2.9 %copy-start.7 = (bf16[512,1024]{1,0:T(8,128)(2,1)S(1)}, bf16[512,1024]{1,0:T(8,128)(2,1)}, u32[]{:S(2)}) copy-start(bf16[512,1024]{1,0:T(8,128)(2,1)} %copy-done.6) | copy-start | bytes 3145732
  52.7 12.3 %copy-start.11 = (s32[128]{0:T(128)S(1)}, s32[128]{0:T(128)}, u32[]{:S(2)}) copy-start(s32[128]{0:T(128)} %param.17) | copy-start | bytes 1540
  54.3 7.2 %collective-permute-start.8 = (f32[24,1024]{1,0:T(8,128)S(1)}, f32[24,1024]{1,0:T(8,128)S(1)}, u32[]{:S(2)}, u32[]{:S(2)}) collective-permute-start(f32[24,1024]{1,0:T(8,128)S(1)} %partial_kernel.1.refs_0_), channel_id=1, source_target_pairs={{0,3},{1,0},{2,1},{3,2},{4,7},{5,4},{6,5},{7,6},{8,11},{9,8},{10,9... | collective-permute-start | bytes 294920 | tf_op jit(solution)/shard_map/packs/ppermute | solution.py:650
  57.5 6.8 %collective-permute-start.7 = (f32[24,1024]{1,0:T(8,128)S(1)}, f32[24,1024]{1,0:T(8,128)S(1)}, u32[]{:S(2)}, u32[]{:S(2)}) collective-permute-start(f32[24,1024]{1,0:T(8,128)S(1)} %partial_kernel.1.refs_0_), channel_id=1, source_target_pairs={{0,2},{1,3},{2,0},{3,1},{4,6},{5,7},{6,4},{7,5},{8,10},{9,11},{10,... | collective-permute-start | bytes 294920 | tf_op jit(solution)/shard_map/packs/ppermute | solution.py:650
  57.5 7.4 %collective-permute-start.6 = (f32[24,1024]{1,0:T(8,128)S(1)}, f32[24,1024]{1,0:T(8,128)S(1)}, u32[]{:S(2)}, u32[]{:S(2)}) collective-permute-start(f32[24,1024]{1,0:T(8,128)S(1)} %partial_kernel.1.refs_0_), channel_id=1, source_target_pairs={{0,1},{1,2},{2,3},{3,0},{4,5},{5,6},{6,7},{7,4},{8,9},{9,10},{10,1... | collective-permute-start | bytes 294920 | tf_op jit(solution)/shard_map/packs/ppermute | solution.py:650
  66.3 12.4 %copy-start.9 = (f32[32,896]{1,0:T(8,128)}, f32[32,896]{1,0:T(8,128)S(1)}, u32[]{:S(2)}) copy-start(f32[32,896]{1,0:T(8,128)S(1)} %get-tuple-element.90.refs_7_.refs_3_) | copy-start | bytes 344068
  66.3 12.4 %all-to-all-start.1 = ((f32[32,1,1280]{2,1,0:T(1,128)}), f32[32,1,1280]{2,1,0:T(1,128)S(1)}, u32[]{:S(2)}, u32[]{:S(2)}) async-start(f32[32,1,1280]{2,1,0:T(1,128)} %get-tuple-element.85), calls=%async_computation.1 | async-start | bytes 327680 | tf_op jit(solution)/shard_map/a2a_sums/all_to_all | solution.py:764
  74.0 1.2 copy-start.1
  75.2 10.2 %copy-start.5 = (bf16[128,1024]{1,0:T(8,128)(2,1)}, bf16[128,1024]{1,0:T(8,128)(2,1)S(1)}, u32[]{:S(2)}) copy-start(bf16[128,1024]{1,0:T(8,128)(2,1)S(1)} %get-tuple-element.92.refs_9_.refs_4_) | copy-start | bytes 786436
  78.7 6.8 %copy-start.2 = (f32[32,1,1280]{2,1,0:T(1,128)}, f32[32,1,1280]{2,1,0:T(1,128)S(1)}, u32[]{:S(2)}) copy-start(f32[32,1,1280]{2,1,0:T(1,128)S(1)} %all-to-all-done.1.refs_0_) | copy-start | bytes 491524
  85.4 10.1 %copy-start.13 = (f32[16,1024]{1,0:T(8,128)}, f32[16,1024]{1,0:T(8,128)S(1)}, u32[]{:S(2)}) copy-start(f32[16,1024]{1,0:T(8,128)S(1)} %get-tuple-element.110.refs_5_) | copy-start | bytes 196612
  85.5 10.1 %copy-start = (bf16[512,1024]{1,0:T(8,128)(2,1)S(1)}, bf16[512,1024]{1,0:T(8,128)(2,1)}, u32[]{:S(2)}) copy-start(bf16[512,1024]{1,0:T(8,128)(2,1)} %get-tuple-element.64.refs_0_) | copy-start | bytes 3145732
  85.5 16.5 %collective-permute-start.12 = (bf16[256,1024]{1,0:T(8,128)(2,1)}, bf16[256,1024]{1,0:T(8,128)(2,1)S(1)}, u32[]{:S(2)}, u32[]{:S(2)}) collective-permute-start(bf16[256,1024]{1,0:T(8,128)(2,1)} %get-tuple-element.105), channel_id=1, source_target_pairs={{0,1},{1,2},{2,3},{3,0},{4,5},{5,6},{6,7},{7,4},{8,9},{9,10},{10,1... | collective-permute-start | bytes 1572872 | tf_op jit(solution)/shard_map/back1/ppermute | solution.py:650
  85.5 17.9 %collective-permute-start.13 = (bf16[256,1024]{1,0:T(8,128)(2,1)}, bf16[256,1024]{1,0:T(8,128)(2,1)S(1)}, u32[]{:S(2)}, u32[]{:S(2)}) collective-permute-start(bf16[256,1024]{1,0:T(8,128)(2,1)} %get-tuple-element.106), channel_id=1, source_target_pairs={{0,3},{1,0},{2,1},{3,2},{4,7},{5,4},{6,5},{7,6},{8,11},{9,8},{10,9... | collective-permute-start | bytes 1572872 | tf_op jit(solution)/shard_map/back1/ppermute | solution.py:650
  88.8 16.4 %collective-permute-start.11 = (f32[16,512]{1,0:T(8,128)S(1)}, f32[16,512]{1,0:T(8,128)S(1)}, u32[]{:S(2)}, u32[]{:S(2)}) collective-permute-start(f32[16,512]{1,0:T(8,128)S(1)} %get-tuple-element.102.refs_0_), channel_id=1, source_target_pairs={{0,3},{1,0},{2,1},{3,2},{4,7},{5,4},{6,5},{7,6},{8,11},{9,8},{10,9... | collective-permute-start | bytes 98312 | tf_op jit(solution)/shard_map/lora_sum/ppermute | solution.py:650
  88.8 17.3 %collective-permute-start.10 = (f32[16,512]{1,0:T(8,128)S(1)}, f32[16,512]{1,0:T(8,128)S(1)}, u32[]{:S(2)}, u32[]{:S(2)}) collective-permute-start(f32[16,512]{1,0:T(8,128)S(1)} %get-tuple-element.102.refs_0_), channel_id=1, source_target_pairs={{0,2},{1,3},{2,0},{3,1},{4,6},{5,7},{6,4},{7,5},{8,10},{9,11},{10,... | collective-permute-start | bytes 98312 | tf_op jit(solution)/shard_map/lora_sum/ppermute | solution.py:650
  89.7 18.7 %collective-permute-start.9 = (f32[16,512]{1,0:T(8,128)S(1)}, f32[16,512]{1,0:T(8,128)S(1)}, u32[]{:S(2)}, u32[]{:S(2)}) collective-permute-start(f32[16,512]{1,0:T(8,128)S(1)} %get-tuple-element.102.refs_0_), channel_id=1, source_target_pairs={{0,1},{1,2},{2,3},{3,0},{4,5},{5,6},{6,7},{7,4},{8,9},{9,10},{10,1... | collective-permute-start | bytes 98312 | tf_op jit(solution)/shard_map/lora_sum/ppermute | solution.py:650
  90.8 39.0 %all-to-all-start.2 = ((bf16[32,24,1152]{2,1,0:T(8,128)(2,1)}), bf16[32,24,1152]{2,1,0:T(8,128)(2,1)}, u32[]{:S(2)}, u32[]{:S(2)}) async-start(bf16[32,24,1152]{2,1,0:T(8,128)(2,1)} %bitcast.9), calls=%async_computation.2 | async-start | bytes 3538944 | tf_op jit(solution)/shard_map/a2a_rows/all_to_all | solution.py:791
  100.6 7.8 %copy-start.14 = (f32[16,1024]{1,0:T(8,128)S(1)}, f32[16,1024]{1,0:T(8,128)}, u32[]{:S(2)}) copy-start(f32[16,1024]{1,0:T(8,128)} %copy-done.13) | copy-start | bytes 196612
  102.0 14.9 %collective-permute-start.14 = (bf16[256,1024]{1,0:T(8,128)(2,1)S(1)}, bf16[256,1024]{1,0:T(8,128)(2,1)S(1)}, u32[]{:S(2)}, u32[]{:S(2)}) collective-permute-start(bf16[256,1024]{1,0:T(8,128)(2,1)S(1)} %get-tuple-element.112), channel_id=1, source_target_pairs={{0,3},{1,0},{2,1},{3,2},{4,7},{5,4},{6,5},{7,6},{8,11},{9,8},{10,9... | collective-permute-start | bytes 1572872 | tf_op jit(solution)/shard_map/back2/ppermute | solution.py:650
  103.4 16.0 %collective-permute-start.15 = (bf16[256,1024]{1,0:T(8,128)(2,1)S(1)}, bf16[256,1024]{1,0:T(8,128)(2,1)S(1)}, u32[]{:S(2)}, u32[]{:S(2)}) collective-permute-start(bf16[256,1024]{1,0:T(8,128)(2,1)S(1)} %get-tuple-element.113), channel_id=1, source_target_pairs={{0,1},{1,2},{2,3},{3,0},{4,5},{5,6},{6,7},{7,4},{8,9},{9,10},{10,1... | collective-permute-start | bytes 1572872 | tf_op jit(solution)/shard_map/back2/ppermute | solution.py:650
  105.2 30.0 %collective-permute-start.23 = (bf16[256,1024]{1,0:T(8,128)(2,1)}, bf16[256,1024]{1,0:T(8,128)(2,1)}, u32[]{:S(2)}, u32[]{:S(2)}) collective-permute-start(bf16[256,1024]{1,0:T(8,128)(2,1)} %get-tuple-element.122), channel_id=1, source_target_pairs={{0,1},{1,2},{2,3},{3,0},{4,5},{5,6},{6,7},{7,4},{8,9},{9,10},{10,1... | collective-permute-start | bytes 1572872 | tf_op jit(solution)/shard_map/back3/ppermute | solution.py:650
  106.1 29.1 %collective-permute-start.24 = (bf16[256,1024]{1,0:T(8,128)(2,1)}, bf16[256,1024]{1,0:T(8,128)(2,1)}, u32[]{:S(2)}, u32[]{:S(2)}) collective-permute-start(bf16[256,1024]{1,0:T(8,128)(2,1)} %get-tuple-element.123), channel_id=1, source_target_pairs={{0,3},{1,0},{2,1},{3,2},{4,7},{5,4},{6,5},{7,6},{8,11},{9,8},{10,9... | collective-permute-start | bytes 1572872 | tf_op jit(solution)/shard_map/back3/ppermute | solution.py:650
  109.9 1.3 collective-permute-start.16
  111.3 13.9 %collective-permute-start.19 = (bf16[32,1024]{1,0:T(8,128)(2,1)S(1)}, bf16[32,1024]{1,0:T(8,128)(2,1)S(1)}, u32[]{:S(2)}, u32[]{:S(2)}) collective-permute-start(bf16[32,1024]{1,0:T(8,128)(2,1)S(1)} %pair_kernel.1.refs_0_), channel_id=1, source_target_pairs={{0,96},{4,100},{8,104},{12,108},{16,112},{20,116},{24,120},{28,124... | collective-permute-start | bytes 196616 | tf_op jit(solution)/shard_map/adapters/ppermute | solution.py:673
  116.9 8.3 %collective-permute-start.18 = (bf16[32,1024]{1,0:T(8,128)(2,1)S(1)}, bf16[32,1024]{1,0:T(8,128)(2,1)S(1)}, u32[]{:S(2)}, u32[]{:S(2)}) collective-permute-start(bf16[32,1024]{1,0:T(8,128)(2,1)S(1)} %pair_kernel.1.refs_0_), channel_id=1, source_target_pairs={{0,64},{4,68},{8,72},{12,76},{16,80},{20,84},{24,88},{28,92},{32,9... | collective-permute-start | bytes 196616 | tf_op jit(solution)/shard_map/adapters/ppermute | solution.py:673
  119.4 5.8 %collective-permute-start.17 = (bf16[32,1024]{1,0:T(8,128)(2,1)S(1)}, bf16[32,1024]{1,0:T(8,128)(2,1)S(1)}, u32[]{:S(2)}, u32[]{:S(2)}) collective-permute-start(bf16[32,1024]{1,0:T(8,128)(2,1)S(1)} %pair_kernel.1.refs_0_), channel_id=1, source_target_pairs={{0,32},{4,36},{8,40},{12,44},{16,48},{20,52},{24,56},{28,60},{32,6... | collective-permute-start | bytes 196616 | tf_op jit(solution)/shard_map/adapters/ppermute | solution.py:673
  125.3 9.2 %collective-permute-start.22 = (bf16[32,1024]{1,0:T(8,128)(2,1)S(1)}, bf16[32,1024]{1,0:T(8,128)(2,1)S(1)}, u32[]{:S(2)}, u32[]{:S(2)}) collective-permute-start(bf16[32,1024]{1,0:T(8,128)(2,1)S(1)} %four_kernel.1.refs_0_), channel_id=1, source_target_pairs={{0,24},{4,28},{8,0},{12,4},{16,8},{20,12},{24,16},{28,20},{32,56},... | collective-permute-start | bytes 196616 | tf_op jit(solution)/shard_map/adapters/ppermute | solution.py:673
  128.1 6.4 %collective-permute-start.21 = (bf16[32,1024]{1,0:T(8,128)(2,1)S(1)}, bf16[32,1024]{1,0:T(8,128)(2,1)S(1)}, u32[]{:S(2)}, u32[]{:S(2)}) collective-permute-start(bf16[32,1024]{1,0:T(8,128)(2,1)S(1)} %four_kernel.1.refs_0_), channel_id=1, source_target_pairs={{0,16},{4,20},{8,24},{12,28},{16,0},{20,4},{24,8},{28,12},{32,48},... | collective-permute-start | bytes 196616 | tf_op jit(solution)/shard_map/adapters/ppermute | solution.py:673
  128.9 5.6 %collective-permute-start.20 = (bf16[32,1024]{1,0:T(8,128)(2,1)S(1)}, bf16[32,1024]{1,0:T(8,128)(2,1)S(1)}, u32[]{:S(2)}, u32[]{:S(2)}) collective-permute-start(bf16[32,1024]{1,0:T(8,128)(2,1)S(1)} %four_kernel.1.refs_0_), channel_id=1, source_target_pairs={{0,8},{4,12},{8,16},{12,20},{16,24},{20,28},{24,0},{28,4},{32,40},... | collective-permute-start | bytes 196616 | tf_op jit(solution)/shard_map/adapters/ppermute | solution.py:673

commit v4 on v3

--- a/solution.py
+++ b/solution.py
@@ -97,26 +97,30 @@
     off = 0
     for piece in pieces:
         lanes = slice(off, off + piece.shape[1])
-        for o in range(32):
-            out[o * 24 : o * 24 + 24, lanes] = piece[o * 32 : o * 32 + 24].astype(BF16)
+        kept = [piece[o * 32 : o * 32 + 24] for o in range(32)]
+        out[:, lanes] = jnp.concatenate(kept, axis=0).astype(BF16)
         off += piece.shape[1]
     stack = jnp.concatenate([last[:, i : i + 128] for i in range(0, width, 128)], axis=0)
     table = fold_map((768, stack.shape[0]), 0).astype(F32).astype(BF16)
     out[:, width : width + 128] = dot(table, stack, ((1,), (0,))).astype(BF16)
 
 
-def unfold(arrived, full):
-    width = full.shape[1]
+def last_rows(extra, width):
     parts = width // 128
     table = fold_map((parts * 32, 768), 1).astype(F32).astype(BF16)
-    stack = dot(table, arrived[:, width : width + 128], ((1,), (0,))).astype(BF16)
+    stack = dot(table, extra, ((1,), (0,)))
     last = jnp.concatenate([stack[c * 32 : c * 32 + 32] for c in range(parts)], axis=1)
-    last = jnp.concatenate([last, jnp.zeros((96, width), BF16)], axis=0)
+    last = jnp.concatenate([last, jnp.zeros((96, width), F32)], axis=0).astype(BF16)
     place = (iota((256, 128), 0) == iota((256, 128), 1) * 8).astype(F32).astype(BF16)
-    rows = dot(place, last, ((1,), (0,))).astype(BF16)
-    for b in range(32):
-        full[b * 32 : b * 32 + 24, :] = arrived[b * 24 : b * 24 + 24, 0:width]
-        full[b * 32 + 24 : b * 32 + 32, :] = rows[b * 8 : b * 8 + 8]
+    return dot(place, last, ((1,), (0,)))
+
+
+def unfold(kept, last, first):
+    pieces = []
+    for i in range(8):
+        pieces.append(kept[i * 24 : i * 24 + 24])
+        pieces.append(last[(first + i) * 8 : (first + i) * 8 + 8])
+    return jnp.concatenate(pieces, axis=0)
 
 
 def last_slots():
@@ -158,12 +162,23 @@
     fold([rows, picked], jnp.concatenate([last, last_values], axis=1), out)
 
 
-def meta_kernel(arrived, qslot, meta, turned):
-    unfold(arrived, qslot)
-    turned[...] = qslot[:, 0:1024].astype(F32).T.astype(BF16)
-    table = qslot[:, 1024:1152].astype(F32).T
-    meta[0:40, :] = table[0:40, :]
-    meta[35:36, :] = table[35:36, :] + table[36:37, :] + table[37:38, :]
+def meta_kernel(arrived, qslot, meta, turned, main, extra, sems):
+    copies = [pltpu.make_async_copy(arrived.at[:, 1152:1280], extra, sems.at[4])]
+    for c in range(4):
+        rows = pl.ds(c * 192, 192)
+        copies.append(pltpu.make_async_copy(arrived.at[rows, 0:1152], main.at[rows, :], sems.at[c]))
+    for copy in copies:
+        copy.start()
+    copies[0].wait()
+    last = last_rows(extra[...], 1152)
+    for c in range(4):
+        copies[c + 1].wait()
+        rows = unfold(main[c * 192 : c * 192 + 192, :].astype(F32), last, c * 8)
+        lanes = slice(c * 256, c * 256 + 256)
+        qslot[lanes, :] = rows.astype(BF16)
+        turned[:, lanes] = rows[:, 0:1024].T.astype(BF16)
+        meta[0:40, lanes] = rows[:, 1024:1152].T[0:40]
+    meta[35:36, :] = meta[35:36, :] + meta[36:37, :] + meta[37:38, :]
 
 
 def own_kernel(top, low, residual, weight, down, stream, middle, buffer, sems):
@@ -565,7 +580,10 @@
     row = jnp.sum(jnp.where(eye, log_col - positive, 0.0), axis=0, keepdims=True)
     loss[...] = row[:, 0:32]
     qinv = batch[:, 768:769]
-    unfold(arrived, listed)
+    last = last_rows(arrived[:, 1024:1152], 1024)
+    for c in range(4):
+        rows = unfold(arrived[c * 192 : c * 192 + 192, 0:1024].astype(F32), last, c * 8)
+        listed[c * 256 : c * 256 + 256, :] = rows.astype(BF16)
     total = dot((mine * value).astype(BF16), listed[...], ((1,), (0,)))
     total = total + dot(extras[:, 128:256].astype(BF16), pooled[...], ((1,), (0,)))
     gradient[...] = (total - (scalar * qinv * qinv) * qown[...].astype(F32)).astype(BF16)
@@ -750,7 +768,11 @@
     qslot, meta, turned = call(
         meta_kernel,
         [((1024, 1152), BF16), ((40, 1024), F32), ((1024, 1024), BF16)],
-        [(qslot, LOAD)],
+        [(qslot, HOLD)],
+        [
+            pltpu.VMEM((768, 1152), BF16), pltpu.VMEM((768, 128), BF16),
+            pltpu.SemaphoreType.DMA((5,)),
+        ],
     )
     (pack,) = call(partial_kernel, [((24, 1024), F32)], [tokens, turned, qown, meta, table])
     with jax.named_scope("packs"):

time: 138 us -> 138 us (level)
  no operation moved by 1% of the time
where the time goes in v4:
time: 138 us
  Pallas kernels  55.4 us (40%)
  starting transfers between devices  52.3 us (38%)
  waiting for transfers between devices  23.4 us (17%)
  local copies, waits for them, and re-layouts  5.35 us (4%)
    pallas_call x19, Pallas kernels, call(): pl.pallas_call(whole, cost_estimate=cost, name=kernel.__name__, out_shape...  55.4 us
    ppermute x18, starting transfers between devices, ring(): return lax.ppermute(x, 'mp', [(i, (i + step) % 4) for i in range(4)])  24.5 us
    ppermute x18, waiting for transfers between devices, ring(): return lax.ppermute(x, 'mp', [(i, (i + step) % 4) for i in range(4)])  16.1 us
    ppermute x7, starting transfers between devices, grid_shift(): return lax.ppermute(v, 'dp', pairs)  11.1 us
    all_to_all x1, starting transfers between devices, body(): qslot = lax.all_to_all(qslot_out, 'dp', 0, 0, tiled=True)  7.45 us
    all_to_all x1, starting transfers between devices, body(): arrived = lax.all_to_all(rows, 'dp', 0, 0, tiled=True)  4.74 us
    all_to_all x1, starting transfers between devices, body(): recv = lax.all_to_all(sums, 'dp', 0, 0, tiled=True)  4.45 us
    unnamed x32, local copies, waits for them, and re-layouts  4.32 us
  transfers between devices with their start and end apart: 28, of which 12 were waited for; matrix products, arithmetic and copies ran while one was open for 1% of the time, Pallas kernels for 28%

profile of v4, /device:TPU:0, one launch (start us, length us, event | category | flops | bytes accessed | tf_op | source)
XLA Modules:
  0.0 137.5 jit_solution(12072753698190346936)
XLA Ops:
  0.6 2.5 %order_kernel.1 = (bf16[256,1024]{1,0:T(8,128)(2,1)}, bf16[256,1024]{1,0:T(8,128)(2,1)S(1)}) custom-call(bf16[512,1024]{1,0:T(8,128)(2,1)} %refs_4_.3), custom_call_target="tpu_custom_call" | custom-call | tf_op jit(solution)/shard_map/order_kernel/pallas_call | solution.py:641
  3.1 2.1 %collective-permute-start = (bf16[256,1024]{1,0:T(8,128)(2,1)}, bf16[256,1024]{1,0:T(8,128)(2,1)S(1)}, u32[]{:S(2)}, u32[]{:S(2)}) collective-permute-start(bf16[256,1024]{1,0:T(8,128)(2,1)} %get-tuple-element.68.refs_0_), channel_id=1, source_target_pairs={{0,1},{1,2},{2,3},{3,0},{4,5},{5,6},{6,7},{7,4},{8,9},{9,10},{10,1... | collective-permute-start | bytes 1572872 | tf_op jit(solution)/shard_map/leg1/ppermute | solution.py:668
  5.2 2.2 %collective-permute-start.2 = (bf16[256,1024]{1,0:T(8,128)(2,1)S(1)}, bf16[256,1024]{1,0:T(8,128)(2,1)S(1)}, u32[]{:S(2)}, u32[]{:S(2)}) collective-permute-start(bf16[256,1024]{1,0:T(8,128)(2,1)S(1)} %get-tuple-element.69.refs_1_), channel_id=1, source_target_pairs={{0,3},{1,0},{2,1},{3,2},{4,7},{5,4},{6,5},{7,6},{8,11},{9,8},{10,9... | collective-permute-start | bytes 1572872 | tf_op jit(solution)/shard_map/leg1/ppermute | solution.py:668
  7.4 1.9 %collective-permute-start.5 = (bf16[256,1024]{1,0:T(8,128)(2,1)}, bf16[256,1024]{1,0:T(8,128)(2,1)S(1)}, u32[]{:S(2)}, u32[]{:S(2)}) collective-permute-start(bf16[256,1024]{1,0:T(8,128)(2,1)} %get-tuple-element.68.refs_0_), channel_id=1, source_target_pairs={{0,3},{1,0},{2,1},{3,2},{4,7},{5,4},{6,5},{7,6},{8,11},{9,8},{10,9... | collective-permute-start | bytes 1572872 | tf_op jit(solution)/shard_map/leg2/ppermute | solution.py:668
  9.3 0.1 collective-permute-start.4
  9.4 0.8 copy.15
  10.2 0.1 reshape.38
  10.3 0.1 reshape.45.refs_1_
  10.5 0.8 copy-done.3
  11.3 3.6 %slot_kernel.1 = (bf16[768,1280]{1,0:T(8,128)(2,1)}, f32[40,1024]{1,0:T(8,128)}) custom-call(s32[1,640]{1,0:T(1,128)S(1)} %reshape.39.refs_0_, s32[640,1]{1,0:T(8,128)S(1)} %reshape.45.refs_1_, bf16[32,1024]{1,0:T(8,128)(2,1)S(1)} %copy-done.3), custom_call_target="tpu_custom_call" | custom-call | tf_op jit(solution)/shard_map/slot_kernel/pallas_call | solution.py:641
  14.9 7.4 %all-to-all-start = ((bf16[32,24,1280]{2,1,0:T(8,128)(2,1)}), bf16[32,24,1280]{2,1,0:T(8,128)(2,1)}, u32[]{:S(2)}, u32[]{:S(2)}) async-start(bf16[32,24,1280]{2,1,0:T(8,128)(2,1)} %bitcast.18), calls=%async_computation | async-start | bytes 3932160 | tf_op jit(solution)/shard_map/a2a_queries/all_to_all | solution.py:739
  22.4 0.1 collective-permute-start.1
  22.5 3.4 %collective-permute-start.3 = (bf16[256,1024]{1,0:T(8,128)(2,1)S(1)}, bf16[256,1024]{1,0:T(8,128)(2,1)S(1)}, u32[]{:S(2)}, u32[]{:S(2)}) collective-permute-start(bf16[256,1024]{1,0:T(8,128)(2,1)S(1)} %collective-permute-done.2.refs_3_), channel_id=1, source_target_pairs={{0,3},{1,0},{2,1},{3,2},{4,7},{5,4},{6,5},{7,6},{8,11},{9,8},{10,9... | collective-permute-start | bytes 1572872 | tf_op jit(solution)/shard_map/leg3/ppermute | solution.py:668
  25.9 1.2 copy-done.12
  27.1 4.2 %own_kernel.1 = (f32[512,1024]{1,0:T(8,128)S(1)}, f32[16,512]{1,0:T(8,128)S(1)}) custom-call(bf16[256,1024]{1,0:T(8,128)(2,1)} %get-tuple-element.68.refs_0_, bf16[256,1024]{1,0:T(8,128)(2,1)S(1)} %get-tuple-element.69.refs_1_, bf16[512,1024]{1,0:T(8,128)(2,1)S(1)} %copy-done.12, bf16[4096,1024]{1,0:T(8,128)(2,1)} %refs_1_.3, bf16[16,4096]{1,0:T(8,128)(2,1)S(1)} %bitcast.10), custom_call_target="tpu_custom_call" | custom-call | flops 17250000896 | tf_op jit(solution)/shard_map/own_kernel/pallas_call | solution.py:641
  31.3 0.2 collective-permute-done.4.refs_1_
  31.5 5.5 %sides_kernel.1 = (f32[512,1024]{1,0:T(8,128)}, f32[16,512]{1,0:T(8,128)S(1)}) custom-call(bf16[256,1024]{1,0:T(8,128)(2,1)S(1)} %collective-permute-done.refs_0_, bf16[256,1024]{1,0:T(8,128)(2,1)S(1)} %collective-permute-done.4.refs_1_, bf16[256,1024]{1,0:T(8,128)(2,1)S(1)} %collective-permute-done.5.refs_2_, ...), custom_call_target="tpu_custom_call" | custom-call | tf_op jit(solution)/shard_map/sides_kernel/pallas_call | solution.py:641
  37.0 4.9 %collective-permute-done.1.refs_0_ = bf16[256,1024]{1,0:T(8,128)(2,1)S(1)} collective-permute-done((bf16[256,1024]{1,0:T(8,128)(2,1)S(1)}, bf16[256,1024]{1,0:T(8,128)(2,1)S(1)}, u32[]{:S(2)}, u32[]{:S(2)}) %collective-permute-start.1) | collective-permute-done | bytes 524320 | tf_op jit(solution)/shard_map/leg3/ppermute | solution.py:668
  41.9 4.4 %far_kernel.1 = (f32[512,1024]{1,0:T(8,128)}, bf16[16,512]{1,0:T(8,128)(2,1)S(1)}, bf16[512,1024]{1,0:T(8,128)(2,1)S(1)}, f32[16,128]{1,0:T(8,128)S(1)}) custom-call(bf16[256,1024]{1,0:T(8,128)(2,1)S(1)} %collective-permute-done.1.refs_0_, bf16[256,1024]{1,0:T(8,128)(2,1)S(1)} %collective-permute-done.3.refs_1_, f32[512,1024]{1,0:T(8,128)} %get-tuple-element.75.refs_2_, ...), custom_call_target="tpu_custom_call" | custom-call | flops 4600000000 | tf_op jit(solution)/shard_map/far_kernel/pallas_call | solution.py:641
  46.4 1.0 copy-done.6
  47.3 2.5 %all-to-all-done = bf16[32,24,1280]{2,1,0:T(8,128)(2,1)} async-done(((bf16[32,24,1280]{2,1,0:T(8,128)(2,1)}), bf16[32,24,1280]{2,1,0:T(8,128)(2,1)}, u32[]{:S(2)}, u32[]{:S(2)}) %all-to-all-start) | async-done | bytes 1966112 | tf_op jit(solution)/shard_map/a2a_queries/all_to_all | solution.py:739
  49.8 2.8 %meta_kernel.1 = (bf16[1024,1152]{1,0:T(8,128)(2,1)S(1)}, f32[40,1024]{1,0:T(8,128)S(1)}, bf16[1024,1024]{1,0:T(8,128)(2,1)S(1)}) custom-call(bf16[768,1280]{1,0:T(8,128)(2,1)} %bitcast.3.refs_0_), custom_call_target="tpu_custom_call" | custom-call | tf_op jit(solution)/shard_map/meta_kernel/pallas_call | solution.py:641
  52.7 1.6 %partial_kernel.1.refs_0_ = f32[24,1024]{1,0:T(8,128)S(1)} custom-call(bf16[512,1024]{1,0:T(8,128)(2,1)S(1)} %copy-done.7, bf16[1024,1024]{1,0:T(8,128)(2,1)S(1)} %get-tuple-element.82.refs_1_, bf16[32,1024]{1,0:T(8,128)(2,1)S(1)} %copy-done.4, f32[40,1024]{1,0:T(8,128)S(1)} %get-tuple-element.83.refs_3_.refs_4_.refs_5_, f32[16,128]{1,0:T(8,128)S(1)} %get-tuple-element.84.refs_4_), custom_call_target="tpu_custom_call" | custom-call | tf_op jit(solution)/shard_map/partial_kernel/pallas_call | solution.py:641
  54.3 3.2 %collective-permute-start.8 = (f32[24,1024]{1,0:T(8,128)S(1)}, f32[24,1024]{1,0:T(8,128)S(1)}, u32[]{:S(2)}, u32[]{:S(2)}) collective-permute-start(f32[24,1024]{1,0:T(8,128)S(1)} %partial_kernel.1.refs_0_), channel_id=1, source_target_pairs={{0,3},{1,0},{2,1},{3,2},{4,7},{5,4},{6,5},{7,6},{8,11},{9,8},{10,9... | collective-permute-start | bytes 294920 | tf_op jit(solution)/shard_map/packs/ppermute | solution.py:668
  57.5 0.9 collective-permute-start.6
  58.4 3.1 %collective-permute-done.8.refs_3_ = f32[24,1024]{1,0:T(8,128)S(1)} collective-permute-done((f32[24,1024]{1,0:T(8,128)S(1)}, f32[24,1024]{1,0:T(8,128)S(1)}, u32[]{:S(2)}, u32[]{:S(2)}) %collective-permute-start.8) | collective-permute-done | bytes 98336 | tf_op jit(solution)/shard_map/packs/ppermute | solution.py:668
  61.5 2.8 %collective-permute-done.7.refs_2_ = f32[24,1024]{1,0:T(8,128)S(1)} collective-permute-done((f32[24,1024]{1,0:T(8,128)S(1)}, f32[24,1024]{1,0:T(8,128)S(1)}, u32[]{:S(2)}, u32[]{:S(2)}) %collective-permute-start.7) | collective-permute-done | bytes 98336 | tf_op jit(solution)/shard_map/packs/ppermute | solution.py:668
  64.2 0.7 collective-permute-done.6.refs_1_
  64.9 1.4 score_kernel.1
  66.3 4.5 %all-to-all-start.1 = ((f32[32,1,1280]{2,1,0:T(1,128)}), f32[32,1,1280]{2,1,0:T(1,128)S(1)}, u32[]{:S(2)}, u32[]{:S(2)}) async-start(f32[32,1,1280]{2,1,0:T(1,128)} %get-tuple-element.85), calls=%async_computation.1 | async-start | bytes 327680 | tf_op jit(solution)/shard_map/a2a_sums/all_to_all | solution.py:786
  70.7 3.2 %pooled_kernel.1 = (bf16[128,1024]{1,0:T(8,128)(2,1)S(1)}, bf16[768,1152]{1,0:T(8,128)(2,1)S(1)}) custom-call(f32[512,1024]{1,0:T(8,128)} %get-tuple-element.87.refs_0_.refs_1_, f32[16,128]{1,0:T(8,128)S(1)} %get-tuple-element.91.refs_1_.refs_8_, f32[1,1024]{1,0:T(1,128)S(1)} %bitcast.15, bf16[1024,1152]{1,0:T(8,128)(2,1)S(1)} %get-tuple-element.88.refs_3_.refs_2_), custom_call_target="tpu_custom_call" | custom-call | tf_op jit(solution)/shard_map/pooled_kernel/pallas_call | solution.py:641
  73.9 1.2 copy-done.1
  75.2 3.5 %all-to-all-done.1.refs_0_ = f32[32,1,1280]{2,1,0:T(1,128)S(1)} async-done(((f32[32,1,1280]{2,1,0:T(1,128)}), f32[32,1,1280]{2,1,0:T(1,128)S(1)}, u32[]{:S(2)}, u32[]{:S(2)}) %all-to-all-start.1) | async-done | bytes 163872 | tf_op jit(solution)/shard_map/a2a_sums/all_to_all | solution.py:786
  78.6 6.8 %gradient_kernel.1 = (bf16[512,1024]{1,0:T(8,128)(2,1)}, bf16[256,1024]{1,0:T(8,128)(2,1)}, bf16[256,1024]{1,0:T(8,128)(2,1)}, f32[16,512]{1,0:T(8,128)S(1)}, f32[32,384]{1,0:T(8,128)}, /*index=5*/f32[16,1024]{1,0:T(8,128)S(1)}) custom-call(f32[32,1,1280]{2,1,0:T(1,128)S(1)} %all-to-all-done.1.refs_0_, f32[512,1024]{1,0:T(8,128)} %get-tuple-element.87.refs_0_.refs_1_, ...), custom_call_target="tpu_custom_call" | custom-call | flops 1150000000 | tf_op jit(solution)/shard_map/gradient_kernel/pallas_call | solution.py:641
  85.4 0.0 copy-start
  85.5 0.1 collective-permute-start.12
  85.5 3.2 %collective-permute-start.13 = (bf16[256,1024]{1,0:T(8,128)(2,1)}, bf16[256,1024]{1,0:T(8,128)(2,1)S(1)}, u32[]{:S(2)}, u32[]{:S(2)}) collective-permute-start(bf16[256,1024]{1,0:T(8,128)(2,1)} %get-tuple-element.106), channel_id=1, source_target_pairs={{0,3},{1,0},{2,1},{3,2},{4,7},{5,4},{6,5},{7,6},{8,11},{9,8},{10,9... | collective-permute-start | bytes 1572872 | tf_op jit(solution)/shard_map/back1/ppermute | solution.py:668
  88.8 0.0 collective-permute-start.11
  88.8 0.9 collective-permute-start.10
  89.7 1.1 collective-permute-start.9
  90.8 4.7 %all-to-all-start.2 = ((bf16[32,24,1152]{2,1,0:T(8,128)(2,1)}), bf16[32,24,1152]{2,1,0:T(8,128)(2,1)}, u32[]{:S(2)}, u32[]{:S(2)}) async-start(bf16[32,24,1152]{2,1,0:T(8,128)(2,1)} %bitcast.9), calls=%async_computation.2 | async-start | bytes 3538944 | tf_op jit(solution)/shard_map/a2a_rows/all_to_all | solution.py:813
  95.6 5.1 %sides_back_kernel.1 = (bf16[256,1024]{1,0:T(8,128)(2,1)S(1)}, bf16[256,1024]{1,0:T(8,128)(2,1)S(1)}, bf16[256,1024]{1,0:T(8,128)(2,1)S(1)}, bf16[256,1024]{1,0:T(8,128)(2,1)S(1)}) custom-call(bf16[512,1024]{1,0:T(8,128)(2,1)S(1)} %copy-done, bf16[4096,1024]{1,0:T(8,128)(2,1)} %refs_1_.3), custom_call_target="tpu_custom_call" | custom-call | flops 1150000000 | tf_op jit(solution)/shard_map/sides_back_kernel/pallas_call | solution.py:641
  100.7 1.2 collective-permute-done.12.refs_2_
  102.0 1.5 %collective-permute-start.14 = (bf16[256,1024]{1,0:T(8,128)(2,1)S(1)}, bf16[256,1024]{1,0:T(8,128)(2,1)S(1)}, u32[]{:S(2)}, u32[]{:S(2)}) collective-permute-start(bf16[256,1024]{1,0:T(8,128)(2,1)S(1)} %get-tuple-element.112), channel_id=1, source_target_pairs={{0,3},{1,0},{2,1},{3,2},{4,7},{5,4},{6,5},{7,6},{8,11},{9,8},{10,9... | collective-permute-start | bytes 1572872 | tf_op jit(solution)/shard_map/back2/ppermute | solution.py:668
  103.4 0.6 collective-permute-start.15
  104.0 1.1 add_kernel.1
  105.1 1.0 collective-permute-start.23
  106.1 2.3 %collective-permute-start.24 = (bf16[256,1024]{1,0:T(8,128)(2,1)}, bf16[256,1024]{1,0:T(8,128)(2,1)}, u32[]{:S(2)}, u32[]{:S(2)}) collective-permute-start(bf16[256,1024]{1,0:T(8,128)(2,1)} %get-tuple-element.123), channel_id=1, source_target_pairs={{0,3},{1,0},{2,1},{3,2},{4,7},{5,4},{6,5},{7,6},{8,11},{9,8},{10,9... | collective-permute-start | bytes 1572872 | tf_op jit(solution)/shard_map/back3/ppermute | solution.py:668
  108.4 1.5 %join_kernel.1 = (bf16[32,1024]{1,0:T(8,128)(2,1)S(1)}, bf16[16,512]{1,0:T(8,128)(2,1)S(1)}) custom-call(f32[16,512]{1,0:T(8,128)S(1)} %get-tuple-element.102.refs_0_, f32[16,512]{1,0:T(8,128)S(1)} %collective-permute-done.9.refs_1_, f32[16,512]{1,0:T(8,128)S(1)} %collective-permute-done.10.refs_2_, f32[16,512]{1,0:T(8,128)S(1)} %collective-permute-done.11.refs_3_, ...), custom_call_target="tpu_custom_call" | custom-call | flops 18400000000 | tf_op jit(solution)/shard_map/join_kernel/pallas_call | solution.py:641
  109.9 0.1 collective-permute-start.16
  110.0 1.2 collective-permute-done.16.refs_1_
  111.2 2.8 %collective-permute-start.19 = (bf16[32,1024]{1,0:T(8,128)(2,1)S(1)}, bf16[32,1024]{1,0:T(8,128)(2,1)S(1)}, u32[]{:S(2)}, u32[]{:S(2)}) collective-permute-start(bf16[32,1024]{1,0:T(8,128)(2,1)S(1)} %pair_kernel.1.refs_0_), channel_id=1, source_target_pairs={{0,96},{4,100},{8,104},{12,108},{16,112},{20,116},{24,120},{28,124... | collective-permute-start | bytes 196616 | tf_op jit(solution)/shard_map/adapters/ppermute | solution.py:691
  114.0 2.8 %collective-permute-done.14.refs_4_ = bf16[256,1024]{1,0:T(8,128)(2,1)S(1)} collective-permute-done((bf16[256,1024]{1,0:T(8,128)(2,1)S(1)}, bf16[256,1024]{1,0:T(8,128)(2,1)S(1)}, u32[]{:S(2)}, u32[]{:S(2)}) %collective-permute-start.14) | collective-permute-done | bytes 524320 | tf_op jit(solution)/shard_map/back2/ppermute | solution.py:668
  116.8 2.1 %collective-permute-start.18 = (bf16[32,1024]{1,0:T(8,128)(2,1)S(1)}, bf16[32,1024]{1,0:T(8,128)(2,1)S(1)}, u32[]{:S(2)}, u32[]{:S(2)}) collective-permute-start(bf16[32,1024]{1,0:T(8,128)(2,1)S(1)} %pair_kernel.1.refs_0_), channel_id=1, source_target_pairs={{0,64},{4,68},{8,72},{12,76},{16,80},{20,84},{24,88},{28,92},{32,9... | collective-permute-start | bytes 196616 | tf_op jit(solution)/shard_map/adapters/ppermute | solution.py:691
  118.9 0.5 collective-permute-done.15.refs_5_
  119.4 1.6 %collective-permute-start.17 = (bf16[32,1024]{1,0:T(8,128)(2,1)S(1)}, bf16[32,1024]{1,0:T(8,128)(2,1)S(1)}, u32[]{:S(2)}, u32[]{:S(2)}) collective-permute-start(bf16[32,1024]{1,0:T(8,128)(2,1)S(1)} %pair_kernel.1.refs_0_), channel_id=1, source_target_pairs={{0,32},{4,36},{8,40},{12,44},{16,48},{20,52},{24,56},{28,60},{32,6... | collective-permute-start | bytes 196616 | tf_op jit(solution)/shard_map/adapters/ppermute | solution.py:691
  121.1 4.1 %own_back_kernel.1.refs_0_ = f32[512,1024]{1,0:T(8,128)S(1)} custom-call(bf16[512,1024]{1,0:T(8,128)(2,1)S(1)} %copy-done, bf16[4096,1024]{1,0:T(8,128)(2,1)} %refs_1_.3, bf16[16,4096]{1,0:T(8,128)(2,1)S(1)} %bitcast.13, bf16[16,512]{1,0:T(8,128)(2,1)S(1)} %get-tuple-element.111.refs_3_, bf16[256,1024]{1,0:T(8,128)(2,1)S(1)} %collective-permute-done.14.refs_4_, ...), custom_call_target="tpu_custom_call" | custom-call | tf_op jit(solution)/shard_map/own_back_kernel/pallas_call | solution.py:641
  125.3 2.8 %collective-permute-start.22 = (bf16[32,1024]{1,0:T(8,128)(2,1)S(1)}, bf16[32,1024]{1,0:T(8,128)(2,1)S(1)}, u32[]{:S(2)}, u32[]{:S(2)}) collective-permute-start(bf16[32,1024]{1,0:T(8,128)(2,1)S(1)} %four_kernel.1.refs_0_), channel_id=1, source_target_pairs={{0,24},{4,28},{8,0},{12,4},{16,8},{20,12},{24,16},{28,20},{32,56},... | collective-permute-start | bytes 196616 | tf_op jit(solution)/shard_map/adapters/ppermute | solution.py:691
  128.1 0.8 collective-permute-start.21
  128.9 0.9 collective-permute-start.20
  129.7 4.7 %query_kernel.1 = (bf16[32,1024]{1,0:T(8,128)(2,1)}, f32[1,32]{1,0:T(1,128)}) custom-call(f32[32,1,1280]{2,1,0:T(1,128)} %copy-done.2, f32[40,1024]{1,0:T(8,128)} %get-tuple-element.86.refs_1_, f32[32,384]{1,0:T(8,128)} %get-tuple-element.94.refs_2_, f32[32,896]{1,0:T(8,128)} %copy-done.9, bf16[128,1024]{1,0:T(8,128)(2,1)} %copy-done.5, ...), custom_call_target="tpu_custom_call" | custom-call | tf_op jit(solution)/shard_map/query_kernel/pallas_call | solution.py:641
  134.4 0.1 collective-permute-done.20.refs_1_
  134.5 0.7 last_kernel.1
  135.2 2.3 %finish_kernel.1 = bf16[512,1024]{1,0:T(8,128)(2,1)} custom-call(f32[512,1024]{1,0:T(8,128)S(1)} %own_back_kernel.1.refs_0_, bf16[256,1024]{1,0:T(8,128)(2,1)} %collective-permute-done.23.refs_1_, bf16[256,1024]{1,0:T(8,128)(2,1)} %collective-permute-done.24.refs_2_), custom_call_target="tpu_custom_call" | custom-call | tf_op jit(solution)/shard_map/finish_kernel/pallas_call | solution.py:641
  (49 shorter events, 0.2 us)
Async XLA Ops:
  3.1 19.3 %collective-permute-start = (bf16[256,1024]{1,0:T(8,128)(2,1)}, bf16[256,1024]{1,0:T(8,128)(2,1)S(1)}, u32[]{:S(2)}, u32[]{:S(2)}) collective-permute-start(bf16[256,1024]{1,0:T(8,128)(2,1)} %get-tuple-element.68.refs_0_), channel_id=1, source_target_pairs={{0,1},{1,2},{2,3},{3,0},{4,5},{5,6},{6,7},{7,4},{8,9},{9,10},{10,1... | collective-permute-start | bytes 1572872 | tf_op jit(solution)/shard_map/leg1/ppermute | solution.py:668
  5.2 17.2 %collective-permute-start.2 = (bf16[256,1024]{1,0:T(8,128)(2,1)S(1)}, bf16[256,1024]{1,0:T(8,128)(2,1)S(1)}, u32[]{:S(2)}, u32[]{:S(2)}) collective-permute-start(bf16[256,1024]{1,0:T(8,128)(2,1)S(1)} %get-tuple-element.69.refs_1_), channel_id=1, source_target_pairs={{0,3},{1,0},{2,1},{3,2},{4,7},{5,4},{6,5},{7,6},{8,11},{9,8},{10,9... | collective-permute-start | bytes 1572872 | tf_op jit(solution)/shard_map/leg1/ppermute | solution.py:668
  7.4 23.9 %collective-permute-start.5 = (bf16[256,1024]{1,0:T(8,128)(2,1)}, bf16[256,1024]{1,0:T(8,128)(2,1)S(1)}, u32[]{:S(2)}, u32[]{:S(2)}) collective-permute-start(bf16[256,1024]{1,0:T(8,128)(2,1)} %get-tuple-element.68.refs_0_), channel_id=1, source_target_pairs={{0,3},{1,0},{2,1},{3,2},{4,7},{5,4},{6,5},{7,6},{8,11},{9,8},{10,9... | collective-permute-start | bytes 1572872 | tf_op jit(solution)/shard_map/leg2/ppermute | solution.py:668
  9.3 22.2 %collective-permute-start.4 = (bf16[256,1024]{1,0:T(8,128)(2,1)S(1)}, bf16[256,1024]{1,0:T(8,128)(2,1)S(1)}, u32[]{:S(2)}, u32[]{:S(2)}) collective-permute-start(bf16[256,1024]{1,0:T(8,128)(2,1)S(1)} %get-tuple-element.69.refs_1_), channel_id=1, source_target_pairs={{0,1},{1,2},{2,3},{3,0},{4,5},{5,6},{6,7},{7,4},{8,9},{9,10},{10,1... | collective-permute-start | bytes 1572872 | tf_op jit(solution)/shard_map/leg2/ppermute | solution.py:668
  10.5 0.8 copy-start.3
  11.3 11.1 %copy-start.15 = (bf16[1024]{0:T(1024)(128)(2,1)S(1)}, bf16[1024]{0:T(1024)(128)(2,1)}, u32[]{:S(2)}) copy-start(bf16[1024]{0:T(1024)(128)(2,1)} %param.14) | copy-start | bytes 6148
  11.3 14.6 %copy-start.8 = (bf16[4096,16]{0,1:T(8,128)(2,1)S(1)}, bf16[4096,16]{0,1:T(8,128)(2,1)}, u32[]{:S(2)}) copy-start(bf16[4096,16]{0,1:T(8,128)(2,1)} %param.12) | copy-start | bytes 393220
  14.9 34.9 %all-to-all-start = ((bf16[32,24,1280]{2,1,0:T(8,128)(2,1)}), bf16[32,24,1280]{2,1,0:T(8,128)(2,1)}, u32[]{:S(2)}, u32[]{:S(2)}) async-start(bf16[32,24,1280]{2,1,0:T(8,128)(2,1)} %bitcast.18), calls=%async_computation | async-start | bytes 3932160 | tf_op jit(solution)/shard_map/a2a_queries/all_to_all | solution.py:739
  22.4 19.5 %collective-permute-start.1 = (bf16[256,1024]{1,0:T(8,128)(2,1)S(1)}, bf16[256,1024]{1,0:T(8,128)(2,1)S(1)}, u32[]{:S(2)}, u32[]{:S(2)}) collective-permute-start(bf16[256,1024]{1,0:T(8,128)(2,1)S(1)} %collective-permute-done.refs_0_), channel_id=1, source_target_pairs={{0,1},{1,2},{2,3},{3,0},{4,5},{5,6},{6,7},{7,4},{8,9},{9,10},{10,1... | collective-permute-start | bytes 1572872 | tf_op jit(solution)/shard_map/leg3/ppermute | solution.py:668
  22.5 19.4 %collective-permute-start.3 = (bf16[256,1024]{1,0:T(8,128)(2,1)S(1)}, bf16[256,1024]{1,0:T(8,128)(2,1)S(1)}, u32[]{:S(2)}, u32[]{:S(2)}) collective-permute-start(bf16[256,1024]{1,0:T(8,128)(2,1)S(1)} %collective-permute-done.2.refs_3_), channel_id=1, source_target_pairs={{0,3},{1,0},{2,1},{3,2},{4,7},{5,4},{6,5},{7,6},{8,11},{9,8},{10,9... | collective-permute-start | bytes 1572872 | tf_op jit(solution)/shard_map/leg3/ppermute | solution.py:668
  25.9 1.2 copy-start.12
  31.5 10.4 %copy-start.10 = (bf16[16,1024]{1,0:T(8,128)(2,1)S(1)}, bf16[16,1024]{1,0:T(8,128)(2,1)}, u32[]{:S(2)}) copy-start(bf16[16,1024]{1,0:T(8,128)(2,1)} %refs_10_.1) | copy-start | bytes 98308
  41.9 10.7 %copy-start.4 = (bf16[32,1024]{1,0:T(8,128)(2,1)S(1)}, bf16[32,1024]{1,0:T(8,128)(2,1)}, u32[]{:S(2)}) copy-start(bf16[32,1024]{1,0:T(8,128)(2,1)} %refs_5_.1) | copy-start | bytes 196612
  46.4 1.0 copy-start.6
  49.8 2.8 %copy-start.7 = (bf16[512,1024]{1,0:T(8,128)(2,1)S(1)}, bf16[512,1024]{1,0:T(8,128)(2,1)}, u32[]{:S(2)}) copy-start(bf16[512,1024]{1,0:T(8,128)(2,1)} %copy-done.6) | copy-start | bytes 3145732
  52.6 12.3 %copy-start.11 = (s32[128]{0:T(128)S(1)}, s32[128]{0:T(128)}, u32[]{:S(2)}) copy-start(s32[128]{0:T(128)} %param.17) | copy-start | bytes 1540
  54.3 7.2 %collective-permute-start.8 = (f32[24,1024]{1,0:T(8,128)S(1)}, f32[24,1024]{1,0:T(8,128)S(1)}, u32[]{:S(2)}, u32[]{:S(2)}) collective-permute-start(f32[24,1024]{1,0:T(8,128)S(1)} %partial_kernel.1.refs_0_), channel_id=1, source_target_pairs={{0,3},{1,0},{2,1},{3,2},{4,7},{5,4},{6,5},{7,6},{8,11},{9,8},{10,9... | collective-permute-start | bytes 294920 | tf_op jit(solution)/shard_map/packs/ppermute | solution.py:668
  57.5 6.8 %collective-permute-start.7 = (f32[24,1024]{1,0:T(8,128)S(1)}, f32[24,1024]{1,0:T(8,128)S(1)}, u32[]{:S(2)}, u32[]{:S(2)}) collective-permute-start(f32[24,1024]{1,0:T(8,128)S(1)} %partial_kernel.1.refs_0_), channel_id=1, source_target_pairs={{0,2},{1,3},{2,0},{3,1},{4,6},{5,7},{6,4},{7,5},{8,10},{9,11},{10,... | collective-permute-start | bytes 294920 | tf_op jit(solution)/shard_map/packs/ppermute | solution.py:668
  57.5 7.4 %collective-permute-start.6 = (f32[24,1024]{1,0:T(8,128)S(1)}, f32[24,1024]{1,0:T(8,128)S(1)}, u32[]{:S(2)}, u32[]{:S(2)}) collective-permute-start(f32[24,1024]{1,0:T(8,128)S(1)} %partial_kernel.1.refs_0_), channel_id=1, source_target_pairs={{0,1},{1,2},{2,3},{3,0},{4,5},{5,6},{6,7},{7,4},{8,9},{9,10},{10,1... | collective-permute-start | bytes 294920 | tf_op jit(solution)/shard_map/packs/ppermute | solution.py:668
  66.3 12.4 %copy-start.9 = (f32[32,896]{1,0:T(8,128)}, f32[32,896]{1,0:T(8,128)S(1)}, u32[]{:S(2)}) copy-start(f32[32,896]{1,0:T(8,128)S(1)} %get-tuple-element.90.refs_7_.refs_3_) | copy-start | bytes 344068
  66.3 12.4 %all-to-all-start.1 = ((f32[32,1,1280]{2,1,0:T(1,128)}), f32[32,1,1280]{2,1,0:T(1,128)S(1)}, u32[]{:S(2)}, u32[]{:S(2)}) async-start(f32[32,1,1280]{2,1,0:T(1,128)} %get-tuple-element.85), calls=%async_computation.1 | async-start | bytes 327680 | tf_op jit(solution)/shard_map/a2a_sums/all_to_all | solution.py:786
  73.9 1.2 copy-start.1
  75.2 10.2 %copy-start.5 = (bf16[128,1024]{1,0:T(8,128)(2,1)}, bf16[128,1024]{1,0:T(8,128)(2,1)S(1)}, u32[]{:S(2)}) copy-start(bf16[128,1024]{1,0:T(8,128)(2,1)S(1)} %get-tuple-element.92.refs_9_.refs_4_) | copy-start | bytes 786436
  78.6 6.8 %copy-start.2 = (f32[32,1,1280]{2,1,0:T(1,128)}, f32[32,1,1280]{2,1,0:T(1,128)S(1)}, u32[]{:S(2)}) copy-start(f32[32,1,1280]{2,1,0:T(1,128)S(1)} %all-to-all-done.1.refs_0_) | copy-start | bytes 491524
  85.4 10.1 %copy-start.13 = (f32[16,1024]{1,0:T(8,128)}, f32[16,1024]{1,0:T(8,128)S(1)}, u32[]{:S(2)}) copy-start(f32[16,1024]{1,0:T(8,128)S(1)} %get-tuple-element.110.refs_5_) | copy-start | bytes 196612
  85.4 10.1 %copy-start = (bf16[512,1024]{1,0:T(8,128)(2,1)S(1)}, bf16[512,1024]{1,0:T(8,128)(2,1)}, u32[]{:S(2)}) copy-start(bf16[512,1024]{1,0:T(8,128)(2,1)} %get-tuple-element.64.refs_0_) | copy-start | bytes 3145732
  85.5 16.5 %collective-permute-start.12 = (bf16[256,1024]{1,0:T(8,128)(2,1)}, bf16[256,1024]{1,0:T(8,128)(2,1)S(1)}, u32[]{:S(2)}, u32[]{:S(2)}) collective-permute-start(bf16[256,1024]{1,0:T(8,128)(2,1)} %get-tuple-element.105), channel_id=1, source_target_pairs={{0,1},{1,2},{2,3},{3,0},{4,5},{5,6},{6,7},{7,4},{8,9},{9,10},{10,1... | collective-permute-start | bytes 1572872 | tf_op jit(solution)/shard_map/back1/ppermute | solution.py:668
  85.5 17.9 %collective-permute-start.13 = (bf16[256,1024]{1,0:T(8,128)(2,1)}, bf16[256,1024]{1,0:T(8,128)(2,1)S(1)}, u32[]{:S(2)}, u32[]{:S(2)}) collective-permute-start(bf16[256,1024]{1,0:T(8,128)(2,1)} %get-tuple-element.106), channel_id=1, source_target_pairs={{0,3},{1,0},{2,1},{3,2},{4,7},{5,4},{6,5},{7,6},{8,11},{9,8},{10,9... | collective-permute-start | bytes 1572872 | tf_op jit(solution)/shard_map/back1/ppermute | solution.py:668
  88.8 16.4 %collective-permute-start.11 = (f32[16,512]{1,0:T(8,128)S(1)}, f32[16,512]{1,0:T(8,128)S(1)}, u32[]{:S(2)}, u32[]{:S(2)}) collective-permute-start(f32[16,512]{1,0:T(8,128)S(1)} %get-tuple-element.102.refs_0_), channel_id=1, source_target_pairs={{0,3},{1,0},{2,1},{3,2},{4,7},{5,4},{6,5},{7,6},{8,11},{9,8},{10,9... | collective-permute-start | bytes 98312 | tf_op jit(solution)/shard_map/lora_sum/ppermute | solution.py:668
  88.8 17.3 %collective-permute-start.10 = (f32[16,512]{1,0:T(8,128)S(1)}, f32[16,512]{1,0:T(8,128)S(1)}, u32[]{:S(2)}, u32[]{:S(2)}) collective-permute-start(f32[16,512]{1,0:T(8,128)S(1)} %get-tuple-element.102.refs_0_), channel_id=1, source_target_pairs={{0,2},{1,3},{2,0},{3,1},{4,6},{5,7},{6,4},{7,5},{8,10},{9,11},{10,... | collective-permute-start | bytes 98312 | tf_op jit(solution)/shard_map/lora_sum/ppermute | solution.py:668
  89.7 18.7 %collective-permute-start.9 = (f32[16,512]{1,0:T(8,128)S(1)}, f32[16,512]{1,0:T(8,128)S(1)}, u32[]{:S(2)}, u32[]{:S(2)}) collective-permute-start(f32[16,512]{1,0:T(8,128)S(1)} %get-tuple-element.102.refs_0_), channel_id=1, source_target_pairs={{0,1},{1,2},{2,3},{3,0},{4,5},{5,6},{6,7},{7,4},{8,9},{9,10},{10,1... | collective-permute-start | bytes 98312 | tf_op jit(solution)/shard_map/lora_sum/ppermute | solution.py:668
  90.8 38.9 %all-to-all-start.2 = ((bf16[32,24,1152]{2,1,0:T(8,128)(2,1)}), bf16[32,24,1152]{2,1,0:T(8,128)(2,1)}, u32[]{:S(2)}, u32[]{:S(2)}) async-start(bf16[32,24,1152]{2,1,0:T(8,128)(2,1)} %bitcast.9), calls=%async_computation.2 | async-start | bytes 3538944 | tf_op jit(solution)/shard_map/a2a_rows/all_to_all | solution.py:813
  100.7 7.7 %copy-start.14 = (f32[16,1024]{1,0:T(8,128)S(1)}, f32[16,1024]{1,0:T(8,128)}, u32[]{:S(2)}) copy-start(f32[16,1024]{1,0:T(8,128)} %copy-done.13) | copy-start | bytes 196612
  102.0 14.9 %collective-permute-start.14 = (bf16[256,1024]{1,0:T(8,128)(2,1)S(1)}, bf16[256,1024]{1,0:T(8,128)(2,1)S(1)}, u32[]{:S(2)}, u32[]{:S(2)}) collective-permute-start(bf16[256,1024]{1,0:T(8,128)(2,1)S(1)} %get-tuple-element.112), channel_id=1, source_target_pairs={{0,3},{1,0},{2,1},{3,2},{4,7},{5,4},{6,5},{7,6},{8,11},{9,8},{10,9... | collective-permute-start | bytes 1572872 | tf_op jit(solution)/shard_map/back2/ppermute | solution.py:668
  103.4 16.0 %collective-permute-start.15 = (bf16[256,1024]{1,0:T(8,128)(2,1)S(1)}, bf16[256,1024]{1,0:T(8,128)(2,1)S(1)}, u32[]{:S(2)}, u32[]{:S(2)}) collective-permute-start(bf16[256,1024]{1,0:T(8,128)(2,1)S(1)} %get-tuple-element.113), channel_id=1, source_target_pairs={{0,1},{1,2},{2,3},{3,0},{4,5},{5,6},{6,7},{7,4},{8,9},{9,10},{10,1... | collective-permute-start | bytes 1572872 | tf_op jit(solution)/shard_map/back2/ppermute | solution.py:668
  105.1 30.1 %collective-permute-start.23 = (bf16[256,1024]{1,0:T(8,128)(2,1)}, bf16[256,1024]{1,0:T(8,128)(2,1)}, u32[]{:S(2)}, u32[]{:S(2)}) collective-permute-start(bf16[256,1024]{1,0:T(8,128)(2,1)} %get-tuple-element.122), channel_id=1, source_target_pairs={{0,1},{1,2},{2,3},{3,0},{4,5},{5,6},{6,7},{7,4},{8,9},{9,10},{10,1... | collective-permute-start | bytes 1572872 | tf_op jit(solution)/shard_map/back3/ppermute | solution.py:668
  106.1 29.1 %collective-permute-start.24 = (bf16[256,1024]{1,0:T(8,128)(2,1)}, bf16[256,1024]{1,0:T(8,128)(2,1)}, u32[]{:S(2)}, u32[]{:S(2)}) collective-permute-start(bf16[256,1024]{1,0:T(8,128)(2,1)} %get-tuple-element.123), channel_id=1, source_target_pairs={{0,3},{1,0},{2,1},{3,2},{4,7},{5,4},{6,5},{7,6},{8,11},{9,8},{10,9... | collective-permute-start | bytes 1572872 | tf_op jit(solution)/shard_map/back3/ppermute | solution.py:668
  109.9 1.3 collective-permute-start.16
  111.2 14.0 %collective-permute-start.19 = (bf16[32,1024]{1,0:T(8,128)(2,1)S(1)}, bf16[32,1024]{1,0:T(8,128)(2,1)S(1)}, u32[]{:S(2)}, u32[]{:S(2)}) collective-permute-start(bf16[32,1024]{1,0:T(8,128)(2,1)S(1)} %pair_kernel.1.refs_0_), channel_id=1, source_target_pairs={{0,96},{4,100},{8,104},{12,108},{16,112},{20,116},{24,120},{28,124... | collective-permute-start | bytes 196616 | tf_op jit(solution)/shard_map/adapters/ppermute | solution.py:691
  116.8 8.4 %collective-permute-start.18 = (bf16[32,1024]{1,0:T(8,128)(2,1)S(1)}, bf16[32,1024]{1,0:T(8,128)(2,1)S(1)}, u32[]{:S(2)}, u32[]{:S(2)}) collective-permute-start(bf16[32,1024]{1,0:T(8,128)(2,1)S(1)} %pair_kernel.1.refs_0_), channel_id=1, source_target_pairs={{0,64},{4,68},{8,72},{12,76},{16,80},{20,84},{24,88},{28,92},{32,9... | collective-permute-start | bytes 196616 | tf_op jit(solution)/shard_map/adapters/ppermute | solution.py:691
  119.4 5.8 %collective-permute-start.17 = (bf16[32,1024]{1,0:T(8,128)(2,1)S(1)}, bf16[32,1024]{1,0:T(8,128)(2,1)S(1)}, u32[]{:S(2)}, u32[]{:S(2)}) collective-permute-start(bf16[32,1024]{1,0:T(8,128)(2,1)S(1)} %pair_kernel.1.refs_0_), channel_id=1, source_target_pairs={{0,32},{4,36},{8,40},{12,44},{16,48},{20,52},{24,56},{28,60},{32,6... | collective-permute-start | bytes 196616 | tf_op jit(solution)/shard_map/adapters/ppermute | solution.py:691
  125.3 9.2 %collective-permute-start.22 = (bf16[32,1024]{1,0:T(8,128)(2,1)S(1)}, bf16[32,1024]{1,0:T(8,128)(2,1)S(1)}, u32[]{:S(2)}, u32[]{:S(2)}) collective-permute-start(bf16[32,1024]{1,0:T(8,128)(2,1)S(1)} %four_kernel.1.refs_0_), channel_id=1, source_target_pairs={{0,24},{4,28},{8,0},{12,4},{16,8},{20,12},{24,16},{28,20},{32,56},... | collective-permute-start | bytes 196616 | tf_op jit(solution)/shard_map/adapters/ppermute | solution.py:691
  128.1 6.4 %collective-permute-start.21 = (bf16[32,1024]{1,0:T(8,128)(2,1)S(1)}, bf16[32,1024]{1,0:T(8,128)(2,1)S(1)}, u32[]{:S(2)}, u32[]{:S(2)}) collective-permute-start(bf16[32,1024]{1,0:T(8,128)(2,1)S(1)} %four_kernel.1.refs_0_), channel_id=1, source_target_pairs={{0,16},{4,20},{8,24},{12,28},{16,0},{20,4},{24,8},{28,12},{32,48},... | collective-permute-start | bytes 196616 | tf_op jit(solution)/shard_map/adapters/ppermute | solution.py:691
  128.9 5.6 %collective-permute-start.20 = (bf16[32,1024]{1,0:T(8,128)(2,1)S(1)}, bf16[32,1024]{1,0:T(8,128)(2,1)S(1)}, u32[]{:S(2)}, u32[]{:S(2)}) collective-permute-start(bf16[32,1024]{1,0:T(8,128)(2,1)S(1)} %four_kernel.1.refs_0_), channel_id=1, source_target_pairs={{0,8},{4,12},{8,16},{12,20},{16,24},{20,28},{24,0},{28,4},{32,40},... | collective-permute-start | bytes 196616 | tf_op jit(solution)/shard_map/adapters/ppermute | solution.py:691

commit v5 on v4

--- a/solution.py
+++ b/solution.py
@@ -528,8 +528,8 @@
 
 
 def finish_kernel(before, from_left, from_right, out):
-    out[0:256, :] = (before[0:256, :] + from_left[...].astype(F32)).astype(BF16)
-    out[256:512, :] = (before[256:512, :] + from_right[...].astype(F32)).astype(BF16)
+    out[0:256, :] = (before[0:256, :].astype(F32) + from_left[...].astype(F32)).astype(BF16)
+    out[256:512, :] = (before[256:512, :].astype(F32) + from_right[...].astype(F32)).astype(BF16)
 
 
 def own_back_kernel(
@@ -544,8 +544,8 @@
         fetch.wait(k)
         lanes = slice(k * 256, k * 256 + 256)
         own = local[:, lanes] + dot(grad[...], buffer[k * 256 : k * 256 + 256, :], ((1,), (1,)))
-        out[0:256, lanes] = own[0:256] + from_right[:, lanes].astype(F32)
-        out[256:512, lanes] = own[256:512] + from_left[:, lanes].astype(F32)
+        out[0:256, lanes] = (own[0:256] + from_right[:, lanes].astype(F32)).astype(BF16)
+        out[256:512, lanes] = (own[256:512] + from_left[:, lanes].astype(F32)).astype(BF16)
 
 
 def query_kernel(
@@ -837,7 +837,7 @@
         to_right_top, to_left_low = ring(right_top, 1), ring(left_low, 3)
     (before,) = call(
         own_back_kernel,
-        [(full, F32)],
+        [(full, BF16)],
         [(grad, ANY), weight, down, lora_back, to_left_top, to_right_low],
         [WEIGHT_BUFFER, FOUR, pltpu.VMEM(full, BF16), FOUR],
         limit=24,

time: 138 us -> 139 us (level)
  starting transfers between devices: 52.3 us -> 49.9 us
  local copies, waits for them, and re-layouts: 5.35 us -> 6.91 us
    ppermute x7, starting transfers between devices: 11.1 us -> 9.55 us  [grid_shift(): return lax.ppermute(v, 'dp', pairs)]
    unnamed x32 -> x36, local copies, waits for them, and re-layouts: 4.32 us -> 5.89 us
    ppermute x7, waiting for transfers between devices: 1.34 us -> 2.82 us  [grid_shift(): return lax.ppermute(v, 'dp', pairs)]
  transfers between devices with their start and end apart: 28 -> 28, of which waited for: 12 -> 13; matrix products, arithmetic and copies ran while one was open for 1% -> 1% of each run, Pallas kernels for 28% -> 28%
where the time goes in v5:
time: 139 us; the launch traced here: 138 us
  Pallas kernels  56 us (40%)
  starting transfers between devices  49.9 us (36%)
  waiting for transfers between devices  24.6 us (18%)
  local copies, waits for them, and re-layouts  6.91 us (5%)
    pallas_call x19, Pallas kernels, call(): pl.pallas_call(whole, cost_estimate=cost, name=kernel.__name__, out_shape...  56 us
    ppermute x18, starting transfers between devices, ring(): return lax.ppermute(x, 'mp', [(i, (i + step) % 4) for i in range(4)])  24.5 us
    ppermute x18, waiting for transfers between devices, ring(): return lax.ppermute(x, 'mp', [(i, (i + step) % 4) for i in range(4)])  15.8 us
    ppermute x7, starting transfers between devices, grid_shift(): return lax.ppermute(v, 'dp', pairs)  9.55 us
    all_to_all x1, starting transfers between devices, body(): qslot = lax.all_to_all(qslot_out, 'dp', 0, 0, tiled=True)  7.45 us
    unnamed x36, local copies, waits for them, and re-layouts  5.89 us
    all_to_all x1, starting transfers between devices, body(): recv = lax.all_to_all(sums, 'dp', 0, 0, tiled=True)  4.48 us
    all_to_all x1, starting transfers between devices, body(): arrived = lax.all_to_all(rows, 'dp', 0, 0, tiled=True)  3.98 us
  transfers between devices with their start and end apart: 28, of which 13 were waited for; matrix products, arithmetic and copies ran while one was open for 1% of the time, Pallas kernels for 28%

profile of v5, /device:TPU:0, one launch (start us, length us, event | category | flops | bytes accessed | tf_op | source)
XLA Modules:
  0.0 138.4 jit_solution(3356310256410292352)
XLA Ops:
  0.6 2.5 %order_kernel.1 = (bf16[256,1024]{1,0:T(8,128)(2,1)}, bf16[256,1024]{1,0:T(8,128)(2,1)S(1)}) custom-call(bf16[512,1024]{1,0:T(8,128)(2,1)} %refs_4_.3), custom_call_target="tpu_custom_call" | custom-call | tf_op jit(solution)/shard_map/order_kernel/pallas_call | solution.py:641
  3.1 2.1 %collective-permute-start = (bf16[256,1024]{1,0:T(8,128)(2,1)}, bf16[256,1024]{1,0:T(8,128)(2,1)S(1)}, u32[]{:S(2)}, u32[]{:S(2)}) collective-permute-start(bf16[256,1024]{1,0:T(8,128)(2,1)} %get-tuple-element.68.refs_0_), channel_id=1, source_target_pairs={{0,1},{1,2},{2,3},{3,0},{4,5},{5,6},{6,7},{7,4},{8,9},{9,10},{10,1... | collective-permute-start | bytes 1572872 | tf_op jit(solution)/shard_map/leg1/ppermute | solution.py:668
  5.2 2.2 %collective-permute-start.2 = (bf16[256,1024]{1,0:T(8,128)(2,1)S(1)}, bf16[256,1024]{1,0:T(8,128)(2,1)S(1)}, u32[]{:S(2)}, u32[]{:S(2)}) collective-permute-start(bf16[256,1024]{1,0:T(8,128)(2,1)S(1)} %get-tuple-element.69.refs_1_), channel_id=1, source_target_pairs={{0,3},{1,0},{2,1},{3,2},{4,7},{5,4},{6,5},{7,6},{8,11},{9,8},{10,9... | collective-permute-start | bytes 1572872 | tf_op jit(solution)/shard_map/leg1/ppermute | solution.py:668
  7.4 1.9 %collective-permute-start.5 = (bf16[256,1024]{1,0:T(8,128)(2,1)}, bf16[256,1024]{1,0:T(8,128)(2,1)S(1)}, u32[]{:S(2)}, u32[]{:S(2)}) collective-permute-start(bf16[256,1024]{1,0:T(8,128)(2,1)} %get-tuple-element.68.refs_0_), channel_id=1, source_target_pairs={{0,3},{1,0},{2,1},{3,2},{4,7},{5,4},{6,5},{7,6},{8,11},{9,8},{10,9... | collective-permute-start | bytes 1572872 | tf_op jit(solution)/shard_map/leg2/ppermute | solution.py:668
  9.3 0.1 collective-permute-start.4
  9.4 0.8 copy.15
  10.2 0.1 reshape.38
  10.3 0.1 reshape.45.refs_1_
  10.5 0.8 copy-done.5
  11.3 3.6 %slot_kernel.1 = (bf16[768,1280]{1,0:T(8,128)(2,1)}, f32[40,1024]{1,0:T(8,128)}) custom-call(s32[1,640]{1,0:T(1,128)S(1)} %reshape.39.refs_0_, s32[640,1]{1,0:T(8,128)S(1)} %reshape.45.refs_1_, bf16[32,1024]{1,0:T(8,128)(2,1)S(1)} %copy-done.5), custom_call_target="tpu_custom_call" | custom-call | tf_op jit(solution)/shard_map/slot_kernel/pallas_call | solution.py:641
  14.9 7.4 %all-to-all-start = ((bf16[32,24,1280]{2,1,0:T(8,128)(2,1)}), bf16[32,24,1280]{2,1,0:T(8,128)(2,1)}, u32[]{:S(2)}, u32[]{:S(2)}) async-start(bf16[32,24,1280]{2,1,0:T(8,128)(2,1)} %bitcast.19), calls=%async_computation | async-start | bytes 3932160 | tf_op jit(solution)/shard_map/a2a_queries/all_to_all | solution.py:739
  22.4 0.1 collective-permute-start.1
  22.5 3.4 %collective-permute-start.3 = (bf16[256,1024]{1,0:T(8,128)(2,1)S(1)}, bf16[256,1024]{1,0:T(8,128)(2,1)S(1)}, u32[]{:S(2)}, u32[]{:S(2)}) collective-permute-start(bf16[256,1024]{1,0:T(8,128)(2,1)S(1)} %collective-permute-done.2.refs_3_), channel_id=1, source_target_pairs={{0,3},{1,0},{2,1},{3,2},{4,7},{5,4},{6,5},{7,6},{8,11},{9,8},{10,9... | collective-permute-start | bytes 1572872 | tf_op jit(solution)/shard_map/leg3/ppermute | solution.py:668
  25.9 1.2 copy-done.14
  27.1 4.2 %own_kernel.1 = (f32[512,1024]{1,0:T(8,128)S(1)}, f32[16,512]{1,0:T(8,128)S(1)}) custom-call(bf16[256,1024]{1,0:T(8,128)(2,1)} %get-tuple-element.68.refs_0_, bf16[256,1024]{1,0:T(8,128)(2,1)S(1)} %get-tuple-element.69.refs_1_, bf16[512,1024]{1,0:T(8,128)(2,1)S(1)} %copy-done.14, bf16[4096,1024]{1,0:T(8,128)(2,1)} %refs_1_.3, bf16[16,4096]{1,0:T(8,128)(2,1)S(1)} %bitcast.11), custom_call_target="tpu_custom_call" | custom-call | flops 17250000896 | tf_op jit(solution)/shard_map/own_kernel/pallas_call | solution.py:641
  31.3 0.2 collective-permute-done.4.refs_1_
  31.5 5.5 %sides_kernel.1 = (f32[512,1024]{1,0:T(8,128)}, f32[16,512]{1,0:T(8,128)S(1)}) custom-call(bf16[256,1024]{1,0:T(8,128)(2,1)S(1)} %collective-permute-done.refs_0_, bf16[256,1024]{1,0:T(8,128)(2,1)S(1)} %collective-permute-done.4.refs_1_, bf16[256,1024]{1,0:T(8,128)(2,1)S(1)} %collective-permute-done.5.refs_2_, ...), custom_call_target="tpu_custom_call" | custom-call | tf_op jit(solution)/shard_map/sides_kernel/pallas_call | solution.py:641
  37.0 4.9 %collective-permute-done.1.refs_0_ = bf16[256,1024]{1,0:T(8,128)(2,1)S(1)} collective-permute-done((bf16[256,1024]{1,0:T(8,128)(2,1)S(1)}, bf16[256,1024]{1,0:T(8,128)(2,1)S(1)}, u32[]{:S(2)}, u32[]{:S(2)}) %collective-permute-start.1) | collective-permute-done | bytes 524320 | tf_op jit(solution)/shard_map/leg3/ppermute | solution.py:668
  41.9 4.4 %far_kernel.1 = (f32[512,1024]{1,0:T(8,128)}, bf16[16,512]{1,0:T(8,128)(2,1)S(1)}, bf16[512,1024]{1,0:T(8,128)(2,1)S(1)}, f32[16,128]{1,0:T(8,128)S(1)}) custom-call(bf16[256,1024]{1,0:T(8,128)(2,1)S(1)} %collective-permute-done.1.refs_0_, bf16[256,1024]{1,0:T(8,128)(2,1)S(1)} %collective-permute-done.3.refs_1_, f32[512,1024]{1,0:T(8,128)} %get-tuple-element.75.refs_2_, ...), custom_call_target="tpu_custom_call" | custom-call | flops 4600000000 | tf_op jit(solution)/shard_map/far_kernel/pallas_call | solution.py:641
  46.4 1.0 copy-done.8
  47.3 2.5 %all-to-all-done = bf16[32,24,1280]{2,1,0:T(8,128)(2,1)} async-done(((bf16[32,24,1280]{2,1,0:T(8,128)(2,1)}), bf16[32,24,1280]{2,1,0:T(8,128)(2,1)}, u32[]{:S(2)}, u32[]{:S(2)}) %all-to-all-start) | async-done | bytes 1966112 | tf_op jit(solution)/shard_map/a2a_queries/all_to_all | solution.py:739
  49.8 2.8 %meta_kernel.1 = (bf16[1024,1152]{1,0:T(8,128)(2,1)S(1)}, f32[40,1024]{1,0:T(8,128)S(1)}, bf16[1024,1024]{1,0:T(8,128)(2,1)S(1)}) custom-call(bf16[768,1280]{1,0:T(8,128)(2,1)} %bitcast.3.refs_0_), custom_call_target="tpu_custom_call" | custom-call | tf_op jit(solution)/shard_map/meta_kernel/pallas_call | solution.py:641
  52.6 1.6 %partial_kernel.1.refs_0_ = f32[24,1024]{1,0:T(8,128)S(1)} custom-call(bf16[512,1024]{1,0:T(8,128)(2,1)S(1)} %copy-done.9, bf16[1024,1024]{1,0:T(8,128)(2,1)S(1)} %get-tuple-element.82.refs_1_, bf16[32,1024]{1,0:T(8,128)(2,1)S(1)} %copy-done.6, f32[40,1024]{1,0:T(8,128)S(1)} %get-tuple-element.83.refs_3_.refs_4_.refs_5_, f32[16,128]{1,0:T(8,128)S(1)} %get-tuple-element.84.refs_4_), custom_call_target="tpu_custom_call" | custom-call | tf_op jit(solution)/shard_map/partial_kernel/pallas_call | solution.py:641
  54.2 3.2 %collective-permute-start.8 = (f32[24,1024]{1,0:T(8,128)S(1)}, f32[24,1024]{1,0:T(8,128)S(1)}, u32[]{:S(2)}, u32[]{:S(2)}) collective-permute-start(f32[24,1024]{1,0:T(8,128)S(1)} %partial_kernel.1.refs_0_), channel_id=1, source_target_pairs={{0,3},{1,0},{2,1},{3,2},{4,7},{5,4},{6,5},{7,6},{8,11},{9,8},{10,9... | collective-permute-start | bytes 294920 | tf_op jit(solution)/shard_map/packs/ppermute | solution.py:668
  57.5 0.9 collective-permute-start.6
  58.4 3.1 %collective-permute-done.8.refs_3_ = f32[24,1024]{1,0:T(8,128)S(1)} collective-permute-done((f32[24,1024]{1,0:T(8,128)S(1)}, f32[24,1024]{1,0:T(8,128)S(1)}, u32[]{:S(2)}, u32[]{:S(2)}) %collective-permute-start.8) | collective-permute-done | bytes 98336 | tf_op jit(solution)/shard_map/packs/ppermute | solution.py:668
  61.5 2.8 %collective-permute-done.7.refs_2_ = f32[24,1024]{1,0:T(8,128)S(1)} collective-permute-done((f32[24,1024]{1,0:T(8,128)S(1)}, f32[24,1024]{1,0:T(8,128)S(1)}, u32[]{:S(2)}, u32[]{:S(2)}) %collective-permute-start.7) | collective-permute-done | bytes 98336 | tf_op jit(solution)/shard_map/packs/ppermute | solution.py:668
  64.2 0.7 collective-permute-done.6.refs_1_
  64.9 1.4 score_kernel.1
  66.3 4.5 %all-to-all-start.1 = ((f32[32,1,1280]{2,1,0:T(1,128)}), f32[32,1,1280]{2,1,0:T(1,128)S(1)}, u32[]{:S(2)}, u32[]{:S(2)}) async-start(f32[32,1,1280]{2,1,0:T(1,128)} %get-tuple-element.85), calls=%async_computation.1 | async-start | bytes 327680 | tf_op jit(solution)/shard_map/a2a_sums/all_to_all | solution.py:786
  70.8 3.2 %pooled_kernel.1 = (bf16[128,1024]{1,0:T(8,128)(2,1)S(1)}, bf16[768,1152]{1,0:T(8,128)(2,1)S(1)}) custom-call(f32[512,1024]{1,0:T(8,128)} %get-tuple-element.87.refs_0_.refs_1_, f32[16,128]{1,0:T(8,128)S(1)} %get-tuple-element.91.refs_1_.refs_8_, f32[1,1024]{1,0:T(1,128)S(1)} %bitcast.16, bf16[1024,1152]{1,0:T(8,128)(2,1)S(1)} %get-tuple-element.88.refs_3_.refs_2_), custom_call_target="tpu_custom_call" | custom-call | tf_op jit(solution)/shard_map/pooled_kernel/pallas_call | solution.py:641
  74.0 1.2 copy-done.3
  75.2 3.5 %all-to-all-done.1.refs_0_ = f32[32,1,1280]{2,1,0:T(1,128)S(1)} async-done(((f32[32,1,1280]{2,1,0:T(1,128)}), f32[32,1,1280]{2,1,0:T(1,128)S(1)}, u32[]{:S(2)}, u32[]{:S(2)}) %all-to-all-start.1) | async-done | bytes 163872 | tf_op jit(solution)/shard_map/a2a_sums/all_to_all | solution.py:786
  78.7 6.7 %gradient_kernel.1 = (bf16[512,1024]{1,0:T(8,128)(2,1)}, bf16[256,1024]{1,0:T(8,128)(2,1)}, bf16[256,1024]{1,0:T(8,128)(2,1)}, f32[16,512]{1,0:T(8,128)}, f32[32,384]{1,0:T(8,128)}, /*index=5*/f32[16,1024]{1,0:T(8,128)S(1)}) custom-call(f32[32,1,1280]{2,1,0:T(1,128)S(1)} %all-to-all-done.1.refs_0_, f32[512,1024]{1,0:T(8,128)} %get-tuple-element.87.refs_0_.refs_1_, ...), custom_call_target="tpu_custom_call" | custom-call | flops 1150000000 | tf_op jit(solution)/shard_map/gradient_kernel/pallas_call | solution.py:641
  85.4 0.6 copy-done.15
  86.1 3.2 %collective-permute-start.13 = (bf16[256,1024]{1,0:T(8,128)(2,1)}, bf16[256,1024]{1,0:T(8,128)(2,1)}, u32[]{:S(2)}, u32[]{:S(2)}) collective-permute-start(bf16[256,1024]{1,0:T(8,128)(2,1)} %get-tuple-element.106), channel_id=1, source_target_pairs={{0,3},{1,0},{2,1},{3,2},{4,7},{5,4},{6,5},{7,6},{8,11},{9,8},{10,9... | collective-permute-start | bytes 1572872 | tf_op jit(solution)/shard_map/back1/ppermute | solution.py:668
  89.3 0.8 collective-permute-start.10
  90.2 1.2 collective-permute-start.9
  91.3 4.0 %all-to-all-start.2 = ((bf16[32,24,1152]{2,1,0:T(8,128)(2,1)}), bf16[32,24,1152]{2,1,0:T(8,128)(2,1)S(1)}, u32[]{:S(2)}, u32[]{:S(2)}) async-start(bf16[32,24,1152]{2,1,0:T(8,128)(2,1)} %bitcast.10), calls=%async_computation.2 | async-start | bytes 3538944 | tf_op jit(solution)/shard_map/a2a_rows/all_to_all | solution.py:813
  95.3 5.1 %sides_back_kernel.1 = (bf16[256,1024]{1,0:T(8,128)(2,1)S(1)}, bf16[256,1024]{1,0:T(8,128)(2,1)S(1)}, bf16[256,1024]{1,0:T(8,128)(2,1)S(1)}, bf16[256,1024]{1,0:T(8,128)(2,1)S(1)}) custom-call(bf16[512,1024]{1,0:T(8,128)(2,1)S(1)} %copy-done, bf16[4096,1024]{1,0:T(8,128)(2,1)} %refs_1_.3), custom_call_target="tpu_custom_call" | custom-call | flops 1150000000 | tf_op jit(solution)/shard_map/sides_back_kernel/pallas_call | solution.py:641
  100.4 2.2 %collective-permute-done.12.refs_2_ = bf16[256,1024]{1,0:T(8,128)(2,1)} collective-permute-done((bf16[256,1024]{1,0:T(8,128)(2,1)}, bf16[256,1024]{1,0:T(8,128)(2,1)}, u32[]{:S(2)}, u32[]{:S(2)}) %collective-permute-start.12) | collective-permute-done | bytes 524320 | tf_op jit(solution)/shard_map/back1/ppermute | solution.py:668
  102.6 0.6 collective-permute-start.14
  103.2 1.5 %collective-permute-start.15 = (bf16[256,1024]{1,0:T(8,128)(2,1)S(1)}, bf16[256,1024]{1,0:T(8,128)(2,1)S(1)}, u32[]{:S(2)}, u32[]{:S(2)}) collective-permute-start(bf16[256,1024]{1,0:T(8,128)(2,1)S(1)} %get-tuple-element.113), channel_id=1, source_target_pairs={{0,1},{1,2},{2,3},{3,0},{4,5},{5,6},{6,7},{7,4},{8,9},{9,10},{10,1... | collective-permute-start | bytes 1572872 | tf_op jit(solution)/shard_map/back2/ppermute | solution.py:668
  104.7 2.4 %add_kernel.1 = (bf16[256,1024]{1,0:T(8,128)(2,1)}, bf16[256,1024]{1,0:T(8,128)(2,1)}) custom-call(bf16[256,1024]{1,0:T(8,128)(2,1)S(1)} %get-tuple-element.103.refs_0_, bf16[256,1024]{1,0:T(8,128)(2,1)S(1)} %get-tuple-element.104.refs_1_, bf16[256,1024]{1,0:T(8,128)(2,1)} %collective-permute-done.12.refs_2_, bf16[256,1024]{1,0:T(8,128)(2,1)} %collective-permute-done.13.refs_3_), custom_call_target="tpu_custom_call" | custom-call | tf_op jit(solution)/shard_map/add_kernel/pallas_call | solution.py:641
  107.0 0.0 collective-permute-start.23
  107.1 3.2 %collective-permute-start.24 = (bf16[256,1024]{1,0:T(8,128)(2,1)}, bf16[256,1024]{1,0:T(8,128)(2,1)}, u32[]{:S(2)}, u32[]{:S(2)}) collective-permute-start(bf16[256,1024]{1,0:T(8,128)(2,1)} %get-tuple-element.123), channel_id=1, source_target_pairs={{0,3},{1,0},{2,1},{3,2},{4,7},{5,4},{6,5},{7,6},{8,11},{9,8},{10,9... | collective-permute-start | bytes 1572872 | tf_op jit(solution)/shard_map/back3/ppermute | solution.py:668
  110.3 2.2 %join_kernel.1 = (bf16[32,1024]{1,0:T(8,128)(2,1)S(1)}, bf16[16,512]{1,0:T(8,128)(2,1)S(1)}) custom-call(f32[16,512]{1,0:T(8,128)} %get-tuple-element.102.refs_0_, f32[16,512]{1,0:T(8,128)S(1)} %collective-permute-done.9.refs_1_, f32[16,512]{1,0:T(8,128)S(1)} %collective-permute-done.10.refs_2_, f32[16,512]{1,0:T(8,128)S(1)} %collective-permute-done.11.refs_3_, ...), custom_call_target="tpu_custom_call" | custom-call | flops 18400000000 | tf_op jit(solution)/shard_map/join_kernel/pallas_call | solution.py:641
  112.5 0.1 collective-permute-start.16
  112.6 1.2 collective-permute-done.16.refs_1_
  113.9 2.0 %collective-permute-start.19 = (bf16[32,1024]{1,0:T(8,128)(2,1)S(1)}, bf16[32,1024]{1,0:T(8,128)(2,1)S(1)}, u32[]{:S(2)}, u32[]{:S(2)}) collective-permute-start(bf16[32,1024]{1,0:T(8,128)(2,1)S(1)} %pair_kernel.1.refs_0_), channel_id=1, source_target_pairs={{0,96},{4,100},{8,104},{12,108},{16,112},{20,116},{24,120},{28,124... | collective-permute-start | bytes 196616 | tf_op jit(solution)/shard_map/adapters/ppermute | solution.py:691
  115.8 1.6 %collective-permute-done.14.refs_4_ = bf16[256,1024]{1,0:T(8,128)(2,1)S(1)} collective-permute-done((bf16[256,1024]{1,0:T(8,128)(2,1)S(1)}, bf16[256,1024]{1,0:T(8,128)(2,1)S(1)}, u32[]{:S(2)}, u32[]{:S(2)}) %collective-permute-start.14) | collective-permute-done | bytes 524320 | tf_op jit(solution)/shard_map/back2/ppermute | solution.py:668
  117.5 1.3 collective-permute-start.18
  118.8 0.4 collective-permute-done.15.refs_5_
  119.2 1.7 %collective-permute-start.17 = (bf16[32,1024]{1,0:T(8,128)(2,1)S(1)}, bf16[32,1024]{1,0:T(8,128)(2,1)S(1)}, u32[]{:S(2)}, u32[]{:S(2)}) collective-permute-start(bf16[32,1024]{1,0:T(8,128)(2,1)S(1)} %pair_kernel.1.refs_0_), channel_id=1, source_target_pairs={{0,32},{4,36},{8,40},{12,44},{16,48},{20,52},{24,56},{28,60},{32,6... | collective-permute-start | bytes 196616 | tf_op jit(solution)/shard_map/adapters/ppermute | solution.py:691
  120.9 4.1 %own_back_kernel.1.refs_0_ = bf16[512,1024]{1,0:T(8,128)(2,1)S(1)} custom-call(bf16[512,1024]{1,0:T(8,128)(2,1)S(1)} %copy-done, bf16[4096,1024]{1,0:T(8,128)(2,1)} %refs_1_.3, bf16[16,4096]{1,0:T(8,128)(2,1)S(1)} %bitcast.14, bf16[16,512]{1,0:T(8,128)(2,1)S(1)} %get-tuple-element.111.refs_3_, bf16[256,1024]{1,0:T(8,128)(2,1)S(1)} %collective-permute-done.14.refs_4_, ...), custom_call_target="tpu_custom_call" | custom-call | tf_op jit(solution)/shard_map/own_back_kernel/pallas_call | solution.py:641
  125.0 1.0 copy-done.1
  126.1 2.8 %collective-permute-start.22 = (bf16[32,1024]{1,0:T(8,128)(2,1)S(1)}, bf16[32,1024]{1,0:T(8,128)(2,1)S(1)}, u32[]{:S(2)}, u32[]{:S(2)}) collective-permute-start(bf16[32,1024]{1,0:T(8,128)(2,1)S(1)} %four_kernel.1.refs_0_), channel_id=1, source_target_pairs={{0,24},{4,28},{8,0},{12,4},{16,8},{20,12},{24,16},{28,20},{32,56},... | collective-permute-start | bytes 196616 | tf_op jit(solution)/shard_map/adapters/ppermute | solution.py:691
  128.8 0.8 collective-permute-start.21
  129.7 0.9 collective-permute-start.20
  130.6 3.2 %query_kernel.1 = (bf16[32,1024]{1,0:T(8,128)(2,1)}, f32[1,32]{1,0:T(1,128)}) custom-call(f32[32,1,1280]{2,1,0:T(1,128)} %copy-done.4, f32[40,1024]{1,0:T(8,128)} %get-tuple-element.86.refs_1_, f32[32,384]{1,0:T(8,128)} %get-tuple-element.94.refs_2_, f32[32,896]{1,0:T(8,128)} %copy-done.11, bf16[128,1024]{1,0:T(8,128)(2,1)} %copy-done.7, ...), custom_call_target="tpu_custom_call" | custom-call | tf_op jit(solution)/shard_map/query_kernel/pallas_call | solution.py:641
  133.7 0.9 collective-permute-done.21.refs_2_
  134.6 0.7 collective-permute-done.20.refs_1_
  135.3 0.7 last_kernel.1
  136.0 2.4 %finish_kernel.1 = bf16[512,1024]{1,0:T(8,128)(2,1)} custom-call(bf16[512,1024]{1,0:T(8,128)(2,1)S(1)} %copy-done.2, bf16[256,1024]{1,0:T(8,128)(2,1)} %collective-permute-done.23.refs_1_, bf16[256,1024]{1,0:T(8,128)(2,1)} %collective-permute-done.24.refs_2_), custom_call_target="tpu_custom_call" | custom-call | tf_op jit(solution)/shard_map/finish_kernel/pallas_call | solution.py:641
  (53 shorter events, 0.2 us)
Async XLA Ops:
  3.1 19.2 %collective-permute-start = (bf16[256,1024]{1,0:T(8,128)(2,1)}, bf16[256,1024]{1,0:T(8,128)(2,1)S(1)}, u32[]{:S(2)}, u32[]{:S(2)}) collective-permute-start(bf16[256,1024]{1,0:T(8,128)(2,1)} %get-tuple-element.68.refs_0_), channel_id=1, source_target_pairs={{0,1},{1,2},{2,3},{3,0},{4,5},{5,6},{6,7},{7,4},{8,9},{9,10},{10,1... | collective-permute-start | bytes 1572872 | tf_op jit(solution)/shard_map/leg1/ppermute | solution.py:668
  5.2 17.2 %collective-permute-start.2 = (bf16[256,1024]{1,0:T(8,128)(2,1)S(1)}, bf16[256,1024]{1,0:T(8,128)(2,1)S(1)}, u32[]{:S(2)}, u32[]{:S(2)}) collective-permute-start(bf16[256,1024]{1,0:T(8,128)(2,1)S(1)} %get-tuple-element.69.refs_1_), channel_id=1, source_target_pairs={{0,3},{1,0},{2,1},{3,2},{4,7},{5,4},{6,5},{7,6},{8,11},{9,8},{10,9... | collective-permute-start | bytes 1572872 | tf_op jit(solution)/shard_map/leg1/ppermute | solution.py:668
  7.4 23.9 %collective-permute-start.5 = (bf16[256,1024]{1,0:T(8,128)(2,1)}, bf16[256,1024]{1,0:T(8,128)(2,1)S(1)}, u32[]{:S(2)}, u32[]{:S(2)}) collective-permute-start(bf16[256,1024]{1,0:T(8,128)(2,1)} %get-tuple-element.68.refs_0_), channel_id=1, source_target_pairs={{0,3},{1,0},{2,1},{3,2},{4,7},{5,4},{6,5},{7,6},{8,11},{9,8},{10,9... | collective-permute-start | bytes 1572872 | tf_op jit(solution)/shard_map/leg2/ppermute | solution.py:668
  9.3 22.2 %collective-permute-start.4 = (bf16[256,1024]{1,0:T(8,128)(2,1)S(1)}, bf16[256,1024]{1,0:T(8,128)(2,1)S(1)}, u32[]{:S(2)}, u32[]{:S(2)}) collective-permute-start(bf16[256,1024]{1,0:T(8,128)(2,1)S(1)} %get-tuple-element.69.refs_1_), channel_id=1, source_target_pairs={{0,1},{1,2},{2,3},{3,0},{4,5},{5,6},{6,7},{7,4},{8,9},{9,10},{10,1... | collective-permute-start | bytes 1572872 | tf_op jit(solution)/shard_map/leg2/ppermute | solution.py:668
  10.5 0.8 copy-start.5
  11.3 11.0 %copy-start.17 = (bf16[1024]{0:T(1024)(128)(2,1)S(1)}, bf16[1024]{0:T(1024)(128)(2,1)}, u32[]{:S(2)}) copy-start(bf16[1024]{0:T(1024)(128)(2,1)} %param.14) | copy-start | bytes 6148
  11.3 14.6 %copy-start.10 = (bf16[4096,16]{0,1:T(8,128)(2,1)S(1)}, bf16[4096,16]{0,1:T(8,128)(2,1)}, u32[]{:S(2)}) copy-start(bf16[4096,16]{0,1:T(8,128)(2,1)} %param.12) | copy-start | bytes 393220
  14.9 34.9 %all-to-all-start = ((bf16[32,24,1280]{2,1,0:T(8,128)(2,1)}), bf16[32,24,1280]{2,1,0:T(8,128)(2,1)}, u32[]{:S(2)}, u32[]{:S(2)}) async-start(bf16[32,24,1280]{2,1,0:T(8,128)(2,1)} %bitcast.19), calls=%async_computation | async-start | bytes 3932160 | tf_op jit(solution)/shard_map/a2a_queries/all_to_all | solution.py:739
  22.4 19.5 %collective-permute-start.1 = (bf16[256,1024]{1,0:T(8,128)(2,1)S(1)}, bf16[256,1024]{1,0:T(8,128)(2,1)S(1)}, u32[]{:S(2)}, u32[]{:S(2)}) collective-permute-start(bf16[256,1024]{1,0:T(8,128)(2,1)S(1)} %collective-permute-done.refs_0_), channel_id=1, source_target_pairs={{0,1},{1,2},{2,3},{3,0},{4,5},{5,6},{6,7},{7,4},{8,9},{9,10},{10,1... | collective-permute-start | bytes 1572872 | tf_op jit(solution)/shard_map/leg3/ppermute | solution.py:668
  22.5 19.4 %collective-permute-start.3 = (bf16[256,1024]{1,0:T(8,128)(2,1)S(1)}, bf16[256,1024]{1,0:T(8,128)(2,1)S(1)}, u32[]{:S(2)}, u32[]{:S(2)}) collective-permute-start(bf16[256,1024]{1,0:T(8,128)(2,1)S(1)} %collective-permute-done.2.refs_3_), channel_id=1, source_target_pairs={{0,3},{1,0},{2,1},{3,2},{4,7},{5,4},{6,5},{7,6},{8,11},{9,8},{10,9... | collective-permute-start | bytes 1572872 | tf_op jit(solution)/shard_map/leg3/ppermute | solution.py:668
  25.9 1.2 copy-start.14
  31.5 10.4 %copy-start.12 = (bf16[16,1024]{1,0:T(8,128)(2,1)S(1)}, bf16[16,1024]{1,0:T(8,128)(2,1)}, u32[]{:S(2)}) copy-start(bf16[16,1024]{1,0:T(8,128)(2,1)} %refs_10_.1) | copy-start | bytes 98308
  41.9 10.7 %copy-start.6 = (bf16[32,1024]{1,0:T(8,128)(2,1)S(1)}, bf16[32,1024]{1,0:T(8,128)(2,1)}, u32[]{:S(2)}) copy-start(bf16[32,1024]{1,0:T(8,128)(2,1)} %refs_5_.1) | copy-start | bytes 196612
  46.4 1.0 copy-start.8
  49.8 2.8 %copy-start.9 = (bf16[512,1024]{1,0:T(8,128)(2,1)S(1)}, bf16[512,1024]{1,0:T(8,128)(2,1)}, u32[]{:S(2)}) copy-start(bf16[512,1024]{1,0:T(8,128)(2,1)} %copy-done.8) | copy-start | bytes 3145732
  52.6 12.3 %copy-start.13 = (s32[128]{0:T(128)S(1)}, s32[128]{0:T(128)}, u32[]{:S(2)}) copy-start(s32[128]{0:T(128)} %param.17) | copy-start | bytes 1540
  54.2 7.2 %collective-permute-start.8 = (f32[24,1024]{1,0:T(8,128)S(1)}, f32[24,1024]{1,0:T(8,128)S(1)}, u32[]{:S(2)}, u32[]{:S(2)}) collective-permute-start(f32[24,1024]{1,0:T(8,128)S(1)} %partial_kernel.1.refs_0_), channel_id=1, source_target_pairs={{0,3},{1,0},{2,1},{3,2},{4,7},{5,4},{6,5},{7,6},{8,11},{9,8},{10,9... | collective-permute-start | bytes 294920 | tf_op jit(solution)/shard_map/packs/ppermute | solution.py:668
  57.5 6.8 %collective-permute-start.7 = (f32[24,1024]{1,0:T(8,128)S(1)}, f32[24,1024]{1,0:T(8,128)S(1)}, u32[]{:S(2)}, u32[]{:S(2)}) collective-permute-start(f32[24,1024]{1,0:T(8,128)S(1)} %partial_kernel.1.refs_0_), channel_id=1, source_target_pairs={{0,2},{1,3},{2,0},{3,1},{4,6},{5,7},{6,4},{7,5},{8,10},{9,11},{10,... | collective-permute-start | bytes 294920 | tf_op jit(solution)/shard_map/packs/ppermute | solution.py:668
  57.5 7.4 %collective-permute-start.6 = (f32[24,1024]{1,0:T(8,128)S(1)}, f32[24,1024]{1,0:T(8,128)S(1)}, u32[]{:S(2)}, u32[]{:S(2)}) collective-permute-start(f32[24,1024]{1,0:T(8,128)S(1)} %partial_kernel.1.refs_0_), channel_id=1, source_target_pairs={{0,1},{1,2},{2,3},{3,0},{4,5},{5,6},{6,7},{7,4},{8,9},{9,10},{10,1... | collective-permute-start | bytes 294920 | tf_op jit(solution)/shard_map/packs/ppermute | solution.py:668
  66.3 12.4 %copy-start.11 = (f32[32,896]{1,0:T(8,128)}, f32[32,896]{1,0:T(8,128)S(1)}, u32[]{:S(2)}) copy-start(f32[32,896]{1,0:T(8,128)S(1)} %get-tuple-element.90.refs_7_.refs_3_) | copy-start | bytes 344068
  66.3 12.4 %all-to-all-start.1 = ((f32[32,1,1280]{2,1,0:T(1,128)}), f32[32,1,1280]{2,1,0:T(1,128)S(1)}, u32[]{:S(2)}, u32[]{:S(2)}) async-start(f32[32,1,1280]{2,1,0:T(1,128)} %get-tuple-element.85), calls=%async_computation.1 | async-start | bytes 327680 | tf_op jit(solution)/shard_map/a2a_sums/all_to_all | solution.py:786
  73.9 1.2 copy-start.3
  75.2 10.2 %copy-start.7 = (bf16[128,1024]{1,0:T(8,128)(2,1)}, bf16[128,1024]{1,0:T(8,128)(2,1)S(1)}, u32[]{:S(2)}) copy-start(bf16[128,1024]{1,0:T(8,128)(2,1)S(1)} %get-tuple-element.92.refs_9_.refs_4_) | copy-start | bytes 786436
  78.7 6.8 %copy-start.4 = (f32[32,1,1280]{2,1,0:T(1,128)}, f32[32,1,1280]{2,1,0:T(1,128)S(1)}, u32[]{:S(2)}) copy-start(f32[32,1,1280]{2,1,0:T(1,128)S(1)} %all-to-all-done.1.refs_0_) | copy-start | bytes 491524
  85.4 0.6 copy-start.15
  86.1 9.3 %copy-start = (bf16[512,1024]{1,0:T(8,128)(2,1)S(1)}, bf16[512,1024]{1,0:T(8,128)(2,1)}, u32[]{:S(2)}) copy-start(bf16[512,1024]{1,0:T(8,128)(2,1)} %get-tuple-element.64.refs_0_) | copy-start | bytes 3145732
  86.1 16.6 %collective-permute-start.12 = (bf16[256,1024]{1,0:T(8,128)(2,1)}, bf16[256,1024]{1,0:T(8,128)(2,1)}, u32[]{:S(2)}, u32[]{:S(2)}) collective-permute-start(bf16[256,1024]{1,0:T(8,128)(2,1)} %get-tuple-element.105), channel_id=1, source_target_pairs={{0,1},{1,2},{2,3},{3,0},{4,5},{5,6},{6,7},{7,4},{8,9},{9,10},{10,1... | collective-permute-start | bytes 1572872 | tf_op jit(solution)/shard_map/back1/ppermute | solution.py:668
  86.1 17.1 %collective-permute-start.13 = (bf16[256,1024]{1,0:T(8,128)(2,1)}, bf16[256,1024]{1,0:T(8,128)(2,1)}, u32[]{:S(2)}, u32[]{:S(2)}) collective-permute-start(bf16[256,1024]{1,0:T(8,128)(2,1)} %get-tuple-element.106), channel_id=1, source_target_pairs={{0,3},{1,0},{2,1},{3,2},{4,7},{5,4},{6,5},{7,6},{8,11},{9,8},{10,9... | collective-permute-start | bytes 1572872 | tf_op jit(solution)/shard_map/back1/ppermute | solution.py:668
  89.3 17.7 %collective-permute-start.11 = (f32[16,512]{1,0:T(8,128)}, f32[16,512]{1,0:T(8,128)S(1)}, u32[]{:S(2)}, u32[]{:S(2)}) collective-permute-start(f32[16,512]{1,0:T(8,128)} %get-tuple-element.102.refs_0_), channel_id=1, source_target_pairs={{0,3},{1,0},{2,1},{3,2},{4,7},{5,4},{6,5},{7,6},{8,11},{9,8},{10,9... | collective-permute-start | bytes 98312 | tf_op jit(solution)/shard_map/lora_sum/ppermute | solution.py:668
  89.3 17.7 %collective-permute-start.10 = (f32[16,512]{1,0:T(8,128)}, f32[16,512]{1,0:T(8,128)S(1)}, u32[]{:S(2)}, u32[]{:S(2)}) collective-permute-start(f32[16,512]{1,0:T(8,128)} %get-tuple-element.102.refs_0_), channel_id=1, source_target_pairs={{0,2},{1,3},{2,0},{3,1},{4,6},{5,7},{6,4},{7,5},{8,10},{9,11},{10,... | collective-permute-start | bytes 98312 | tf_op jit(solution)/shard_map/lora_sum/ppermute | solution.py:668
  90.2 20.1 %collective-permute-start.9 = (f32[16,512]{1,0:T(8,128)}, f32[16,512]{1,0:T(8,128)S(1)}, u32[]{:S(2)}, u32[]{:S(2)}) collective-permute-start(f32[16,512]{1,0:T(8,128)} %get-tuple-element.102.refs_0_), channel_id=1, source_target_pairs={{0,1},{1,2},{2,3},{3,0},{4,5},{5,6},{6,7},{7,4},{8,9},{9,10},{10,1... | collective-permute-start | bytes 98312 | tf_op jit(solution)/shard_map/lora_sum/ppermute | solution.py:668
  91.3 39.2 %all-to-all-start.2 = ((bf16[32,24,1152]{2,1,0:T(8,128)(2,1)}), bf16[32,24,1152]{2,1,0:T(8,128)(2,1)S(1)}, u32[]{:S(2)}, u32[]{:S(2)}) async-start(bf16[32,24,1152]{2,1,0:T(8,128)(2,1)} %bitcast.10), calls=%async_computation.2 | async-start | bytes 3538944 | tf_op jit(solution)/shard_map/a2a_rows/all_to_all | solution.py:813
  100.4 9.8 %copy-start.16 = (f32[16,1024]{1,0:T(8,128)S(1)}, f32[16,1024]{1,0:T(8,128)}, u32[]{:S(2)}) copy-start(f32[16,1024]{1,0:T(8,128)} %copy-done.15) | copy-start | bytes 196612
  102.6 14.9 %collective-permute-start.14 = (bf16[256,1024]{1,0:T(8,128)(2,1)S(1)}, bf16[256,1024]{1,0:T(8,128)(2,1)S(1)}, u32[]{:S(2)}, u32[]{:S(2)}) collective-permute-start(bf16[256,1024]{1,0:T(8,128)(2,1)S(1)} %get-tuple-element.112), channel_id=1, source_target_pairs={{0,3},{1,0},{2,1},{3,2},{4,7},{5,4},{6,5},{7,6},{8,11},{9,8},{10,9... | collective-permute-start | bytes 1572872 | tf_op jit(solution)/shard_map/back2/ppermute | solution.py:668
  103.2 16.0 %collective-permute-start.15 = (bf16[256,1024]{1,0:T(8,128)(2,1)S(1)}, bf16[256,1024]{1,0:T(8,128)(2,1)S(1)}, u32[]{:S(2)}, u32[]{:S(2)}) collective-permute-start(bf16[256,1024]{1,0:T(8,128)(2,1)S(1)} %get-tuple-element.113), channel_id=1, source_target_pairs={{0,1},{1,2},{2,3},{3,0},{4,5},{5,6},{6,7},{7,4},{8,9},{9,10},{10,1... | collective-permute-start | bytes 1572872 | tf_op jit(solution)/shard_map/back2/ppermute | solution.py:668
  107.0 29.0 %collective-permute-start.23 = (bf16[256,1024]{1,0:T(8,128)(2,1)}, bf16[256,1024]{1,0:T(8,128)(2,1)}, u32[]{:S(2)}, u32[]{:S(2)}) collective-permute-start(bf16[256,1024]{1,0:T(8,128)(2,1)} %get-tuple-element.122), channel_id=1, source_target_pairs={{0,1},{1,2},{2,3},{3,0},{4,5},{5,6},{6,7},{7,4},{8,9},{9,10},{10,1... | collective-permute-start | bytes 1572872 | tf_op jit(solution)/shard_map/back3/ppermute | solution.py:668
  107.1 28.9 %collective-permute-start.24 = (bf16[256,1024]{1,0:T(8,128)(2,1)}, bf16[256,1024]{1,0:T(8,128)(2,1)}, u32[]{:S(2)}, u32[]{:S(2)}) collective-permute-start(bf16[256,1024]{1,0:T(8,128)(2,1)} %get-tuple-element.123), channel_id=1, source_target_pairs={{0,3},{1,0},{2,1},{3,2},{4,7},{5,4},{6,5},{7,6},{8,11},{9,8},{10,9... | collective-permute-start | bytes 1572872 | tf_op jit(solution)/shard_map/back3/ppermute | solution.py:668
  112.5 1.3 collective-permute-start.16
  113.9 12.1 %collective-permute-start.19 = (bf16[32,1024]{1,0:T(8,128)(2,1)S(1)}, bf16[32,1024]{1,0:T(8,128)(2,1)S(1)}, u32[]{:S(2)}, u32[]{:S(2)}) collective-permute-start(bf16[32,1024]{1,0:T(8,128)(2,1)S(1)} %pair_kernel.1.refs_0_), channel_id=1, source_target_pairs={{0,96},{4,100},{8,104},{12,108},{16,112},{20,116},{24,120},{28,124... | collective-permute-start | bytes 196616 | tf_op jit(solution)/shard_map/adapters/ppermute | solution.py:691
  117.5 8.5 %collective-permute-start.18 = (bf16[32,1024]{1,0:T(8,128)(2,1)S(1)}, bf16[32,1024]{1,0:T(8,128)(2,1)S(1)}, u32[]{:S(2)}, u32[]{:S(2)}) collective-permute-start(bf16[32,1024]{1,0:T(8,128)(2,1)S(1)} %pair_kernel.1.refs_0_), channel_id=1, source_target_pairs={{0,64},{4,68},{8,72},{12,76},{16,80},{20,84},{24,88},{28,92},{32,9... | collective-permute-start | bytes 196616 | tf_op jit(solution)/shard_map/adapters/ppermute | solution.py:691
  119.2 6.8 %collective-permute-start.17 = (bf16[32,1024]{1,0:T(8,128)(2,1)S(1)}, bf16[32,1024]{1,0:T(8,128)(2,1)S(1)}, u32[]{:S(2)}, u32[]{:S(2)}) collective-permute-start(bf16[32,1024]{1,0:T(8,128)(2,1)S(1)} %pair_kernel.1.refs_0_), channel_id=1, source_target_pairs={{0,32},{4,36},{8,40},{12,44},{16,48},{20,52},{24,56},{28,60},{32,6... | collective-permute-start | bytes 196616 | tf_op jit(solution)/shard_map/adapters/ppermute | solution.py:691
  125.0 1.0 copy-start.1
  126.0 10.0 %copy-start.2 = (bf16[512,1024]{1,0:T(8,128)(2,1)S(1)}, bf16[512,1024]{1,0:T(8,128)(2,1)}, u32[]{:S(2)}) copy-start(bf16[512,1024]{1,0:T(8,128)(2,1)} %copy-done.1) | copy-start | bytes 3145732
  126.1 7.7 %collective-permute-start.22 = (bf16[32,1024]{1,0:T(8,128)(2,1)S(1)}, bf16[32,1024]{1,0:T(8,128)(2,1)S(1)}, u32[]{:S(2)}, u32[]{:S(2)}) collective-permute-start(bf16[32,1024]{1,0:T(8,128)(2,1)S(1)} %four_kernel.1.refs_0_), channel_id=1, source_target_pairs={{0,24},{4,28},{8,0},{12,4},{16,8},{20,12},{24,16},{28,20},{32,56},... | collective-permute-start | bytes 196616 | tf_op jit(solution)/shard_map/adapters/ppermute | solution.py:691
  128.8 5.8 %collective-permute-start.21 = (bf16[32,1024]{1,0:T(8,128)(2,1)S(1)}, bf16[32,1024]{1,0:T(8,128)(2,1)S(1)}, u32[]{:S(2)}, u32[]{:S(2)}) collective-permute-start(bf16[32,1024]{1,0:T(8,128)(2,1)S(1)} %four_kernel.1.refs_0_), channel_id=1, source_target_pairs={{0,16},{4,20},{8,24},{12,28},{16,0},{20,4},{24,8},{28,12},{32,48},... | collective-permute-start | bytes 196616 | tf_op jit(solution)/shard_map/adapters/ppermute | solution.py:691
  129.7 5.6 %collective-permute-start.20 = (bf16[32,1024]{1,0:T(8,128)(2,1)S(1)}, bf16[32,1024]{1,0:T(8,128)(2,1)S(1)}, u32[]{:S(2)}, u32[]{:S(2)}) collective-permute-start(bf16[32,1024]{1,0:T(8,128)(2,1)S(1)} %four_kernel.1.refs_0_), channel_id=1, source_target_pairs={{0,8},{4,12},{8,16},{12,20},{16,24},{20,28},{24,0},{28,4},{32,40},... | collective-permute-start | bytes 196616 | tf_op jit(solution)/shard_map/adapters/ppermute | solution.py:691
